TPU v7x, 32 devices: a whole 2x2x4 slice. The times are simulated.
32 devices in a mesh: sub: 8 (over z, core), slab: 4 (over y, x).
Axes of the slice: x: 2, y: 2, z: 4, core: 2. Of those that a mesh axis runs over, the one named last changes fastest.
Arguments:
- interface_rhs: float32 [8, 4, 3, 8, 3, 128], P('sub', 'slab'), may hold values from -180 to 180
- order: int32 [8, 4, 3, 768], P('sub', 'slab'), may hold values from 0 to 767, each once within a row
- inverse_rr: bfloat16 [8, 4, 3, 768, 768], P('sub', 'slab'), may hold values from -1 to 6, as said below
- corner_response: bfloat16 [8, 4, 3, 8, 768], P('sub', 'slab'), may hold values from -1.5 to 1.5
- corners: int32 [8, 4, 3, 8], P('sub', 'slab'), may hold values from 0 to 95, as said below
- coarse_factor: float32 [96, 96], P('slab'), may hold values from -1 to 2, as said below
Outputs:
- multipliers: float32 [8, 4, 3, 8, 3, 128], P('sub', 'slab')
- residual: float32 [8, 4, 3, 8, 3, 128], P('sub', 'slab')
Inputs may be any that keep to these rules, and one draw needn't show every extreme that they name: `corners`: each subdomain lists the numbers of its corner vertices at the offsets (0,0,0), (0,0,1), (0,1,0), (0,1,1), (1,0,0), (1,0,1), (1,1,0), (1,1,1) along the three grid dimensions; the vertices of the periodic grid of subdomains carry the numbers 0 to 95, each once, and all subdomains that meet at a vertex list its number. `coarse_factor`: lower triangular with a positive diagonal. `inverse_rr`: each subdomain's matrix is symmetric and positive definite.
All inputs are finite; a program needn't handle non-finite values.
Results may differ from a plain program's by a relative error of at most 0.014.
Values sent between devices are 32-bit elements; how exact they have to be, the bound alone decides.
No kernel may reach another device: no remote copies, remote signals or barrier semaphores. Data moves between devices by JAX's collectives and lax.ppermute only.
A program may use at most 128 MiB of HBM per device.

v0:
```python
import jax
import jax.numpy as jnp
from jax import lax
from jax.sharding import PartitionSpec as P

ITERS = 3


def shifted(value, axis, steps):
    count = lax.axis_size(axis)
    pairs = [(source, (source + steps) % count) for source in range(count)]
    return lax.ppermute(value, axis, pairs)


def local(interface_rhs, order, inverse_rr, corner_response, corners, coarse_factor):
    samples = interface_rhs.shape[3]
    face_size = interface_rhs.shape[5]
    local_size = 6 * face_size
    subdomains = order.shape[0] * order.shape[1] * order.shape[2]
    ncoarse = coarse_factor.shape[1]
    sum_dims = (0, 1, 2, 4, 5)
    whole_factor = lax.all_gather(coarse_factor, "slab", axis=0, tiled=True)
    local_order = order.reshape(subdomains, local_size)
    unorder = jnp.argsort(local_order, axis=-1)
    matrices = inverse_rr.reshape(subdomains, local_size, local_size)
    responses = corner_response.reshape(subdomains, 8, local_size)
    responses_wide = responses.astype(jnp.float32)
    corner_ids = corners.reshape(subdomains * 8)
    multipliers = jnp.zeros_like(interface_rhs)
    residual = interface_rhs
    direction = interface_rhs
    norm_now = lax.psum(jnp.sum(residual * residual, axis=sum_dims), ("sub", "slab"))
    for iteration in range(ITERS):
        back_first = shifted(direction[..., 0, :], "sub", 1)
        back_second = shifted(direction[..., 1, :], "slab", 1)
        back_third = jnp.roll(direction[..., 2, :], 1, axis=2)
        back_faces = jnp.stack([back_first, back_second, back_third], axis=-2)
        canonical = jnp.concatenate([-back_faces, direction], axis=-2).reshape(
            subdomains, samples, local_size
        )
        vector = jnp.take_along_axis(canonical, local_order[:, None, :], axis=2).astype(
            jnp.bfloat16
        )
        local_solution = jnp.einsum(
            "srl,slm->srm", vector, matrices, preferred_element_type=jnp.float32
        )
        corner_terms = jnp.einsum(
            "srl,skl->skr", vector, responses, preferred_element_type=jnp.float32
        ).reshape(subdomains * 8, samples)
        empty = jnp.zeros((ncoarse, samples), jnp.float32)
        coarse_rhs = lax.psum(empty.at[corner_ids].add(corner_terms), ("sub", "slab"))
        coarse = jax.scipy.linalg.cho_solve((whole_factor, True), coarse_rhs)
        picked = coarse[corner_ids].reshape(subdomains, 8, samples)
        lifted = local_solution + jnp.einsum(
            "skr,skl->srl", picked, responses_wide, precision=lax.Precision.HIGHEST
        )
        placed = jnp.take_along_axis(lifted, unorder[:, None, :], axis=2).reshape(
            direction.shape[:4] + (6, face_size)
        )
        ahead_first = shifted(placed[..., 0, :], "sub", -1)
        ahead_second = shifted(placed[..., 1, :], "slab", -1)
        ahead_third = jnp.roll(placed[..., 2, :], -1, axis=2)
        image = placed[..., 3:, :] - jnp.stack([ahead_first, ahead_second, ahead_third], axis=-2)
        curvature = lax.psum(jnp.sum(direction * image, axis=sum_dims), ("sub", "slab"))
        step_size = norm_now / curvature
        step_wide = step_size[:, None, None]
        multipliers = multipliers + step_wide * direction
        residual = residual - step_wide * image
        norm_next = lax.psum(jnp.sum(residual * residual, axis=sum_dims), ("sub", "slab"))
        direction = residual + (norm_next / norm_now)[:, None, None] * direction
        norm_now = norm_next
    return (multipliers, residual)


def solution(mesh):
    in_specs = (
        P("sub", "slab", None, None, None, None),
        P("sub", "slab", None, None),
        P("sub", "slab", None, None, None),
        P("sub", "slab", None, None, None),
        P("sub", "slab", None, None),
        P("slab", None),
    )
    out_specs = (P("sub", "slab", None, None, None, None), P("sub", "slab", None, None, None, None))
    return jax.shard_map(local, mesh=mesh, in_specs=in_specs, out_specs=out_specs, check_vma=False)
```

profile of v0, /device:TPU:0, one launch (start us, length us, event | category | flops | bytes accessed | tf_op | source)
XLA Modules:
  0.0 629.8 jit_solution(17242683301513142842)
XLA Ops:
  9.2 2.5 collective-permute-start.1
  19.1 8.2 %all_gather.3 = f32[96,96]{1,0:T(8,128)S(1)} all-gather(f32[24,96]{1,0:T(8,128)} %param.15), channel_id=1, replica_groups=mesh['sub'=8,'slab'=4] {'slab'}, dimensions={0}, use_global_device_ids=true | all-gather | bytes 46080 | tf_op jit(solution)/shard_map/all_gather | solution.py:22
  31.2 8.8 %custom-call.20 = f32[1,96,96]{1,2,0:T(8,128)} custom-call(f32[1,96,96]{2,1,0:T(8,128)} %select_bitcast_fusion.3), custom_call_target="InvertDiagBlocksLowerTriangular" | custom-call | tf_op jit(solution)/shard_map/jit(_cho_solve)/triangular_solve | solution.py:52
  42.2 1.8 copy.85
  44.0 26.5 %gather_fusion.3 = bf16[2304,8]{1,0:T(8,128)(2,1)} fusion(bf16[3,8,768]{1,2,0:T(8,128)(2,1)} %bitcast.224, s32[2304]{0:T(1024)S(1)} %reshape.410), kind=kCustom, calls=%fused_computation.clone | custom fusion | bytes 92160 | tf_op jit(solution)/shard_map/jit(take_along_axis)/gather | solution.py:41
  70.5 1.9 copy.86
  72.4 1.5 convolution_bitcast_fusion.2
  76.1 40.3 %psum.64 = f32[96,8]{1,0:T(8,128)} all-reduce(f32[96,8]{1,0:T(8,128)} %scatter_custom_fusion), channel_id=1, replica_groups=mesh['sub'=8,'slab'=4] {'sub','slab'}, use_global_device_ids=true, to_apply=%region_3.5 | all-reduce | flops 768 | bytes 6144 | tf_op jit(solution)/shard_map/psum | solution.py:51
  117.4 1.6 fusion.23
  121.5 2.0 fusion.6
  123.5 2.3 copy.91
  129.1 22.4 %gather_fusion.4 = f32[2304,8]{1,0:T(8,128)} fusion(f32[3,8,768]{1,2,0:T(8,128)} %copy.91, s32[2304]{0:T(1024)S(1)} %reshape.415), kind=kCustom, calls=%fused_computation.1.clone | custom fusion | bytes 165888 | tf_op jit(solution)/shard_map/jit(take_along_axis)/gather | solution.py:57
  151.5 2.2 copy.92
  155.7 2.3 collective-permute-start.3
  161.4 40.6 %all-reduce = (f32[8]{0:T(128)}, f32[8]{0:T(128)}) all-reduce(f32[8]{0:T(128)} %multiply_reduce_fusion.5, f32[8]{0:T(128)} %multiply_reduce_fusion.4), channel_id=1, replica_groups=mesh['sub'=8,'slab'=4] {'sub','slab'}, use_global_device_ids=true, to_apply=%region_1.2 | all-reduce | flops 16 | bytes 128 | tf_op jit(solution)/shard_map/psum | solution.py:32
  203.1 2.1 multiply_reduce_fusion.3
  205.3 40.2 %psum.66 = f32[8]{0:T(128)} all-reduce(f32[8]{0:T(128)} %get-tuple-element.14), channel_id=1, replica_groups=mesh['sub'=8,'slab'=4] {'sub','slab'}, use_global_device_ids=true, to_apply=%region_8.11 | all-reduce | flops 8 | bytes 64 | tf_op jit(solution)/shard_map/psum | solution.py:69
  247.1 2.3 collective-permute-start.5
  249.4 2.6 collective-permute-done.4
  252.7 1.8 copy.100
  254.5 26.7 %gather_fusion.5 = bf16[2304,8]{1,0:T(8,128)(2,1)} fusion(bf16[3,8,768]{1,2,0:T(8,128)(2,1)} %bitcast.225, s32[2304]{0:T(1024)} %copy-done.1), kind=kCustom, calls=%fused_computation.2.clone | custom fusion | bytes 92160 | tf_op jit(solution)/shard_map/jit(take_along_axis)/gather | solution.py:41
  281.1 1.9 copy.101
  283.0 1.5 convolution_bitcast_fusion.1
  287.3 40.9 %psum.67 = f32[96,8]{1,0:T(8,128)} all-reduce(f32[96,8]{1,0:T(8,128)} %scatter_custom_fusion.1), channel_id=1, replica_groups=mesh['sub'=8,'slab'=4] {'sub','slab'}, use_global_device_ids=true, to_apply=%region_10.13 | all-reduce | flops 768 | bytes 6144 | tf_op jit(solution)/shard_map/psum | solution.py:51
  329.3 1.6 fusion.19
  330.9 2.1 gather_fusion.1
  334.0 2.0 fusion.9
  336.0 2.3 copy.106
  338.2 22.4 %gather_fusion.6 = f32[2304,8]{1,0:T(8,128)} fusion(f32[3,8,768]{1,2,0:T(8,128)} %copy.106, s32[2304]{0:T(1024)S(1)} %reshape.415), kind=kCustom, calls=%fused_computation.3.clone | custom fusion | bytes 165888 | tf_op jit(solution)/shard_map/jit(take_along_axis)/gather | solution.py:57
  360.6 2.2 copy.107
  364.5 3.0 collective-permute-start.7
  370.9 40.0 %psum.68 = f32[8]{0:T(128)} all-reduce(f32[8]{0:T(128)} %multiply_reduce_fusion.2), channel_id=1, replica_groups=mesh['sub'=8,'slab'=4] {'sub','slab'}, use_global_device_ids=true, to_apply=%region_12.15 | all-reduce | flops 8 | bytes 64 | tf_op jit(solution)/shard_map/psum | solution.py:64
  412.1 2.2 multiply_reduce_fusion.1
  414.3 41.2 %psum.69 = f32[8]{0:T(128)} all-reduce(f32[8]{0:T(128)} %get-tuple-element.12), channel_id=1, replica_groups=mesh['sub'=8,'slab'=4] {'sub','slab'}, use_global_device_ids=true, to_apply=%region_14.17 | all-reduce | flops 8 | bytes 64 | tf_op jit(solution)/shard_map/psum | solution.py:69
  457.2 2.3 collective-permute-start.9
  459.5 2.6 collective-permute-done.8
  462.7 1.8 copy.112
  464.5 26.7 %gather_fusion.7 = bf16[2304,8]{1,0:T(8,128)(2,1)} fusion(bf16[3,8,768]{1,2,0:T(8,128)(2,1)} %bitcast.223, s32[2304]{0:T(1024)} %copy-done.1), kind=kCustom, calls=%fused_computation.4.clone | custom fusion | bytes 92160 | tf_op jit(solution)/shard_map/jit(take_along_axis)/gather | solution.py:41
  491.2 1.9 copy.113
  497.4 39.4 %psum.70 = f32[96,8]{1,0:T(8,128)} all-reduce(f32[96,8]{1,0:T(8,128)} %scatter_custom_fusion.2), channel_id=1, replica_groups=mesh['sub'=8,'slab'=4] {'sub','slab'}, use_global_device_ids=true, to_apply=%region_16.19 | all-reduce | flops 768 | bytes 6144 | tf_op jit(solution)/shard_map/psum | solution.py:51
  537.8 1.6 fusion.15
  539.4 2.1 gather_fusion.2
  542.5 2.0 fusion.12
  544.5 2.3 copy.118
  546.8 22.4 %gather_fusion.8 = f32[2304,8]{1,0:T(8,128)} fusion(f32[3,8,768]{1,2,0:T(8,128)} %copy.118, s32[2304]{0:T(1024)S(1)} %reshape.415), kind=kCustom, calls=%fused_computation.5.clone | custom fusion | bytes 165888 | tf_op jit(solution)/shard_map/jit(take_along_axis)/gather | solution.py:57
  569.2 2.2 copy.119
  572.8 3.3 collective-permute-start.11
  579.1 41.1 %psum.71 = f32[8]{0:T(128)} all-reduce(f32[8]{0:T(128)S(1)} %multiply_reduce_fusion), channel_id=1, replica_groups=mesh['sub'=8,'slab'=4] {'sub','slab'}, use_global_device_ids=true, to_apply=%region_18.21 | all-reduce | flops 8 | bytes 64 | tf_op jit(solution)/shard_map/psum | solution.py:64
  (132 shorter events, 59.9 us)
Async XLA Ops:
  7.2 114.4 %copy-start = (bf16[1,1,3,768,768]{4,3,2,1,0:T(8,128)(2,1)S(1)}, bf16[1,1,3,768,768]{4,3,2,1,0:T(8,128)(2,1)}, u32[]{:S(2)}) copy-start(bf16[1,1,3,768,768]{4,3,2,1,0:T(8,128)(2,1)} %param.12) | copy-start | bytes 10616836
  7.2 118.6 %sort.19.cloned.1.call-start = ((), (), s32[]{:S(2)}) async-start(), calls=%async_computation | async-start | bytes 73760 | tf_op jit(solution)/shard_map/jit(argsort)/sort | solution.py:24
  8.7 31.3 %collective-permute-start = (f32[1,1,3,8,128]{4,3,2,1,0:T(8,128)}, f32[1,1,3,8,128]{4,3,2,1,0:T(8,128)}, u32[]{:S(2)}, u32[]{:S(2)}) collective-permute-start(f32[1,1,3,8,128]{4,3,2,1,0:T(8,128)} %get-tuple-element.31), channel_id=1, source_target_pairs={{0,4},{4,8},{8,12},{12,16},{16,20},{20,24},{24,28},{28,0},{1,5},{5... | collective-permute-start | bytes 36872 | tf_op jit(solution)/shard_map/ppermute | solution.py:12
  9.2 30.9 %collective-permute-start.1 = (f32[1,1,3,8,128]{4,3,2,1,0:T(8,128)}, f32[1,1,3,8,128]{4,3,2,1,0:T(8,128)}, u32[]{:S(2)}, u32[]{:S(2)}) collective-permute-start(f32[1,1,3,8,128]{4,3,2,1,0:T(8,128)} %get-tuple-element.32), channel_id=1, source_target_pairs={{0,1},{1,2},{2,3},{3,0},{4,5},{5,6},{6,7},{7,4},{8,9},{9,10},{10,1... | collective-permute-start | bytes 36872 | tf_op jit(solution)/shard_map/ppermute | solution.py:12
  19.1 10.8 %copy-start.18 = (s32[24]{0:T(128)}, s32[24]{0:T(128)S(1)}, u32[]{:S(2)}) copy-start(s32[24]{0:T(128)S(1)} %fusion.49) | copy-start | bytes 292
  31.2 41.2 %copy-start.1 = (s32[2304]{0:T(1024)}, s32[2304]{0:T(1024)S(1)}, u32[]{:S(2)}) copy-start(s32[2304]{0:T(1024)S(1)} %reshape.410) | copy-start | bytes 27652
  154.7 4.7 copy-start.5
  154.7 3.3 collective-permute-start.2
  155.7 3.7 collective-permute-start.3
  158.0 1.4 copy-start.7
  158.0 1.4 copy-start.11
  159.4 0.6 copy-start.13
  202.6 0.5 copy-start.16
  247.0 5.0 copy-start.2
  247.0 5.0 collective-permute-start.4
  247.1 4.9 collective-permute-start.5
  363.7 5.1 copy-start.6
  363.8 3.7 collective-permute-start.6
  364.5 4.4 collective-permute-start.7
  367.5 1.4 copy-start.8
  367.5 1.4 copy-start.12
  368.9 0.6 copy-start.14
  411.6 0.5 copy-start.17
  457.1 5.0 copy-start.3
  457.1 5.0 collective-permute-start.8
  457.2 4.9 collective-permute-start.9
  546.8 24.6 %copy-start.15 = (pred[3,768]{1,0:T(4,128)(4,1)S(1)}, pred[3,768]{1,0:T(4,128)(4,1)}, u32[]{:S(2)}) copy-start(pred[3,768]{1,0:T(4,128)(4,1)} %and_bitcast_fusion) | copy-start | bytes 6916
  572.3 5.3 copy-start.4
  572.3 3.8 collective-permute-start.10
  572.8 4.7 collective-permute-start.11
  576.2 1.4 copy-start.9
  577.6 0.6 copy-start.10
Sparse Core Ops, SparseCore 0:
  13.7 3.6 sort.21.cloned.1.call-done
  (1 shorter events, 0.0 us)
where the time goes:
time: 635 us; the launch traced here: 630 us
  blocking collectives  332 us (52%)
  local copies, waits for them, and re-layouts  191 us (30%)
  other arithmetic  43 us (7%)
  matrix products  21.5 us (3%)
  starting transfers between devices  18.5 us (3%)
  between operations  14.3 us (2%)
  waiting for transfers between devices  9.38 us (1%)
    psum x3, blocking collectives, local(): lax.psum(jnp.sum(residual * residual, axis=sum_dims), ('sub', 'slab'))  122 us
    psum x3, blocking collectives, local(): lax.psum(empty.at[corner_ids].add(corner_terms), ('sub', 'slab'))  121 us
    gather x7, local copies, waits for them, and re-layouts, local(): jnp.take_along_axis(canonical, local_order[:, None, :], axis=2)  86.2 us
    psum x2, blocking collectives, local(): lax.psum(jnp.sum(direction * image, axis=sum_dims), ('sub', 'slab'))  81.1 us
    gather x7, local copies, waits for them, and re-layouts, local(): jnp.take_along_axis(lifted, unorder[:, None, :], axis=2)  74.6 us
    ppermute x12, starting transfers between devices, shifted(): return lax.ppermute(value, axis, pairs)  18.5 us
  transfers between devices with their start and end apart: 12, of which 5 were waited for; matrix products, arithmetic and copies ran while one was open for 3% of the time, Pallas kernels for 0%

commit v1 on v0

v1 whole, which is shorter than its diff:
```python
import functools

import jax
import jax.numpy as jnp
from jax import lax
from jax.experimental import pallas as pl
from jax.experimental.pallas import tpu as pltpu
from jax.sharding import PartitionSpec as P

ITERS = 3
F32 = jnp.float32
LANES = 128
CORNERS = 8
SIDES = 6
BACK_X, AHEAD_X, BACK_Y, AHEAD_Y = range(4)


def lane_iota():
    return lax.broadcasted_iota(jnp.int32, (8, LANES), 1)


def pick_lanes(tiles, high, low):
    out = None
    for number, tile in enumerate(tiles):
        moved = jnp.take_along_axis(tile, low, axis=1, mode="promise_in_bounds")
        out = moved if out is None else jnp.where(high == number, moved, out)
    return out


def two_parts(value):
    upper = value.astype(jnp.bfloat16)
    lower = (value - upper.astype(F32)).astype(jnp.bfloat16)
    return jnp.concatenate([upper, lower], axis=0)


def lane_sum(tile):
    return jnp.sum(tile, axis=1, keepdims=True)


def order_tiles(order_ref, z):
    high, low = [], []
    for block in range(SIDES):
        row = order_ref[z : z + 1, block * LANES : (block + 1) * LANES]
        row = jnp.broadcast_to(row, (8, LANES))
        high.append(lax.shift_right_logical(row, 7))
        low.append(lax.bitwise_and(row, LANES - 1))
    return high, low


def prepare_kernel(nz, corners_ref, order_ref, response_ref, high_ref, low_ref, faces_ref, ids_ref):
    response = response_ref[...].astype(F32)
    lane = lane_iota()
    lane_square = lax.broadcasted_iota(jnp.int32, (LANES, LANES), 1)
    ids = jnp.zeros((8, LANES), jnp.int32)
    for z in range(nz):
        total = jnp.zeros((16, SIDES * LANES), F32)
        for block in range(SIDES):
            row = order_ref[z : z + 1, block * LANES : (block + 1) * LANES]
            column = jnp.broadcast_to(row, (LANES, LANES)).T
            hot = jnp.concatenate(
                [
                    jnp.where(column == lane_square + side * LANES, 1.0, 0.0).astype(jnp.bfloat16)
                    for side in range(SIDES)
                ],
                axis=1,
            )
            places = jnp.concatenate([lane.astype(F32), jnp.full((8, LANES), block, F32)], axis=0)
            total += jnp.dot(places.astype(jnp.bfloat16), hot, preferred_element_type=F32)
        own = [response[z][:, side * LANES : (side + 1) * LANES] for side in range(SIDES)]
        for side in range(SIDES):
            span = slice(side * LANES, (side + 1) * LANES)
            low = total[:8, span].astype(jnp.int32)
            high = total[8:, span].astype(jnp.int32)
            low_ref[z * SIDES + side] = low
            high_ref[z * SIDES + side] = high
            faces_ref[z * SIDES + side] = pick_lanes(own, high, low)
        for corner in range(CORNERS):
            ids = jnp.where(lane == z * CORNERS + corner, corners_ref[z, corner], ids)
    ids_ref[...] = ids


def factor_kernel(count, factor_ref, inverse_ref, square):
    size = square.shape[0]
    row = lax.broadcasted_iota(jnp.int32, (size, size), 0)
    column = lax.broadcasted_iota(jnp.int32, (size, size), 1)
    square[...] = jnp.where(row == column, 1.0, 0.0)
    square[0:count, 0:count] = factor_ref[...]
    factor = square[...]
    inverse = jnp.where(row == column, 1.0 / factor, 0.0)
    width = 1
    while width < count:
        below = (row // (2 * width) == column // (2 * width)) & (row // width > column // width)
        part = jnp.where(below, factor, 0.0)
        inner = jnp.dot(part, inverse, precision=lax.Precision.HIGHEST, preferred_element_type=F32)
        inverse = inverse - jnp.dot(
            inverse, inner, precision=lax.Precision.HIGHEST, preferred_element_type=F32
        )
        width *= 2
    both = lax.dot_general(
        inverse,
        inverse,
        (((0,), (0,)), ((), ())),
        precision=lax.Precision.HIGHEST,
        preferred_element_type=F32,
    )
    inverse_ref[...] = jnp.where((row < count) & (column < count), both, 0.0)


def send_side(nz, parity_ref, axis, faces, outs):
    even = parity_ref[axis] == 0
    first, second = outs
    for z in range(nz):
        up, down = faces[z * SIDES + 3 + axis], faces[z * SIDES + axis]
        first[z] = jnp.where(even, up, down)
        second[z] = jnp.where(even, down, up)


def local_part(nz, ncoarse, residual, image, refs):
    (order_ref, matrix_ref, response_ref, corners_ref, high_ref, low_ref, faces_ref, sums_ref) = refs
    own, back = residual
    lane = lane_iota()
    energy = jnp.zeros((8, LANES), F32)
    parts = []
    faces = [None] * (nz * SIDES)
    for z in range(nz):
        sides = [
            -back[z],
            -back[nz + z],
            -own[((z - 1) % nz) * 3 + 2],
            own[z * 3],
            own[z * 3 + 1],
            own[z * 3 + 2],
        ]
        high, low = order_tiles(order_ref, z)
        vector = jnp.concatenate([pick_lanes(sides, high[s], low[s]) for s in range(SIDES)], axis=1)
        parts.append(two_parts(vector))
        solved = jnp.dot(parts[z], matrix_ref[z], preferred_element_type=F32)
        solved = solved[:8] + solved[8:]
        tiles = [solved[:, s * LANES : (s + 1) * LANES] for s in range(SIDES)]
        for s in range(SIDES):
            energy += tiles[s] * vector[:, s * LANES : (s + 1) * LANES]
            face = pick_lanes(tiles, high_ref[z * SIDES + s], low_ref[z * SIDES + s])
            faces[z * SIDES + s] = face
            faces_ref[z * SIDES + s] = face
    response = response_ref[...]
    terms = []
    for z in range(nz):
        both = lax.dot_general(
            parts[z], response[z], (((1,), (1,)), ((), ())), preferred_element_type=F32
        )
        terms.append(both[:8] + both[8:])
    norm = jnp.zeros((8, LANES), F32)
    cross = jnp.zeros((8, LANES), F32)
    for at in range(nz * 3):
        norm += own[at] * own[at]
        if image is not None:
            cross += own[at] * image[at]
    numbers = (lane_sum(norm), lane_sum(cross), lane_sum(energy))
    for block in range(sums_ref.shape[0]):
        where = lane + block * LANES
        tile = jnp.zeros((8, LANES), F32)
        for z in range(nz):
            for corner in range(CORNERS):
                tile += jnp.where(where == corners_ref[z, corner], terms[z][:, corner : corner + 1], 0.0)
        for at, number in enumerate(numbers):
            tile += jnp.where(where == ncoarse + at, number, 0.0)
        sums_ref[block] = tile
    return faces


def start_kernel(
    nz, ncoarse, parity_ref, corners_ref, rhs_ref, back_x_ref, back_y_ref, order_ref, matrix_ref,
    response_ref, high_ref, low_ref, response_faces_ref, ids_ref,
    residual_ref, faces_ref, sums_ref, x_first, x_second, y_first, y_second,
):
    own = [rhs_ref[z][:, d, :] for z in range(nz) for d in range(3)]
    back = [back_x_ref[z][:, 0, :] for z in range(nz)] + [back_y_ref[z][:, 1, :] for z in range(nz)]
    for at, tile in enumerate(own + back):
        residual_ref[at] = tile
    refs = (order_ref, matrix_ref, response_ref, corners_ref, high_ref, low_ref, faces_ref, sums_ref)
    faces = local_part(nz, ncoarse, (own, back), None, refs)
    numbers = ids_ref[...].astype(F32)
    responses = [response_faces_ref[at] for at in range(nz * SIDES)]
    for axis, outs in ((0, (x_first, x_second)), (1, (y_first, y_second))):
        send_side(nz, parity_ref, axis, faces, outs)
        send_side(nz, parity_ref, axis, responses, [out.at[nz : 2 * nz] for out in outs])
        for out in outs:
            out[2 * nz] = numbers


def step_kernel(first, last, nz, ncoarse, *refs):
    refs = list(refs)

    def take(count):
        taken = refs[:count]
        del refs[:count]
        return taken

    parity_ref, corners_ref, sums_ref, inverse_ref = take(4)
    received = take(4)
    faces_ref, response_faces_ref, residual_ref = take(3)
    if first:
        (ids_ref,) = take(1)
    else:
        ids_ref, near_ref, image_ref, direction_ref, multipliers_ref, scalars_ref = take(6)
    if not last:
        order_ref, matrix_ref, response_ref, high_ref, low_ref = take(5)
        (out_residual, out_image, out_direction, out_multipliers, out_scalars, out_faces, out_sums) = take(7)
        sends = take(4)
        if first:
            out_ids, out_near = take(2)
    else:
        out_multipliers, out_residual = take(2)

    even_x, even_y = parity_ref[0] == 0, parity_ref[1] == 0
    lane = lane_iota()

    def ahead_and_back(at):
        x_first, x_second, y_first, y_second = [ref[at] for ref in received]
        return {
            AHEAD_X: jnp.where(even_x, x_first, x_second),
            BACK_X: jnp.where(even_x, x_second, x_first),
            AHEAD_Y: jnp.where(even_y, y_first, y_second),
            BACK_Y: jnp.where(even_y, y_second, y_first),
        }

    near_faces, near_responses = {}, {}
    for z in range(nz):
        for side, tile in ahead_and_back(z).items():
            near_faces[side, z] = tile
    if first:
        ids = ids_ref[...]
        for side, tile in ahead_and_back(2 * nz).items():
            shift = nz * CORNERS * (side + 1)
            moved = pltpu.roll(tile, shift, axis=1).astype(jnp.int32)
            ids = jnp.where((lane >= shift) & (lane < shift + nz * CORNERS), moved, ids)
        out_ids[...] = ids
        for z in range(nz):
            for side, tile in ahead_and_back(nz + z).items():
                near_responses[side, z] = tile
                out_near[side * nz + z] = tile
    else:
        ids = ids_ref[...]
        for z in range(nz):
            for side in range(4):
                near_responses[side, z] = near_ref[side * nz + z]

    sums = [sums_ref[block] for block in range(sums_ref.shape[0])]
    coarse = jnp.dot(
        jnp.concatenate(sums, axis=1),
        inverse_ref[...],
        precision=lax.Precision.HIGHEST,
        preferred_element_type=F32,
    )
    coarse = [coarse[:, b * LANES : (b + 1) * LANES] for b in range(coarse.shape[1] // LANES)]
    energy = sum(lane_sum(a * b) for a, b in zip(sums, coarse))

    def number(at):
        block, place = divmod(ncoarse + at, LANES)
        return sums[block][:, place : place + 1]

    norm, cross, energy = number(0), number(1), energy + number(2)
    if first:
        curvature = energy
    else:
        last_norm, last_curvature = scalars_ref[0][:, 0:1], scalars_ref[1][:, 0:1]
        ratio = norm / last_norm
        curvature = energy + 2.0 * ratio * cross + ratio * ratio * last_curvature
    step = norm / curvature

    picked = pick_lanes(coarse, lax.shift_right_logical(ids, 7), lax.bitwise_and(ids, LANES - 1))

    def lifted(tile, response, slot):
        for corner in range(CORNERS):
            at = slot * CORNERS + corner
            tile = tile + picked[:, at : at + 1] * response[corner : corner + 1, :]
        return tile

    def own_side(z, side):
        at = z * SIDES + side
        return lifted(faces_ref[at], response_faces_ref[at], z)

    def near_side(side, z):
        return lifted(near_faces[side, z], near_responses[side, z], nz * (side + 1) + z)

    fresh = [None] * (nz * 5)
    third_down = [own_side(z, 2) for z in range(nz)]
    for z in range(nz):
        fresh[z * 3] = own_side(z, 3) - near_side(AHEAD_X, z)
        fresh[z * 3 + 1] = own_side(z, 4) - near_side(AHEAD_Y, z)
        fresh[z * 3 + 2] = own_side(z, 5) - third_down[(z + 1) % nz]
        if not last:
            fresh[nz * 3 + z] = near_side(BACK_X, z) - own_side(z, 0)
            fresh[nz * 4 + z] = near_side(BACK_Y, z) - own_side(z, 1)

    count = nz * 3 if last else nz * 5
    residual, image = [], []
    for at in range(count):
        new_image = fresh[at] if first else fresh[at] + ratio * image_ref[at]
        old_residual = residual_ref[at]
        residual.append(old_residual - step * new_image)
        image.append(new_image)
        if at < nz * 3:
            direction = old_residual if first else old_residual + ratio * direction_ref[at]
            multipliers = step * direction if first else multipliers_ref[at] + step * direction
            if last:
                z, d = divmod(at, 3)
                out_multipliers[z, :, d, :] = multipliers
                out_residual[z, :, d, :] = residual[at]
            else:
                out_direction[at] = direction
                out_multipliers[at] = multipliers
    if last:
        return
    for at in range(count):
        out_residual[at] = residual[at]
        out_image[at] = image[at]
    out_scalars[0] = jnp.broadcast_to(norm, (8, LANES))
    out_scalars[1] = jnp.broadcast_to(curvature, (8, LANES))
    refs = (order_ref, matrix_ref, response_ref, corners_ref, high_ref, low_ref, out_faces, out_sums)
    faces = local_part(nz, ncoarse, (residual[: nz * 3], residual[nz * 3 :]), image, refs)
    send_side(nz, parity_ref, 0, faces, sends[:2])
    send_side(nz, parity_ref, 1, faces, sends[2:])


def tiles(count, kind=F32):
    return jax.ShapeDtypeStruct((count, 8, LANES), kind)


def call(kernel, outs, operands, scalars, flops, scratch=()):
    vmem = pl.BlockSpec(memory_space=pltpu.VMEM)
    smem = pl.BlockSpec(memory_space=pltpu.SMEM)
    return pl.pallas_call(
        kernel,
        out_shape=outs,
        in_specs=[smem] * scalars + [vmem] * (len(operands) - scalars),
        out_specs=[vmem] * len(outs),
        scratch_shapes=scratch,
        compiler_params=pltpu.CompilerParams(vmem_limit_bytes=48 * 2**20),
        cost_estimate=pl.CostEstimate(flops=flops, bytes_accessed=2**20, transcendentals=0),
    )(*operands)


def shifted(value, axis, steps):
    count = lax.axis_size(axis)
    return lax.ppermute(value, axis, [(i, (i + steps) % count) for i in range(count)])


def paired(value, axis, mask):
    return lax.ppermute(value, axis, [(i, i ^ mask) for i in range(lax.axis_size(axis))])


def paired_other(value, axis):
    count = lax.axis_size(axis)
    return lax.ppermute(value, axis, [(i, (i + 1 if i % 2 else i - 1) % count) for i in range(count)])


def exchange(sums, sends):
    lead = sums.shape[0]
    x_first, x_second, y_first, y_second = sends
    got_x_second = paired_other(x_second, "sub")
    got = paired(jnp.concatenate([sums, x_first]), "sub", 1)
    sums, got_x_first = sums + got[:lead], got[lead:]
    got = paired(jnp.concatenate([sums, y_first]), "slab", 1)
    sums, got_y_first = sums + got[:lead], got[lead:]
    mask = 2
    if lax.axis_size("slab") == 4:
        got = paired(jnp.concatenate([sums, y_second]), "slab", 3)
        sums, got_y_second = sums + got[:lead], got[lead:]
        mask = 4
    else:
        got_y_second = paired_other(y_second, "slab")
    while mask < lax.axis_size("slab"):
        sums = sums + paired(sums, "slab", mask)
        mask *= 2
    mask = 2
    while mask < lax.axis_size("sub"):
        sums = sums + paired(sums, "sub", mask)
        mask *= 2
    return sums, [got_x_first, got_x_second, got_y_first, got_y_second]


def coarse_inverse(coarse_factor, width):
    factor = lax.all_gather(coarse_factor, "slab", axis=0, tiled=True)
    count = factor.shape[0]
    if count <= LANES == width:
        return call(
            functools.partial(factor_kernel, count),
            [jax.ShapeDtypeStruct((LANES, LANES), F32)],
            [factor],
            0,
            2**26,
            [pltpu.VMEM((LANES, LANES), F32)],
        )[0]
    inverse = lax.linalg.triangular_solve(
        factor, jnp.eye(count, dtype=F32), left_side=True, lower=True
    )
    both = jnp.dot(inverse.T, inverse, precision=lax.Precision.HIGHEST)
    columns = -(-count // LANES) * LANES
    return jnp.pad(both, ((0, width - count), (0, columns - count)))


def local(interface_rhs, order, inverse_rr, corner_response, corners, coarse_factor):
    nz, samples, dirs, face = interface_rhs.shape[2:]
    ncoarse = coarse_factor.shape[1]
    local_size = SIDES * face
    blocks = -(-(ncoarse + 3) // LANES)
    rhs = interface_rhs.reshape(nz, samples, dirs, face)
    order = order.reshape(nz, local_size)
    matrices = inverse_rr.reshape(nz, local_size, local_size)
    responses = corner_response.reshape(nz, CORNERS, local_size)
    corners = corners.reshape(nz, CORNERS)
    parity = jnp.stack([lax.axis_index("sub") % 2, lax.axis_index("slab") % 2]).astype(jnp.int32)

    back_x = shifted(rhs, "sub", 1)
    back_y = shifted(rhs, "slab", 1)
    inverse = coarse_inverse(coarse_factor, blocks * LANES)
    tables = nz * SIDES
    high, low, response_faces, ids = call(
        functools.partial(prepare_kernel, nz),
        [tiles(tables, jnp.int32), tiles(tables, jnp.int32), tiles(tables),
         jax.ShapeDtypeStruct((8, LANES), jnp.int32)],
        [corners, order, responses],
        1,
        2**26,
    )
    own = [order, matrices, responses, high, low]
    residual, faces, sums, *sends = call(
        functools.partial(start_kernel, nz, ncoarse),
        [tiles(nz * 5), tiles(tables), tiles(blocks)] + [tiles(2 * nz + 1)] * 4,
        [parity, corners, rhs, back_x, back_y] + own + [response_faces, ids],
        2,
        2**28,
    )
    state = [residual, ids]
    for iteration in range(ITERS):
        first, last = iteration == 0, iteration == ITERS - 1
        sums, received = exchange(sums, sends)
        operands = [parity, corners, sums, inverse] + received + [faces, response_faces] + state
        kernel = functools.partial(step_kernel, first, last, nz, ncoarse)
        if last:
            shape = jax.ShapeDtypeStruct(rhs.shape, F32)
            multipliers, residual = call(kernel, [shape, shape], operands, 2, 2**24)
            break
        outs = [tiles(nz * 5), tiles(nz * 5), tiles(nz * 3), tiles(nz * 3), tiles(2)]
        outs += [tiles(tables), tiles(blocks)] + [tiles(nz)] * 4
        if first:
            outs += [jax.ShapeDtypeStruct((8, LANES), jnp.int32), tiles(nz * 4)]
        results = call(kernel, outs, operands + own, 2, 2**28)
        residual, image, direction, multipliers, scalars, faces, sums = results[:7]
        sends = results[7:11]
        if first:
            ids, near = results[11:]
        state = [residual, ids, near, image, direction, multipliers, scalars]
    return multipliers.reshape(interface_rhs.shape), residual.reshape(interface_rhs.shape)


def solution(mesh):
    in_specs = (
        P("sub", "slab", None, None, None, None),
        P("sub", "slab", None, None),
        P("sub", "slab", None, None, None),
        P("sub", "slab", None, None, None),
        P("sub", "slab", None, None),
        P("slab", None),
    )
    out_specs = (P("sub", "slab", None, None, None, None), P("sub", "slab", None, None, None, None))
    return jax.shard_map(local, mesh=mesh, in_specs=in_specs, out_specs=out_specs, check_vma=False)
```

time: 635 us -> 79.8 us (0.13)
  blocking collectives: 332 us -> 8.23 us
  local copies, waits for them, and re-layouts: 191 us -> 6.23 us
  other arithmetic: 43 us -> 0.18 us
  waiting for transfers between devices: 9.38 us -> 31.2 us
  matrix products: 21.5 us -> 0 us
  between operations: 14.3 us -> 0.81 us
  Pallas kernels: 0 us -> 11.3 us
    psum x8 -> x0, blocking collectives: 324 us -> none  [the longest x3 122 us: local(): lax.psum(jnp.sum(residual * residual, axis=sum_dims), ('sub', 'slab'))]
    gather x17 -> x0, local copies, waits for them, and re-layouts: 166 us -> none  [the longest x7 86.2 us: local(): jnp.take_along_axis(canonical, local_order[:, None, :], axis=2)]
    ppermute x12 -> x20, waiting for transfers between devices: 9.38 us -> 31.2 us  [the longest x15 29.6 us: paired(): lax.ppermute(value, axis, [(i, i ^ mask) for i in range(lax.axis_size(axi...]
    dot_general x9 -> x0, matrix products: 13.5 us -> none  [the longest x3 5.96 us: local(): jnp.einsum('srl,slm->srm', vector, matrices, preferred_element_type=jnp.f...]
    pallas_call x0 -> x6, Pallas kernels: none -> 11.3 us  [call(): pl.pallas_call(kernel, out_shape=outs, in_specs=[smem] * scalars + [vmem]...]
    another operation x8 -> x1, other arithmetic: 10.7 us -> 0.07 us  [local(): jnp.stack([lax.axis_index('sub') % 2, lax.axis_index('slab') % 2])]
    reduce_sum x6 -> x0, other arithmetic: 9.51 us -> none  [the longest x3 5.79 us: local(): jnp.sum(residual * residual, axis=sum_dims)]
    another operation x6 -> x0, matrix products: 7.94 us -> none  [local(): coarse = jax.scipy.linalg.cho_solve((whole_factor, True), coarse_rhs)]
  transfers between devices with their start and end apart: 12 -> 20, of which waited for: 5 -> 14; matrix products, arithmetic and copies ran while one was open for 3% -> 2% of each run, Pallas kernels for 0% -> 6%
where the time goes in v1:
time: 79.8 us; the launch traced here: 79.4 us
  waiting for transfers between devices  31.2 us (39%)
  starting transfers between devices  21.5 us (27%)
  Pallas kernels  11.3 us (14%)
  blocking collectives  8.23 us (10%)
  local copies, waits for them, and re-layouts  6.23 us (8%)
  between operations  0.81 us (1%)
    ppermute x15, waiting for transfers between devices, paired(): lax.ppermute(value, axis, [(i, i ^ mask) for i in range(lax.axis_size(axi...  29.6 us
    ppermute x15, starting transfers between devices, paired(): lax.ppermute(value, axis, [(i, i ^ mask) for i in range(lax.axis_size(axi...  16.6 us
    pallas_call x6, Pallas kernels, call(): pl.pallas_call(kernel, out_shape=outs, in_specs=[smem] * scalars + [vmem]...  11.3 us
    all_gather x1, blocking collectives, coarse_inverse(): factor = lax.all_gather(coarse_factor, 'slab', axis=0, tiled=True)  8.23 us
    unnamed x15, local copies, waits for them, and re-layouts  6.2 us
    ppermute x2, starting transfers between devices, shifted(): lax.ppermute(value, axis, [(i, (i + steps) % count) for i in range(count)])  2.99 us
    ppermute x3, starting transfers between devices, paired_other(): lax.ppermute(value, axis, [(i, (i + 1 if i % 2 else i - 1) % count) for i...  1.9 us
  transfers between devices with their start and end apart: 20, of which 14 were waited for; matrix products, arithmetic and copies ran while one was open for 2% of the time, Pallas kernels for 6%

profile of v1, /device:TPU:0, one launch (start us, length us, event | category | flops | bytes accessed | tf_op | source)
XLA Modules:
  0.0 79.4 jit_solution(1312821376077937325)
XLA Ops:
  0.7 0.8 %copy.16 = f32[1,1,3,8,3,128]{5,4,3,2,1,0:T(4,128)S(1)} copy(f32[1,1,3,8,3,128]{5,3,4,2,1,0:T(8,128)} %param.6) | data formatting | bytes 73728 | tf_op args[0]
  1.4 3.0 %collective-permute-start.1 = (f32[3,8,3,128]{3,2,1,0:T(4,128)S(1)}, f32[3,8,3,128]{3,2,1,0:T(4,128)S(1)}, u32[]{:S(2)}, u32[]{:S(2)}) collective-permute-start(f32[3,8,3,128]{3,2,1,0:T(4,128)S(1)} %bitcast.22), channel_id=1, source_target_pairs={{0,1},{1,2},{2,3},{3,0},{4,5},{5,6},{6,7},{7,4},{8,9},{9,10},{10,1... | collective-permute-start | bytes 110600 | tf_op jit(solution)/shard_map/ppermute | solution.py:346
  4.4 0.1 pad_add_fusion.parity_ref.refs_0_
  4.5 0.7 copy.18
  5.2 0.7 copy.17
  5.9 0.8 copy-done.2
  6.7 1.5 %shard_map.77 = (s32[18,8,128]{2,1,0:T(8,128)S(1)}, s32[18,8,128]{2,1,0:T(8,128)S(1)}, f32[18,8,128]{2,1,0:T(8,128)S(1)}, s32[8,128]{1,0:T(8,128)S(1)}) custom-call(s32[3,8]{1,0:T(4,128)S(1)} %bitcast.29, s32[3,768]{1,0:T(4,128)S(1)} %bitcast.25, bf16[3,8,768]{2,1,0:T(8,128)(2,1)S(1)} %bitcast.18), custom_call_target="tpu_custom_call" | custom-call | flops 67108864 | bytes 1048576 | tf_op jit(solution)/shard_map/pallas_call | solution.py:333
  8.2 1.6 %collective-permute-done.back_x_ref = f32[3,8,3,128]{3,2,1,0:T(4,128)S(1)} collective-permute-done((f32[3,8,3,128]{3,2,1,0:T(4,128)S(1)}, f32[3,8,3,128]{3,2,1,0:T(4,128)S(1)}, u32[]{:S(2)}, u32[]{:S(2)}) %collective-permute-start) | collective-permute-done | bytes 36896 | tf_op jit(solution)/shard_map/ppermute | solution.py:346
  9.8 2.0 %copy-done = bf16[1,1,3,768,768]{4,3,2,1,0:T(8,128)(2,1)S(1)} copy-done((bf16[1,1,3,768,768]{4,3,2,1,0:T(8,128)(2,1)S(1)}, bf16[1,1,3,768,768]{4,3,2,1,0:T(8,128)(2,1)}, u32[]{:S(2)}) %copy-start) | copy-done | bytes 3538968
  11.8 1.4 %shard_map.78 = (f32[15,8,128]{2,1,0:T(8,128)S(1)}, f32[18,8,128]{2,1,0:T(8,128)S(1)}, f32[1,8,128]{2,1,0:T(8,128)S(1)}, f32[7,8,128]{2,1,0:T(8,128)S(1)}, f32[7...) custom-call(s32[2]{0:T(128)S(1)} %pad_add_fusion.parity_ref.refs_0_, s32[3,8]{1,0:T(4,128)S(1)} %bitcast.30, ...), custom_call_target="tpu_custom_call" | custom-call | flops 268435456 | bytes 1048576 | tf_op jit(solution)/shard_map/pallas_call | solution.py:333
  13.2 0.2 collective-permute-start.2
  13.4 1.1 %collective-permute-done.2 = f32[8,8,128]{2,1,0:T(8,128)S(1)} collective-permute-done((f32[8,8,128]{2,1,0:T(8,128)S(1)}, f32[8,8,128]{2,1,0:T(8,128)S(1)}, u32[]{:S(2)}, u32[]{:S(2)}) %collective-permute-start.2) | collective-permute-done | bytes 32800 | tf_op jit(solution)/shard_map/ppermute | solution.py:350
  14.5 1.5 %collective-permute-start.3 = (f32[8,8,128]{2,1,0:T(8,128)S(1)}, f32[8,8,128]{2,1,0:T(8,128)S(1)}, u32[]{:S(2)}, u32[]{:S(2)}) collective-permute-start(f32[8,8,128]{2,1,0:T(8,128)S(1)} %pad_maximum_fusion.1), channel_id=1, source_target_pairs={{0,1},{1,0},{2,3},{3,2},{4,5},{5,4},{6,7},{7,6},{8,9},{9,8},{10,11... | collective-permute-start | bytes 98312 | tf_op jit(solution)/shard_map/ppermute | solution.py:350
  15.9 2.4 %collective-permute-done.3 = f32[8,8,128]{2,1,0:T(8,128)S(1)} collective-permute-done((f32[8,8,128]{2,1,0:T(8,128)S(1)}, f32[8,8,128]{2,1,0:T(8,128)S(1)}, u32[]{:S(2)}, u32[]{:S(2)}) %collective-permute-start.3) | collective-permute-done | bytes 32800 | tf_op jit(solution)/shard_map/ppermute | solution.py:350
  18.4 1.2 %collective-permute-start.4 = (f32[8,8,128]{2,1,0:T(8,128)S(1)}, f32[8,8,128]{2,1,0:T(8,128)S(1)}, u32[]{:S(2)}, u32[]{:S(2)}) collective-permute-start(f32[8,8,128]{2,1,0:T(8,128)S(1)} %pad_maximum_fusion.2), channel_id=1, source_target_pairs={{0,3},{1,2},{2,1},{3,0},{4,7},{5,6},{6,5},{7,4},{8,11},{9,10},{10,... | collective-permute-start | bytes 98312 | tf_op jit(solution)/shard_map/ppermute | solution.py:350
  19.6 0.6 collective-permute-start.7
  20.2 3.0 %collective-permute-done.4 = f32[8,8,128]{2,1,0:T(8,128)S(1)} collective-permute-done((f32[8,8,128]{2,1,0:T(8,128)S(1)}, f32[8,8,128]{2,1,0:T(8,128)S(1)}, u32[]{:S(2)}, u32[]{:S(2)}) %collective-permute-start.4) | collective-permute-done | bytes 32800 | tf_op jit(solution)/shard_map/ppermute | solution.py:350
  23.2 1.4 %collective-permute-start.5 = (f32[1,8,128]{2,1,0:T(8,128)S(1)}, f32[1,8,128]{2,1,0:T(8,128)S(1)}, u32[]{:S(2)}, u32[]{:S(2)}) collective-permute-start(f32[1,8,128]{2,1,0:T(8,128)S(1)} %slice_add_fusion.6), channel_id=1, source_target_pairs={{0,8},{4,12},{8,0},{12,4},{16,24},{20,28},{24,16},{28,20},{1,9},{5... | collective-permute-start | bytes 12296 | tf_op jit(solution)/shard_map/ppermute | solution.py:350
  24.6 8.2 %all_gather.3.factor_ref = f32[96,96]{1,0:T(8,128)S(1)} all-gather(f32[24,96]{1,0:T(8,128)S(1)} %copy-done.4), channel_id=1, replica_groups=mesh['sub'=8,'slab'=4] {'slab'}, dimensions={0}, use_global_device_ids=true | all-gather | bytes 46080 | tf_op jit(solution)/shard_map/all_gather | solution.py:384
  32.8 1.3 %collective-permute-start.6 = (f32[1,8,128]{2,1,0:T(8,128)S(1)}, f32[1,8,128]{2,1,0:T(8,128)S(1)}, u32[]{:S(2)}, u32[]{:S(2)}) collective-permute-start(f32[1,8,128]{2,1,0:T(8,128)S(1)} %add.57), channel_id=1, source_target_pairs={{0,16},{4,20},{8,24},{12,28},{16,0},{20,4},{24,8},{28,12},{1,17},{... | collective-permute-start | bytes 12296 | tf_op jit(solution)/shard_map/ppermute | solution.py:350
  34.1 3.3 %shard_map.79.refs_3_ = f32[128,128]{1,0:T(8,128)S(1)} custom-call(f32[96,96]{1,0:T(8,128)S(1)} %all_gather.3.factor_ref), custom_call_target="tpu_custom_call" | custom-call | flops 67108864 | bytes 1048576 | tf_op jit(solution)/shard_map/pallas_call | solution.py:333
  37.6 2.0 %shard_map.80 = (f32[15,8,128]{2,1,0:T(8,128)S(1)}, f32[15,8,128]{2,1,0:T(8,128)S(1)}, f32[9,8,128]{2,1,0:T(8,128)S(1)}, f32[9,8,128]{2,1,0:T(8,128)S(1)}, f32[2...) custom-call(s32[2]{0:T(128)S(1)} %pad_add_fusion.parity_ref.refs_0_,, ...), custom_call_target="tpu_custom_call" | custom-call | flops 268435456 | bytes 1048576 | tf_op jit(solution)/shard_map/pallas_call | solution.py:333
  39.6 0.1 collective-permute-start.8
  39.7 1.2 %collective-permute-done.8 = f32[4,8,128]{2,1,0:T(8,128)S(1)} collective-permute-done((f32[4,8,128]{2,1,0:T(8,128)S(1)}, f32[4,8,128]{2,1,0:T(8,128)S(1)}, u32[]{:S(2)}, u32[]{:S(2)}) %collective-permute-start.8) | collective-permute-done | bytes 16416 | tf_op jit(solution)/shard_map/ppermute | solution.py:350
  40.9 0.5 collective-permute-start.9
  41.4 3.2 %collective-permute-done.9 = f32[4,8,128]{2,1,0:T(8,128)S(1)} collective-permute-done((f32[4,8,128]{2,1,0:T(8,128)S(1)}, f32[4,8,128]{2,1,0:T(8,128)S(1)}, u32[]{:S(2)}, u32[]{:S(2)}) %collective-permute-start.9) | collective-permute-done | bytes 16416 | tf_op jit(solution)/shard_map/ppermute | solution.py:350
  44.6 1.5 %collective-permute-start.10 = (f32[4,8,128]{2,1,0:T(8,128)S(1)}, f32[4,8,128]{2,1,0:T(8,128)S(1)}, u32[]{:S(2)}, u32[]{:S(2)}) collective-permute-start(f32[4,8,128]{2,1,0:T(8,128)S(1)} %pad_maximum_fusion.5), channel_id=1, source_target_pairs={{0,3},{1,2},{2,1},{3,0},{4,7},{5,6},{6,5},{7,4},{8,11},{9,10},{10,... | collective-permute-start | bytes 49160 | tf_op jit(solution)/shard_map/ppermute | solution.py:350
  46.1 0.7 collective-permute-start.13
  46.7 2.5 %collective-permute-done.10 = f32[4,8,128]{2,1,0:T(8,128)S(1)} collective-permute-done((f32[4,8,128]{2,1,0:T(8,128)S(1)}, f32[4,8,128]{2,1,0:T(8,128)S(1)}, u32[]{:S(2)}, u32[]{:S(2)}) %collective-permute-start.10) | collective-permute-done | bytes 16416 | tf_op jit(solution)/shard_map/ppermute | solution.py:350
  49.3 1.8 %collective-permute-start.11 = (f32[1,8,128]{2,1,0:T(8,128)S(1)}, f32[1,8,128]{2,1,0:T(8,128)S(1)}, u32[]{:S(2)}, u32[]{:S(2)}) collective-permute-start(f32[1,8,128]{2,1,0:T(8,128)S(1)} %slice_add_fusion.3), channel_id=1, source_target_pairs={{0,8},{4,12},{8,0},{12,4},{16,24},{20,28},{24,16},{28,20},{1,9},{5... | collective-permute-start | bytes 12296 | tf_op jit(solution)/shard_map/ppermute | solution.py:350
  51.1 1.8 %collective-permute-done.11 = f32[1,8,128]{2,1,0:T(8,128)S(1)} collective-permute-done((f32[1,8,128]{2,1,0:T(8,128)S(1)}, f32[1,8,128]{2,1,0:T(8,128)S(1)}, u32[]{:S(2)}, u32[]{:S(2)}) %collective-permute-start.11) | collective-permute-done | bytes 4128 | tf_op jit(solution)/shard_map/ppermute | solution.py:350
  52.9 1.7 %collective-permute-start.12 = (f32[1,8,128]{2,1,0:T(8,128)S(1)}, f32[1,8,128]{2,1,0:T(8,128)S(1)}, u32[]{:S(2)}, u32[]{:S(2)}) collective-permute-start(f32[1,8,128]{2,1,0:T(8,128)S(1)} %add.62), channel_id=1, source_target_pairs={{0,16},{4,20},{8,24},{12,28},{16,0},{20,4},{24,8},{28,12},{1,17},{... | collective-permute-start | bytes 12296 | tf_op jit(solution)/shard_map/ppermute | solution.py:350
  54.6 2.8 %collective-permute-done.12 = f32[1,8,128]{2,1,0:T(8,128)S(1)} collective-permute-done((f32[1,8,128]{2,1,0:T(8,128)S(1)}, f32[1,8,128]{2,1,0:T(8,128)S(1)}, u32[]{:S(2)}, u32[]{:S(2)}) %collective-permute-start.12) | collective-permute-done | bytes 4128 | tf_op jit(solution)/shard_map/ppermute | solution.py:350
  57.4 2.0 %shard_map.81 = (f32[15,8,128]{2,1,0:T(8,128)S(1)}, f32[15,8,128]{2,1,0:T(8,128)S(1)}, f32[9,8,128]{2,1,0:T(8,128)S(1)}, f32[9,8,128]{2,1,0:T(8,128)S(1)}, f32[2...) custom-call(s32[2]{0:T(128)S(1)} %pad_add_fusion.parity_ref.refs_0_,, ...), custom_call_target="tpu_custom_call" | custom-call | flops 268435456 | bytes 1048576 | tf_op jit(solution)/shard_map/pallas_call | solution.py:333
  59.4 0.1 collective-permute-start.14
  59.4 1.2 %collective-permute-done.14 = f32[4,8,128]{2,1,0:T(8,128)S(1)} collective-permute-done((f32[4,8,128]{2,1,0:T(8,128)S(1)}, f32[4,8,128]{2,1,0:T(8,128)S(1)}, u32[]{:S(2)}, u32[]{:S(2)}) %collective-permute-start.14) | collective-permute-done | bytes 16416 | tf_op jit(solution)/shard_map/ppermute | solution.py:350
  60.6 0.5 collective-permute-start.15
  61.1 3.2 %collective-permute-done.15 = f32[4,8,128]{2,1,0:T(8,128)S(1)} collective-permute-done((f32[4,8,128]{2,1,0:T(8,128)S(1)}, f32[4,8,128]{2,1,0:T(8,128)S(1)}, u32[]{:S(2)}, u32[]{:S(2)}) %collective-permute-start.15) | collective-permute-done | bytes 16416 | tf_op jit(solution)/shard_map/ppermute | solution.py:350
  64.4 1.5 %collective-permute-start.16 = (f32[4,8,128]{2,1,0:T(8,128)S(1)}, f32[4,8,128]{2,1,0:T(8,128)S(1)}, u32[]{:S(2)}, u32[]{:S(2)}) collective-permute-start(f32[4,8,128]{2,1,0:T(8,128)S(1)} %pad_maximum_fusion.8), channel_id=1, source_target_pairs={{0,3},{1,2},{2,1},{3,0},{4,7},{5,6},{6,5},{7,4},{8,11},{9,10},{10,... | collective-permute-start | bytes 49160 | tf_op jit(solution)/shard_map/ppermute | solution.py:350
  65.8 0.6 collective-permute-start.19
  66.5 2.5 %collective-permute-done.16 = f32[4,8,128]{2,1,0:T(8,128)S(1)} collective-permute-done((f32[4,8,128]{2,1,0:T(8,128)S(1)}, f32[4,8,128]{2,1,0:T(8,128)S(1)}, u32[]{:S(2)}, u32[]{:S(2)}) %collective-permute-start.16) | collective-permute-done | bytes 16416 | tf_op jit(solution)/shard_map/ppermute | solution.py:350
  69.0 1.8 %collective-permute-start.17 = (f32[1,8,128]{2,1,0:T(8,128)S(1)}, f32[1,8,128]{2,1,0:T(8,128)S(1)}, u32[]{:S(2)}, u32[]{:S(2)}) collective-permute-start(f32[1,8,128]{2,1,0:T(8,128)S(1)} %slice_add_fusion), channel_id=1, source_target_pairs={{0,8},{4,12},{8,0},{12,4},{16,24},{20,28},{24,16},{28,20},{1,9},{5... | collective-permute-start | bytes 12296 | tf_op jit(solution)/shard_map/ppermute | solution.py:350
  70.8 1.8 %collective-permute-done.17 = f32[1,8,128]{2,1,0:T(8,128)S(1)} collective-permute-done((f32[1,8,128]{2,1,0:T(8,128)S(1)}, f32[1,8,128]{2,1,0:T(8,128)S(1)}, u32[]{:S(2)}, u32[]{:S(2)}) %collective-permute-start.17) | collective-permute-done | bytes 4128 | tf_op jit(solution)/shard_map/ppermute | solution.py:350
  72.6 1.7 %collective-permute-start.18 = (f32[1,8,128]{2,1,0:T(8,128)S(1)}, f32[1,8,128]{2,1,0:T(8,128)S(1)}, u32[]{:S(2)}, u32[]{:S(2)}) collective-permute-start(f32[1,8,128]{2,1,0:T(8,128)S(1)} %add.67), channel_id=1, source_target_pairs={{0,16},{4,20},{8,24},{12,28},{16,0},{20,4},{24,8},{28,12},{1,17},{... | collective-permute-start | bytes 12296 | tf_op jit(solution)/shard_map/ppermute | solution.py:350
  74.3 2.8 %collective-permute-done.18 = f32[1,8,128]{2,1,0:T(8,128)S(1)} collective-permute-done((f32[1,8,128]{2,1,0:T(8,128)S(1)}, f32[1,8,128]{2,1,0:T(8,128)S(1)}, u32[]{:S(2)}, u32[]{:S(2)}) %collective-permute-start.18) | collective-permute-done | bytes 4128 | tf_op jit(solution)/shard_map/ppermute | solution.py:350
  77.1 1.1 %shard_map.82 = (f32[3,8,3,128]{3,2,1,0:T(4,128)S(1)}, f32[3,8,3,128]{3,2,1,0:T(4,128)S(1)}) custom-call(s32[2]{0:T(128)S(1)} %pad_add_fusion.parity_ref.refs_0_, s32[3,8]{1,0:T(4,128)S(1)} %bitcast.33, f32[1,8,128]{2,1,0:T(8,128)S(1)} %add.68.refs_2_, f32[128,128]{1,0:T(8,128)S(1)} %shard_map.79.refs_3_, f32[3,8,128]{2,1,0:T(8,128)S(1)} %slice.87.refs_4_, ...), custom_call_target="tpu_custom_call" | custom-call | flops 16777216 | bytes 1048576 | tf_op jit(solution)/shard_map/pallas_call | solution.py:333
  78.2 0.6 copy.9
  78.8 0.6 copy.10
  (48 shorter events, 0.2 us)
Async XLA Ops:
  0.6 36.9 %copy-start.3 = (bf16[1,1,3,8,768]{4,3,2,1,0:T(8,128)(2,1)S(1)}, bf16[1,1,3,8,768]{4,3,2,1,0:T(8,128)(2,1)}, u32[]{:S(2)}) copy-start(bf16[1,1,3,8,768]{4,3,2,1,0:T(8,128)(2,1)} %param.9) | copy-start | bytes 110596
  0.6 23.9 %copy-start.4 = (f32[24,96]{1,0:T(8,128)S(1)}, f32[24,96]{1,0:T(8,128)}, u32[]{:S(2)}) copy-start(f32[24,96]{1,0:T(8,128)} %param.11) | copy-start | bytes 27652
  1.4 6.7 %collective-permute-start.1 = (f32[3,8,3,128]{3,2,1,0:T(4,128)S(1)}, f32[3,8,3,128]{3,2,1,0:T(4,128)S(1)}, u32[]{:S(2)}, u32[]{:S(2)}) collective-permute-start(f32[3,8,3,128]{3,2,1,0:T(4,128)S(1)} %bitcast.22), channel_id=1, source_target_pairs={{0,1},{1,2},{2,3},{3,0},{4,5},{5,6},{6,7},{7,4},{8,9},{9,10},{10,1... | collective-permute-start | bytes 110600 | tf_op jit(solution)/shard_map/ppermute | solution.py:346
  4.4 5.3 %collective-permute-start = (f32[3,8,3,128]{3,2,1,0:T(4,128)S(1)}, f32[3,8,3,128]{3,2,1,0:T(4,128)S(1)}, u32[]{:S(2)}, u32[]{:S(2)}) collective-permute-start(f32[3,8,3,128]{3,2,1,0:T(4,128)S(1)} %bitcast.23), channel_id=1, source_target_pairs={{0,4},{4,8},{8,12},{12,16},{16,20},{20,24},{24,28},{28,0},{1,5},{5... | collective-permute-start | bytes 110600 | tf_op jit(solution)/shard_map/ppermute | solution.py:346
  5.9 0.8 copy-start.2
  9.8 2.0 %copy-start = (bf16[1,1,3,768,768]{4,3,2,1,0:T(8,128)(2,1)S(1)}, bf16[1,1,3,768,768]{4,3,2,1,0:T(8,128)(2,1)}, u32[]{:S(2)}) copy-start(bf16[1,1,3,768,768]{4,3,2,1,0:T(8,128)(2,1)} %param.8) | copy-start | bytes 10616836
  11.8 25.8 %copy-start.1 = (bf16[1,1,3,768,768]{4,3,2,1,0:T(8,128)(2,1)S(1)}, bf16[1,1,3,768,768]{4,3,2,1,0:T(8,128)(2,1)}, u32[]{:S(2)}) copy-start(bf16[1,1,3,768,768]{4,3,2,1,0:T(8,128)(2,1)} %param.8) | copy-start | bytes 10616836
  13.2 1.3 %collective-permute-start.2 = (f32[8,8,128]{2,1,0:T(8,128)S(1)}, f32[8,8,128]{2,1,0:T(8,128)S(1)}, u32[]{:S(2)}, u32[]{:S(2)}) collective-permute-start(f32[8,8,128]{2,1,0:T(8,128)S(1)} %pad_maximum_fusion), channel_id=1, source_target_pairs={{0,4},{4,0},{8,12},{12,8},{16,20},{20,16},{24,28},{28,24},{1,5},{5... | collective-permute-start | bytes 98312 | tf_op jit(solution)/shard_map/ppermute | solution.py:350
  14.5 3.9 %collective-permute-start.3 = (f32[8,8,128]{2,1,0:T(8,128)S(1)}, f32[8,8,128]{2,1,0:T(8,128)S(1)}, u32[]{:S(2)}, u32[]{:S(2)}) collective-permute-start(f32[8,8,128]{2,1,0:T(8,128)S(1)} %pad_maximum_fusion.1), channel_id=1, source_target_pairs={{0,1},{1,0},{2,3},{3,2},{4,5},{5,4},{6,7},{7,6},{8,9},{9,8},{10,11... | collective-permute-start | bytes 98312 | tf_op jit(solution)/shard_map/ppermute | solution.py:350
  18.4 4.8 %collective-permute-start.4 = (f32[8,8,128]{2,1,0:T(8,128)S(1)}, f32[8,8,128]{2,1,0:T(8,128)S(1)}, u32[]{:S(2)}, u32[]{:S(2)}) collective-permute-start(f32[8,8,128]{2,1,0:T(8,128)S(1)} %pad_maximum_fusion.2), channel_id=1, source_target_pairs={{0,3},{1,2},{2,1},{3,0},{4,7},{5,6},{6,5},{7,4},{8,11},{9,10},{10,... | collective-permute-start | bytes 98312 | tf_op jit(solution)/shard_map/ppermute | solution.py:350
  19.6 17.9 %collective-permute-start.7 = (f32[7,8,128]{2,1,0:T(8,128)S(1)}, f32[7,8,128]{2,1,0:T(8,128)S(1)}, u32[]{:S(2)}, u32[]{:S(2)}) collective-permute-start(f32[7,8,128]{2,1,0:T(8,128)S(1)} %get-tuple-element.47), channel_id=1, source_target_pairs={{0,28},{4,8},{8,4},{12,16},{16,12},{20,24},{24,20},{28,0},{1,29},{... | collective-permute-start | bytes 86024 | tf_op jit(solution)/shard_map/ppermute | solution.py:355
  23.2 9.6 %collective-permute-start.5 = (f32[1,8,128]{2,1,0:T(8,128)S(1)}, f32[1,8,128]{2,1,0:T(8,128)S(1)}, u32[]{:S(2)}, u32[]{:S(2)}) collective-permute-start(f32[1,8,128]{2,1,0:T(8,128)S(1)} %slice_add_fusion.6), channel_id=1, source_target_pairs={{0,8},{4,12},{8,0},{12,4},{16,24},{20,28},{24,16},{28,20},{1,9},{5... | collective-permute-start | bytes 12296 | tf_op jit(solution)/shard_map/ppermute | solution.py:350
  32.8 4.7 %collective-permute-start.6 = (f32[1,8,128]{2,1,0:T(8,128)S(1)}, f32[1,8,128]{2,1,0:T(8,128)S(1)}, u32[]{:S(2)}, u32[]{:S(2)}) collective-permute-start(f32[1,8,128]{2,1,0:T(8,128)S(1)} %add.57), channel_id=1, source_target_pairs={{0,16},{4,20},{8,24},{12,28},{16,0},{20,4},{24,8},{28,12},{1,17},{... | collective-permute-start | bytes 12296 | tf_op jit(solution)/shard_map/ppermute | solution.py:350
  39.6 1.2 %collective-permute-start.8 = (f32[4,8,128]{2,1,0:T(8,128)S(1)}, f32[4,8,128]{2,1,0:T(8,128)S(1)}, u32[]{:S(2)}, u32[]{:S(2)}) collective-permute-start(f32[4,8,128]{2,1,0:T(8,128)S(1)} %pad_maximum_fusion.3), channel_id=1, source_target_pairs={{0,4},{4,0},{8,12},{12,8},{16,20},{20,16},{24,28},{28,24},{1,5},{5... | collective-permute-start | bytes 49160 | tf_op jit(solution)/shard_map/ppermute | solution.py:350
  40.9 3.7 %collective-permute-start.9 = (f32[4,8,128]{2,1,0:T(8,128)S(1)}, f32[4,8,128]{2,1,0:T(8,128)S(1)}, u32[]{:S(2)}, u32[]{:S(2)}) collective-permute-start(f32[4,8,128]{2,1,0:T(8,128)S(1)} %pad_maximum_fusion.4), channel_id=1, source_target_pairs={{0,1},{1,0},{2,3},{3,2},{4,5},{5,4},{6,7},{7,6},{8,9},{9,8},{10,11... | collective-permute-start | bytes 49160 | tf_op jit(solution)/shard_map/ppermute | solution.py:350
  44.6 4.6 %collective-permute-start.10 = (f32[4,8,128]{2,1,0:T(8,128)S(1)}, f32[4,8,128]{2,1,0:T(8,128)S(1)}, u32[]{:S(2)}, u32[]{:S(2)}) collective-permute-start(f32[4,8,128]{2,1,0:T(8,128)S(1)} %pad_maximum_fusion.5), channel_id=1, source_target_pairs={{0,3},{1,2},{2,1},{3,0},{4,7},{5,6},{6,5},{7,4},{8,11},{9,10},{10,... | collective-permute-start | bytes 49160 | tf_op jit(solution)/shard_map/ppermute | solution.py:350
  46.1 11.3 %collective-permute-start.13 = (f32[3,8,128]{2,1,0:T(8,128)S(1)}, f32[3,8,128]{2,1,0:T(8,128)S(1)}, u32[]{:S(2)}, u32[]{:S(2)}) collective-permute-start(f32[3,8,128]{2,1,0:T(8,128)S(1)} %get-tuple-element.54), channel_id=1, source_target_pairs={{0,28},{4,8},{8,4},{12,16},{16,12},{20,24},{24,20},{28,0},{1,29},{... | collective-permute-start | bytes 36872 | tf_op jit(solution)/shard_map/ppermute | solution.py:355
  49.3 3.6 %collective-permute-start.11 = (f32[1,8,128]{2,1,0:T(8,128)S(1)}, f32[1,8,128]{2,1,0:T(8,128)S(1)}, u32[]{:S(2)}, u32[]{:S(2)}) collective-permute-start(f32[1,8,128]{2,1,0:T(8,128)S(1)} %slice_add_fusion.3), channel_id=1, source_target_pairs={{0,8},{4,12},{8,0},{12,4},{16,24},{20,28},{24,16},{28,20},{1,9},{5... | collective-permute-start | bytes 12296 | tf_op jit(solution)/shard_map/ppermute | solution.py:350
  52.9 4.5 %collective-permute-start.12 = (f32[1,8,128]{2,1,0:T(8,128)S(1)}, f32[1,8,128]{2,1,0:T(8,128)S(1)}, u32[]{:S(2)}, u32[]{:S(2)}) collective-permute-start(f32[1,8,128]{2,1,0:T(8,128)S(1)} %add.62), channel_id=1, source_target_pairs={{0,16},{4,20},{8,24},{12,28},{16,0},{20,4},{24,8},{28,12},{1,17},{... | collective-permute-start | bytes 12296 | tf_op jit(solution)/shard_map/ppermute | solution.py:350
  59.4 1.2 %collective-permute-start.14 = (f32[4,8,128]{2,1,0:T(8,128)S(1)}, f32[4,8,128]{2,1,0:T(8,128)S(1)}, u32[]{:S(2)}, u32[]{:S(2)}) collective-permute-start(f32[4,8,128]{2,1,0:T(8,128)S(1)} %pad_maximum_fusion.6), channel_id=1, source_target_pairs={{0,4},{4,0},{8,12},{12,8},{16,20},{20,16},{24,28},{28,24},{1,5},{5... | collective-permute-start | bytes 49160 | tf_op jit(solution)/shard_map/ppermute | solution.py:350
  60.6 3.7 %collective-permute-start.15 = (f32[4,8,128]{2,1,0:T(8,128)S(1)}, f32[4,8,128]{2,1,0:T(8,128)S(1)}, u32[]{:S(2)}, u32[]{:S(2)}) collective-permute-start(f32[4,8,128]{2,1,0:T(8,128)S(1)} %pad_maximum_fusion.7), channel_id=1, source_target_pairs={{0,1},{1,0},{2,3},{3,2},{4,5},{5,4},{6,7},{7,6},{8,9},{9,8},{10,11... | collective-permute-start | bytes 49160 | tf_op jit(solution)/shard_map/ppermute | solution.py:350
  64.4 4.6 %collective-permute-start.16 = (f32[4,8,128]{2,1,0:T(8,128)S(1)}, f32[4,8,128]{2,1,0:T(8,128)S(1)}, u32[]{:S(2)}, u32[]{:S(2)}) collective-permute-start(f32[4,8,128]{2,1,0:T(8,128)S(1)} %pad_maximum_fusion.8), channel_id=1, source_target_pairs={{0,3},{1,2},{2,1},{3,0},{4,7},{5,6},{6,5},{7,4},{8,11},{9,10},{10,... | collective-permute-start | bytes 49160 | tf_op jit(solution)/shard_map/ppermute | solution.py:350
  65.8 11.3 %collective-permute-start.19 = (f32[3,8,128]{2,1,0:T(8,128)S(1)}, f32[3,8,128]{2,1,0:T(8,128)S(1)}, u32[]{:S(2)}, u32[]{:S(2)}) collective-permute-start(f32[3,8,128]{2,1,0:T(8,128)S(1)} %get-tuple-element.67), channel_id=1, source_target_pairs={{0,28},{4,8},{8,4},{12,16},{16,12},{20,24},{24,20},{28,0},{1,29},{... | collective-permute-start | bytes 36872 | tf_op jit(solution)/shard_map/ppermute | solution.py:355
  69.0 3.6 %collective-permute-start.17 = (f32[1,8,128]{2,1,0:T(8,128)S(1)}, f32[1,8,128]{2,1,0:T(8,128)S(1)}, u32[]{:S(2)}, u32[]{:S(2)}) collective-permute-start(f32[1,8,128]{2,1,0:T(8,128)S(1)} %slice_add_fusion), channel_id=1, source_target_pairs={{0,8},{4,12},{8,0},{12,4},{16,24},{20,28},{24,16},{28,20},{1,9},{5... | collective-permute-start | bytes 12296 | tf_op jit(solution)/shard_map/ppermute | solution.py:350
  72.6 4.5 %collective-permute-start.18 = (f32[1,8,128]{2,1,0:T(8,128)S(1)}, f32[1,8,128]{2,1,0:T(8,128)S(1)}, u32[]{:S(2)}, u32[]{:S(2)}) collective-permute-start(f32[1,8,128]{2,1,0:T(8,128)S(1)} %add.67), channel_id=1, source_target_pairs={{0,16},{4,20},{8,24},{12,28},{16,0},{20,4},{24,8},{28,12},{1,17},{... | collective-permute-start | bytes 12296 | tf_op jit(solution)/shard_map/ppermute | solution.py:350

commit v2 on v1

--- a/solution.py
+++ b/solution.py
@@ -40,14 +40,20 @@
 def order_tiles(order_ref, z):
     high, low = [], []
     for block in range(SIDES):
-        row = order_ref[z : z + 1, block * LANES : (block + 1) * LANES]
-        row = jnp.broadcast_to(row, (8, LANES))
+        row = jnp.broadcast_to(order_ref[z, :, block * LANES : (block + 1) * LANES], (8, LANES))
         high.append(lax.shift_right_logical(row, 7))
         low.append(lax.bitwise_and(row, LANES - 1))
     return high, low
 
 
-def prepare_kernel(nz, corners_ref, order_ref, response_ref, high_ref, low_ref, faces_ref, ids_ref):
+def prepare_kernel(
+    nz, corners_ref, order_ref, response_ref, matrix_ref, factor_ref,
+    high_ref, low_ref, faces_ref, ids_ref, rows_ref,
+):
+    if rows_ref is not None:
+        rows_ref[...] = jnp.zeros_like(rows_ref)
+        for at in range(rows_ref.shape[0]):
+            rows_ref[at, :, 0 : factor_ref.shape[1]] = factor_ref[at * 8 : (at + 1) * 8, :]
     response = response_ref[...].astype(F32)
     lane = lane_iota()
     lane_square = lax.broadcasted_iota(jnp.int32, (LANES, LANES), 1)
@@ -55,7 +61,7 @@
     for z in range(nz):
         total = jnp.zeros((16, SIDES * LANES), F32)
         for block in range(SIDES):
-            row = order_ref[z : z + 1, block * LANES : (block + 1) * LANES]
+            row = order_ref[z, :, block * LANES : (block + 1) * LANES]
             column = jnp.broadcast_to(row, (LANES, LANES)).T
             hot = jnp.concatenate(
                 [
@@ -75,16 +81,22 @@
             high_ref[z * SIDES + side] = high
             faces_ref[z * SIDES + side] = pick_lanes(own, high, low)
         for corner in range(CORNERS):
-            ids = jnp.where(lane == z * CORNERS + corner, corners_ref[z, corner], ids)
+            ids = jnp.where(lane == z * CORNERS + corner, corners_ref[z, 0, corner], ids)
     ids_ref[...] = ids
 
 
-def factor_kernel(count, factor_ref, inverse_ref, square):
+def factor_kernel(count, place_ref, *refs):
+    *blocks, inverse_ref, square = refs
     size = square.shape[0]
     row = lax.broadcasted_iota(jnp.int32, (size, size), 0)
     column = lax.broadcasted_iota(jnp.int32, (size, size), 1)
     square[...] = jnp.where(row == column, 1.0, 0.0)
-    square[0:count, 0:count] = factor_ref[...]
+    for mask, block in zip((0, 1, 3, 2), blocks):
+        tall = block.shape[0] * 8
+        start = lax.bitwise_xor(place_ref[2], mask) * tall
+        for at in range(block.shape[0]):
+            square[pl.ds(pl.multiple_of(start + at * 8, 8), 8), :] = block[at]
+    square[...] = jnp.where(row < count, square[...], jnp.where(row == column, 1.0, 0.0))
     factor = square[...]
     inverse = jnp.where(row == column, 1.0 / factor, 0.0)
     width = 1
@@ -161,7 +173,7 @@
         tile = jnp.zeros((8, LANES), F32)
         for z in range(nz):
             for corner in range(CORNERS):
-                tile += jnp.where(where == corners_ref[z, corner], terms[z][:, corner : corner + 1], 0.0)
+                tile += jnp.where(where == corners_ref[z, 0, corner], terms[z][:, corner : corner + 1], 0.0)
         for at, number in enumerate(numbers):
             tile += jnp.where(where == ncoarse + at, number, 0.0)
         sums_ref[block] = tile
@@ -173,8 +185,8 @@
     response_ref, high_ref, low_ref, response_faces_ref, ids_ref,
     residual_ref, faces_ref, sums_ref, x_first, x_second, y_first, y_second,
 ):
-    own = [rhs_ref[z][:, d, :] for z in range(nz) for d in range(3)]
-    back = [back_x_ref[z][:, 0, :] for z in range(nz)] + [back_y_ref[z][:, 1, :] for z in range(nz)]
+    own = [rhs_ref[at] for at in range(nz * 3)]
+    back = [back_x_ref[z * 3] for z in range(nz)] + [back_y_ref[z * 3 + 1] for z in range(nz)]
     for at, tile in enumerate(own + back):
         residual_ref[at] = tile
     refs = (order_ref, matrix_ref, response_ref, corners_ref, high_ref, low_ref, faces_ref, sums_ref)
@@ -304,9 +316,8 @@
             direction = old_residual if first else old_residual + ratio * direction_ref[at]
             multipliers = step * direction if first else multipliers_ref[at] + step * direction
             if last:
-                z, d = divmod(at, 3)
-                out_multipliers[z, :, d, :] = multipliers
-                out_residual[z, :, d, :] = residual[at]
+                out_multipliers[at] = multipliers
+                out_residual[at] = residual[at]
             else:
                 out_direction[at] = direction
                 out_multipliers[at] = multipliers
@@ -355,43 +366,46 @@
     return lax.ppermute(value, axis, [(i, (i + 1 if i % 2 else i - 1) % count) for i in range(count)])
 
 
-def exchange(sums, sends):
+def exchange(sums, sends, rows=None):
     lead = sums.shape[0]
     x_first, x_second, y_first, y_second = sends
-    got_x_second = paired_other(x_second, "sub")
+    near = x_first.shape[0]
+    blocks = []
+    if lax.axis_size("slab") == 4:
+        extra = [] if rows is None else [rows]
+        got = paired(jnp.concatenate([sums, y_first] + extra), "slab", 1)
+        sums, got_y_first = sums + got[:lead], got[lead : lead + near]
+        extra += [] if rows is None else [got[lead + near :]]
+        got = paired(jnp.concatenate([sums, y_second] + extra), "slab", 3)
+        sums, got_y_second = sums + got[:lead], got[lead : lead + near]
+        if rows is not None:
+            count = rows.shape[0]
+            blocks = extra + [got[lead + near : lead + near + count], got[lead + near + count :]]
+    else:
+        got_y_first, got_y_second = paired(y_first, "slab", 1), paired_other(y_second, "slab")
+        sums = doubled(sums, "slab", 1)
     got = paired(jnp.concatenate([sums, x_first]), "sub", 1)
     sums, got_x_first = sums + got[:lead], got[lead:]
-    got = paired(jnp.concatenate([sums, y_first]), "slab", 1)
-    sums, got_y_first = sums + got[:lead], got[lead:]
-    mask = 2
-    if lax.axis_size("slab") == 4:
-        got = paired(jnp.concatenate([sums, y_second]), "slab", 3)
-        sums, got_y_second = sums + got[:lead], got[lead:]
-        mask = 4
-    else:
-        got_y_second = paired_other(y_second, "slab")
-    while mask < lax.axis_size("slab"):
-        sums = sums + paired(sums, "slab", mask)
+    got = paired_other(jnp.concatenate([sums, x_second]), "sub")
+    got_x_second = got[lead:]
+    if lax.axis_size("sub") == 8:
+        beside, opposite = got[:lead], paired(sums, "sub", 4)
+        sums = sums + opposite + (beside + paired(beside, "sub", 1))
+    else:
+        sums = doubled(sums, "sub", 2)
+    return sums, [got_x_first, got_x_second, got_y_first, got_y_second], blocks
+
+
+def doubled(sums, axis, mask):
+    while mask < lax.axis_size(axis):
+        sums = sums + paired(sums, axis, mask)
         mask *= 2
-    mask = 2
-    while mask < lax.axis_size("sub"):
-        sums = sums + paired(sums, "sub", mask)
-        mask *= 2
-    return sums, [got_x_first, got_x_second, got_y_first, got_y_second]
+    return sums
 
 
 def coarse_inverse(coarse_factor, width):
     factor = lax.all_gather(coarse_factor, "slab", axis=0, tiled=True)
     count = factor.shape[0]
-    if count <= LANES == width:
-        return call(
-            functools.partial(factor_kernel, count),
-            [jax.ShapeDtypeStruct((LANES, LANES), F32)],
-            [factor],
-            0,
-            2**26,
-            [pltpu.VMEM((LANES, LANES), F32)],
-        )[0]
     inverse = lax.linalg.triangular_solve(
         factor, jnp.eye(count, dtype=F32), left_side=True, lower=True
     )
@@ -405,24 +419,26 @@
     ncoarse = coarse_factor.shape[1]
     local_size = SIDES * face
     blocks = -(-(ncoarse + 3) // LANES)
-    rhs = interface_rhs.reshape(nz, samples, dirs, face)
-    order = order.reshape(nz, local_size)
+    rhs = interface_rhs.transpose(0, 1, 2, 4, 3, 5).reshape(nz * dirs, samples, face)
+    order = order.reshape(nz, 1, local_size)
     matrices = inverse_rr.reshape(nz, local_size, local_size)
     responses = corner_response.reshape(nz, CORNERS, local_size)
-    corners = corners.reshape(nz, CORNERS)
-    parity = jnp.stack([lax.axis_index("sub") % 2, lax.axis_index("slab") % 2]).astype(jnp.int32)
+    corners = corners.reshape(nz, 1, CORNERS)
+    place = lax.axis_index("slab")
+    parity = jnp.stack([lax.axis_index("sub") % 2, place % 2, place]).astype(jnp.int32)
 
     back_x = shifted(rhs, "sub", 1)
     back_y = shifted(rhs, "slab", 1)
-    inverse = coarse_inverse(coarse_factor, blocks * LANES)
+    riding = blocks == 1 and lax.axis_size("slab") == 4 and coarse_factor.shape[0] % 8 == 0
     tables = nz * SIDES
-    high, low, response_faces, ids = call(
+    rows = coarse_factor.shape[0] // 8 if riding else 1
+    high, low, response_faces, ids, rows = call(
         functools.partial(prepare_kernel, nz),
         [tiles(tables, jnp.int32), tiles(tables, jnp.int32), tiles(tables),
-         jax.ShapeDtypeStruct((8, LANES), jnp.int32)],
-        [corners, order, responses],
+         jax.ShapeDtypeStruct((8, LANES), jnp.int32), tiles(rows)],
+        [corners, order, responses, matrices, coarse_factor[: rows * 8, :LANES]],
         1,
-        2**26,
+        2**30,
     )
     own = [order, matrices, responses, high, low]
     residual, faces, sums, *sends = call(
@@ -430,29 +446,41 @@
         [tiles(nz * 5), tiles(tables), tiles(blocks)] + [tiles(2 * nz + 1)] * 4,
         [parity, corners, rhs, back_x, back_y] + own + [response_faces, ids],
         2,
-        2**28,
+        2**30,
     )
     state = [residual, ids]
     for iteration in range(ITERS):
         first, last = iteration == 0, iteration == ITERS - 1
-        sums, received = exchange(sums, sends)
+        sums, received, factor = exchange(sums, sends, rows if first and riding else None)
+        if first and riding:
+            square = jax.ShapeDtypeStruct((LANES, LANES), F32)
+            inverse = call(
+                functools.partial(factor_kernel, ncoarse), [square], [parity] + factor, 1, 3 * 2**30,
+                [pltpu.VMEM(square.shape, F32)],
+            )[0]
+        elif first:
+            inverse = coarse_inverse(coarse_factor, blocks * LANES)
         operands = [parity, corners, sums, inverse] + received + [faces, response_faces] + state
         kernel = functools.partial(step_kernel, first, last, nz, ncoarse)
         if last:
-            shape = jax.ShapeDtypeStruct(rhs.shape, F32)
-            multipliers, residual = call(kernel, [shape, shape], operands, 2, 2**24)
+            multipliers, residual = call(kernel, [tiles(nz * 3)] * 2, operands, 2, 2**30)
             break
         outs = [tiles(nz * 5), tiles(nz * 5), tiles(nz * 3), tiles(nz * 3), tiles(2)]
         outs += [tiles(tables), tiles(blocks)] + [tiles(nz)] * 4
         if first:
             outs += [jax.ShapeDtypeStruct((8, LANES), jnp.int32), tiles(nz * 4)]
-        results = call(kernel, outs, operands + own, 2, 2**28)
+        results = call(kernel, outs, operands + own, 2, 2**31)
         residual, image, direction, multipliers, scalars, faces, sums = results[:7]
         sends = results[7:11]
         if first:
             ids, near = results[11:]
         state = [residual, ids, near, image, direction, multipliers, scalars]
-    return multipliers.reshape(interface_rhs.shape), residual.reshape(interface_rhs.shape)
+
+    def placed(value):
+        value = value.reshape(interface_rhs.shape[:3] + (dirs, samples, face))
+        return value.transpose(0, 1, 2, 4, 3, 5)
+
+    return placed(multipliers), placed(residual)
 
 
 def solution(mesh):

time: 79.8 us -> 70.7 us (0.89)
  blocking collectives: 8.23 us -> 0 us
  starting transfers between devices: 21.5 us -> 19.6 us
  local copies, waits for them, and re-layouts: 6.23 us -> 4.93 us
  Pallas kernels: 11.3 us -> 12.4 us
  waiting for transfers between devices: 31.2 us -> 32.3 us
    all_gather x1 -> x0, blocking collectives: 8.23 us -> none  [coarse_inverse(): factor = lax.all_gather(coarse_factor, 'slab', axis=0, tiled=True)]
    ppermute x15, starting transfers between devices: 16.6 us -> 8.67 us  [paired(): lax.ppermute(value, axis, [(i, i ^ mask) for i in range(lax.axis_size(axi...]
    ppermute x3, waiting for transfers between devices: 0.01 us -> 7.14 us  [paired_other(): lax.ppermute(value, axis, [(i, (i + 1 if i % 2 else i - 1) % count) for i...]
    ppermute x3, starting transfers between devices: 1.9 us -> 7.91 us  [paired_other(): lax.ppermute(value, axis, [(i, (i + 1 if i % 2 else i - 1) % count) for i...]
    ppermute x15, waiting for transfers between devices: 29.6 us -> 25.2 us  [paired(): lax.ppermute(value, axis, [(i, i ^ mask) for i in range(lax.axis_size(axi...]
    ppermute x2, waiting for transfers between devices: 1.56 us -> 0.01 us  [shifted(): lax.ppermute(value, axis, [(i, (i + steps) % count) for i in range(count)])]
    unnamed x15 -> x20, local copies, waits for them, and re-layouts: 6.2 us -> 4.88 us
    pallas_call x6, Pallas kernels: 11.3 us -> 12.4 us  [call(): pl.pallas_call(kernel, out_shape=outs, in_specs=[smem] * scalars + [vmem]...]
  transfers between devices with their start and end apart: 20 -> 20, of which waited for: 14 -> 15; matrix products, arithmetic and copies ran while one was open for 2% -> 0% of each run, Pallas kernels for 6% -> 8%
where the time goes in v2:
time: 70.7 us; the launch traced here: 70.3 us
  waiting for transfers between devices  32.3 us (46%)
  starting transfers between devices  19.6 us (28%)
  Pallas kernels  12.4 us (18%)
  local copies, waits for them, and re-layouts  4.93 us (7%)
  between operations  0.9 us (1%)
    ppermute x15, waiting for transfers between devices, paired(): lax.ppermute(value, axis, [(i, i ^ mask) for i in range(lax.axis_size(axi...  25.2 us
    pallas_call x6, Pallas kernels, call(): pl.pallas_call(kernel, out_shape=outs, in_specs=[smem] * scalars + [vmem]...  12.4 us
    ppermute x15, starting transfers between devices, paired(): lax.ppermute(value, axis, [(i, i ^ mask) for i in range(lax.axis_size(axi...  8.67 us
    ppermute x3, starting transfers between devices, paired_other(): lax.ppermute(value, axis, [(i, (i + 1 if i % 2 else i - 1) % count) for i...  7.91 us
    ppermute x3, waiting for transfers between devices, paired_other(): lax.ppermute(value, axis, [(i, (i + 1 if i % 2 else i - 1) % count) for i...  7.14 us
    unnamed x20, local copies, waits for them, and re-layouts  4.88 us
    ppermute x2, starting transfers between devices, shifted(): lax.ppermute(value, axis, [(i, (i + steps) % count) for i in range(count)])  2.99 us
  transfers between devices with their start and end apart: 20, of which 15 were waited for; matrix products, arithmetic and copies ran while one was open for 0% of the time, Pallas kernels for 8%

profile of v2, /device:TPU:0, one launch (start us, length us, event | category | flops | bytes accessed | tf_op | source)
XLA Modules:
  0.0 70.3 jit_solution(17026928909898831765)
XLA Ops:
  0.6 3.0 %collective-permute-start.1 = (f32[9,8,128]{2,1,0:T(8,128)}, f32[9,8,128]{2,1,0:T(8,128)S(1)}, u32[]{:S(2)}, u32[]{:S(2)}) collective-permute-start(f32[9,8,128]{2,1,0:T(8,128)} %bitcast.20), channel_id=1, source_target_pairs={{0,1},{1,2},{2,3},{3,0},{4,5},{5,6},{6,7},{7,4},{8,9},{9,10},{10,1... | collective-permute-start | bytes 110600 | tf_op jit(solution)/shard_map/ppermute | solution.py:357
  3.6 0.0 collective-permute-start
  3.6 0.1 pad_add_fusion.parity_ref.place_ref.refs_0_
  3.7 2.0 %copy-done = bf16[1,1,3,768,768]{4,3,2,1,0:T(8,128)(2,1)S(1)} copy-done((bf16[1,1,3,768,768]{4,3,2,1,0:T(8,128)(2,1)S(1)}, bf16[1,1,3,768,768]{4,3,2,1,0:T(8,128)(2,1)}, u32[]{:S(2)}) %copy-start) | copy-done | bytes 3538968
  5.7 0.8 %copy-done.3 = bf16[1,1,3,8,768]{4,3,2,1,0:T(8,128)(2,1)S(1)} copy-done((bf16[1,1,3,8,768]{4,3,2,1,0:T(8,128)(2,1)S(1)}, bf16[1,1,3,8,768]{4,3,2,1,0:T(8,128)(2,1)}, u32[]{:S(2)}) %copy-start.3) | copy-done | bytes 36888
  6.5 0.7 %copy-done.5 = f32[24,96]{1,0:T(8,128)S(1)} copy-done((f32[24,96]{1,0:T(8,128)S(1)}, f32[24,96]{1,0:T(8,128)}, u32[]{:S(2)}) %copy-start.5) | copy-done | bytes 9240
  7.2 0.7 copy-done.6
  7.9 0.7 copy-done.8
  8.6 1.5 %shard_map.77 = (s32[18,8,128]{2,1,0:T(8,128)S(1)}, s32[18,8,128]{2,1,0:T(8,128)S(1)}, f32[18,8,128]{2,1,0:T(8,128)S(1)}, s32[8,128]{1,0:T(8,128)S(1)}, f32[3,8,128]{2,1,0:T(8,128)S(1)}) custom-call(s32[3,1,8]{2,1,0:T(1,128)S(1)} %bitcast.31, s32[3,1,768]{2,1,0:T(1,128)S(1)} %bitcast.27, bf16[3,8,768]{2,1,0:T(8,128)(2,1)S(1)} %bitcast.23, ...), custom_call_target="tpu_custom_call" | custom-call | flops 1073741824 | bytes 1048576 | tf_op jit(solution)/shard_map/pallas_call | solution.py:344
  10.1 0.0 collective-permute-done.1.back_y_ref
  10.1 0.0 collective-permute-done.back_x_ref
  10.1 1.4 %shard_map.78 = (f32[15,8,128]{2,1,0:T(8,128)S(1)}, f32[18,8,128]{2,1,0:T(8,128)S(1)}, f32[1,8,128]{2,1,0:T(8,128)S(1)}, f32[7,8,128]{2,1,0:T(8,128)S(1)}, f32[7...) custom-call(s32[3]{0:T(128)S(1)} %pad_add_fusion.parity_ref.place_ref.refs_0_, ...), custom_call_target="tpu_custom_call" | custom-call | flops 1073741824 | bytes 1048576 | tf_op jit(solution)/shard_map/pallas_call | solution.py:344
  11.5 1.6 %collective-permute-start.2 = (f32[11,8,128]{2,1,0:T(8,128)S(1)}, f32[11,8,128]{2,1,0:T(8,128)S(1)}, u32[]{:S(2)}, u32[]{:S(2)}) collective-permute-start(f32[11,8,128]{2,1,0:T(8,128)S(1)} %pad_maximum_fusion.1), channel_id=1, source_target_pairs={{0,1},{1,0},{2,3},{3,2},{4,5},{5,4},{6,7},{7,6},{8,9},{9,8},{10,11... | collective-permute-start | bytes 135176 | tf_op jit(solution)/shard_map/ppermute | solution.py:361
  13.1 2.6 %collective-permute-done.2 = f32[11,8,128]{2,1,0:T(8,128)S(1)} collective-permute-done((f32[11,8,128]{2,1,0:T(8,128)S(1)}, f32[11,8,128]{2,1,0:T(8,128)S(1)}, u32[]{:S(2)}, u32[]{:S(2)}) %collective-permute-start.2) | collective-permute-done | bytes 45088 | tf_op jit(solution)/shard_map/ppermute | solution.py:361
  15.6 1.1 %collective-permute-start.3 = (f32[14,8,128]{2,1,0:T(8,128)S(1)}, f32[14,8,128]{2,1,0:T(8,128)S(1)}, u32[]{:S(2)}, u32[]{:S(2)}) collective-permute-start(f32[14,8,128]{2,1,0:T(8,128)S(1)} %pad_maximum_fusion), channel_id=1, source_target_pairs={{0,3},{1,2},{2,1},{3,0},{4,7},{5,6},{6,5},{7,4},{8,11},{9,10},{10,... | collective-permute-start | bytes 172040 | tf_op jit(solution)/shard_map/ppermute | solution.py:361
  16.8 4.2 %collective-permute-done.3 = f32[14,8,128]{2,1,0:T(8,128)S(1)} collective-permute-done((f32[14,8,128]{2,1,0:T(8,128)S(1)}, f32[14,8,128]{2,1,0:T(8,128)S(1)}, u32[]{:S(2)}, u32[]{:S(2)}) %collective-permute-start.3) | collective-permute-done | bytes 57376 | tf_op jit(solution)/shard_map/ppermute | solution.py:361
  21.0 0.0 collective-permute-start.4
  21.0 1.2 %collective-permute-done.4 = f32[8,8,128]{2,1,0:T(8,128)S(1)} collective-permute-done((f32[8,8,128]{2,1,0:T(8,128)S(1)}, f32[8,8,128]{2,1,0:T(8,128)S(1)}, u32[]{:S(2)}, u32[]{:S(2)}) %collective-permute-start.4) | collective-permute-done | bytes 32800 | tf_op jit(solution)/shard_map/ppermute | solution.py:361
  22.2 3.2 %collective-permute-start.6 = (f32[8,8,128]{2,1,0:T(8,128)S(1)}, f32[8,8,128]{2,1,0:T(8,128)S(1)}, u32[]{:S(2)}, u32[]{:S(2)}) collective-permute-start(f32[8,8,128]{2,1,0:T(8,128)S(1)} %pad_maximum_fusion.3), channel_id=1, source_target_pairs={{0,28},{4,8},{8,4},{12,16},{16,12},{20,24},{24,20},{28,0},{1,29},{... | collective-permute-start | bytes 98312 | tf_op jit(solution)/shard_map/ppermute | solution.py:366
  25.4 0.0 collective-permute-start.5
  25.4 1.9 %collective-permute-done.6 = f32[8,8,128]{2,1,0:T(8,128)S(1)} collective-permute-done((f32[8,8,128]{2,1,0:T(8,128)S(1)}, f32[8,8,128]{2,1,0:T(8,128)S(1)}, u32[]{:S(2)}, u32[]{:S(2)}) %collective-permute-start.6) | collective-permute-done | bytes 32800 | tf_op jit(solution)/shard_map/ppermute | solution.py:366
  27.4 0.0 copy-start.7
  27.4 0.0 copy-start.9
  27.4 3.9 %shard_map.79.refs_3_ = f32[128,128]{1,0:T(8,128)S(1)} custom-call(s32[3]{0:T(128)S(1)} %pad_add_fusion.parity_ref.place_ref.refs_0_, f32[3,8,128]{2,1,0:T(8,128)S(1)} %get-tuple-element.46.refs_0_, f32[3,8,128]{2,1,0:T(8,128)S(1)} %slice.109.refs_1_, f32[3,8,128]{2,1,0:T(8,128)S(1)} %get-tuple-element.79.refs_2_, f32[3,8,128]{2,1,0:T(8,128)S(1)} %get-tuple-element.78.refs_3_), custom_call_target="tpu_custom_call" | custom-call | flops 3221225472 | bytes 1048576 | tf_op jit(solution)/shard_map/pallas_call | solution.py:344
  31.3 0.0 collective-permute-done.5
  31.4 2.0 %shard_map.80 = (f32[15,8,128]{2,1,0:T(8,128)S(1)}, f32[15,8,128]{2,1,0:T(8,128)S(1)}, f32[9,8,128]{2,1,0:T(8,128)S(1)}, f32[9,8,128]{2,1,0:T(8,128)S(1)}, f32[2...) custom-call(s32[3]{0:T(128)S(1)} %pad_add_fusion.parity_ref.place_re, ...), custom_call_target="tpu_custom_call" | custom-call | flops 2147483648 | bytes 1048576 | tf_op jit(solution)/shard_map/pallas_call | solution.py:344
  33.4 1.6 %collective-permute-start.8 = (f32[4,8,128]{2,1,0:T(8,128)S(1)}, f32[4,8,128]{2,1,0:T(8,128)S(1)}, u32[]{:S(2)}, u32[]{:S(2)}) collective-permute-start(f32[4,8,128]{2,1,0:T(8,128)S(1)} %pad_maximum_fusion.4), channel_id=1, source_target_pairs={{0,1},{1,0},{2,3},{3,2},{4,5},{5,4},{6,7},{7,6},{8,9},{9,8},{10,11... | collective-permute-start | bytes 49160 | tf_op jit(solution)/shard_map/ppermute | solution.py:361
  35.0 2.2 %collective-permute-done.8 = f32[4,8,128]{2,1,0:T(8,128)S(1)} collective-permute-done((f32[4,8,128]{2,1,0:T(8,128)S(1)}, f32[4,8,128]{2,1,0:T(8,128)S(1)}, u32[]{:S(2)}, u32[]{:S(2)}) %collective-permute-start.8) | collective-permute-done | bytes 16416 | tf_op jit(solution)/shard_map/ppermute | solution.py:361
  37.2 1.4 %collective-permute-start.9 = (f32[4,8,128]{2,1,0:T(8,128)S(1)}, f32[4,8,128]{2,1,0:T(8,128)S(1)}, u32[]{:S(2)}, u32[]{:S(2)}) collective-permute-start(f32[4,8,128]{2,1,0:T(8,128)S(1)} %pad_maximum_fusion.5), channel_id=1, source_target_pairs={{0,3},{1,2},{2,1},{3,0},{4,7},{5,6},{6,5},{7,4},{8,11},{9,10},{10,... | collective-permute-start | bytes 49160 | tf_op jit(solution)/shard_map/ppermute | solution.py:361
  38.6 3.2 %collective-permute-done.9 = f32[4,8,128]{2,1,0:T(8,128)S(1)} collective-permute-done((f32[4,8,128]{2,1,0:T(8,128)S(1)}, f32[4,8,128]{2,1,0:T(8,128)S(1)}, u32[]{:S(2)}, u32[]{:S(2)}) %collective-permute-start.9) | collective-permute-done | bytes 16416 | tf_op jit(solution)/shard_map/ppermute | solution.py:361
  41.9 0.0 collective-permute-start.10
  41.9 1.2 %collective-permute-done.10 = f32[4,8,128]{2,1,0:T(8,128)S(1)} collective-permute-done((f32[4,8,128]{2,1,0:T(8,128)S(1)}, f32[4,8,128]{2,1,0:T(8,128)S(1)}, u32[]{:S(2)}, u32[]{:S(2)}) %collective-permute-start.10) | collective-permute-done | bytes 16416 | tf_op jit(solution)/shard_map/ppermute | solution.py:361
  43.1 3.3 %collective-permute-start.12 = (f32[4,8,128]{2,1,0:T(8,128)S(1)}, f32[4,8,128]{2,1,0:T(8,128)S(1)}, u32[]{:S(2)}, u32[]{:S(2)}) collective-permute-start(f32[4,8,128]{2,1,0:T(8,128)S(1)} %pad_maximum_fusion.7), channel_id=1, source_target_pairs={{0,28},{4,8},{8,4},{12,16},{16,12},{20,24},{24,20},{28,0},{1,29},{... | collective-permute-start | bytes 49160 | tf_op jit(solution)/shard_map/ppermute | solution.py:366
  46.4 1.6 %collective-permute-done.12 = f32[4,8,128]{2,1,0:T(8,128)S(1)} collective-permute-done((f32[4,8,128]{2,1,0:T(8,128)S(1)}, f32[4,8,128]{2,1,0:T(8,128)S(1)}, u32[]{:S(2)}, u32[]{:S(2)}) %collective-permute-start.12) | collective-permute-done | bytes 16416 | tf_op jit(solution)/shard_map/ppermute | solution.py:366
  48.0 0.0 collective-permute-start.13
  48.1 2.8 %collective-permute-done.11 = f32[1,8,128]{2,1,0:T(8,128)S(1)} collective-permute-done((f32[1,8,128]{2,1,0:T(8,128)S(1)}, f32[1,8,128]{2,1,0:T(8,128)S(1)}, u32[]{:S(2)}, u32[]{:S(2)}) %collective-permute-start.11) | collective-permute-done | bytes 4128 | tf_op jit(solution)/shard_map/ppermute | solution.py:361
  50.9 2.0 %shard_map.81 = (f32[15,8,128]{2,1,0:T(8,128)S(1)}, f32[15,8,128]{2,1,0:T(8,128)S(1)}, f32[9,8,128]{2,1,0:T(8,128)S(1)}, f32[9,8,128]{2,1,0:T(8,128)S(1)}, f32[2...) custom-call(s32[3]{0:T(128)S(1)} %pad_add_fusion.parity_ref.place_re, ...), custom_call_target="tpu_custom_call" | custom-call | flops 2147483648 | bytes 1048576 | tf_op jit(solution)/shard_map/pallas_call | solution.py:344
  52.9 1.6 %collective-permute-start.14 = (f32[4,8,128]{2,1,0:T(8,128)S(1)}, f32[4,8,128]{2,1,0:T(8,128)S(1)}, u32[]{:S(2)}, u32[]{:S(2)}) collective-permute-start(f32[4,8,128]{2,1,0:T(8,128)S(1)} %pad_maximum_fusion.8), channel_id=1, source_target_pairs={{0,1},{1,0},{2,3},{3,2},{4,5},{5,4},{6,7},{7,6},{8,9},{9,8},{10,11... | collective-permute-start | bytes 49160 | tf_op jit(solution)/shard_map/ppermute | solution.py:361
  54.4 2.2 %collective-permute-done.14 = f32[4,8,128]{2,1,0:T(8,128)S(1)} collective-permute-done((f32[4,8,128]{2,1,0:T(8,128)S(1)}, f32[4,8,128]{2,1,0:T(8,128)S(1)}, u32[]{:S(2)}, u32[]{:S(2)}) %collective-permute-start.14) | collective-permute-done | bytes 16416 | tf_op jit(solution)/shard_map/ppermute | solution.py:361
  56.7 1.4 %collective-permute-start.15 = (f32[4,8,128]{2,1,0:T(8,128)S(1)}, f32[4,8,128]{2,1,0:T(8,128)S(1)}, u32[]{:S(2)}, u32[]{:S(2)}) collective-permute-start(f32[4,8,128]{2,1,0:T(8,128)S(1)} %pad_maximum_fusion.9), channel_id=1, source_target_pairs={{0,3},{1,2},{2,1},{3,0},{4,7},{5,6},{6,5},{7,4},{8,11},{9,10},{10,... | collective-permute-start | bytes 49160 | tf_op jit(solution)/shard_map/ppermute | solution.py:361
  58.1 3.2 %collective-permute-done.15 = f32[4,8,128]{2,1,0:T(8,128)S(1)} collective-permute-done((f32[4,8,128]{2,1,0:T(8,128)S(1)}, f32[4,8,128]{2,1,0:T(8,128)S(1)}, u32[]{:S(2)}, u32[]{:S(2)}) %collective-permute-start.15) | collective-permute-done | bytes 16416 | tf_op jit(solution)/shard_map/ppermute | solution.py:361
  61.4 0.0 collective-permute-start.16
  61.4 1.2 %collective-permute-done.16 = f32[4,8,128]{2,1,0:T(8,128)S(1)} collective-permute-done((f32[4,8,128]{2,1,0:T(8,128)S(1)}, f32[4,8,128]{2,1,0:T(8,128)S(1)}, u32[]{:S(2)}, u32[]{:S(2)}) %collective-permute-start.16) | collective-permute-done | bytes 16416 | tf_op jit(solution)/shard_map/ppermute | solution.py:361
  62.5 1.4 %collective-permute-start.18 = (f32[4,8,128]{2,1,0:T(8,128)S(1)}, f32[4,8,128]{2,1,0:T(8,128)S(1)}, u32[]{:S(2)}, u32[]{:S(2)}) collective-permute-start(f32[4,8,128]{2,1,0:T(8,128)S(1)} %pad_maximum_fusion.11), channel_id=1, source_target_pairs={{0,28},{4,8},{8,4},{12,16},{16,12},{20,24},{24,20},{28,0},{1,29},{... | collective-permute-start | bytes 49160 | tf_op jit(solution)/shard_map/ppermute | solution.py:366
  63.9 3.6 %collective-permute-done.18 = f32[4,8,128]{2,1,0:T(8,128)S(1)} collective-permute-done((f32[4,8,128]{2,1,0:T(8,128)S(1)}, f32[4,8,128]{2,1,0:T(8,128)S(1)}, u32[]{:S(2)}, u32[]{:S(2)}) %collective-permute-start.18) | collective-permute-done | bytes 16416 | tf_op jit(solution)/shard_map/ppermute | solution.py:366
  67.6 0.9 %collective-permute-done.17 = f32[1,8,128]{2,1,0:T(8,128)S(1)} collective-permute-done((f32[1,8,128]{2,1,0:T(8,128)S(1)}, f32[1,8,128]{2,1,0:T(8,128)S(1)}, u32[]{:S(2)}, u32[]{:S(2)}) %collective-permute-start.17) | collective-permute-done | bytes 4128 | tf_op jit(solution)/shard_map/ppermute | solution.py:361
  68.4 0.2 collective-permute-done.19
  68.7 1.6 %shard_map.82 = (f32[9,8,128]{2,1,0:T(8,128)}, f32[9,8,128]{2,1,0:T(8,128)}) custom-call(s32[3]{0:T(128)S(1)} %pad_add_fusion.parity_ref.place_ref.refs_0_, s32[3,1,8]{2,1,0:T(1,128)S(1)} %bitcast.35, f32[1,8,128]{2,1,0:T(8,128)S(1)} %add_add_fusion.refs_2_, f32[128,128]{1,0:T(8,128)S(1)} %shard_map.79.refs_3_, f32[3,8,128]{2,1,0:T(8,128)S(1)} %slice.131.refs_4_, ...), custom_call_target="tpu_custom_call" | custom-call | flops 1073741824 | bytes 1048576 | tf_op jit(solution)/shard_map/pallas_call | solution.py:344
  (60 shorter events, 0.2 us)
Async XLA Ops:
  0.6 9.5 %copy-start.2 = (f32[1,1,3,8,3,128]{5,3,4,2,1,0:T(8,128)S(1)}, f32[1,1,3,8,3,128]{5,3,4,2,1,0:T(8,128)}, u32[]{:S(2)}) copy-start(f32[1,1,3,8,3,128]{5,3,4,2,1,0:T(8,128)} %param.6) | copy-start | bytes 110596
  0.6 9.4 %collective-permute-start.1 = (f32[9,8,128]{2,1,0:T(8,128)}, f32[9,8,128]{2,1,0:T(8,128)S(1)}, u32[]{:S(2)}, u32[]{:S(2)}) collective-permute-start(f32[9,8,128]{2,1,0:T(8,128)} %bitcast.20), channel_id=1, source_target_pairs={{0,1},{1,2},{2,3},{3,0},{4,5},{5,6},{6,7},{7,4},{8,9},{9,10},{10,1... | collective-permute-start | bytes 110600 | tf_op jit(solution)/shard_map/ppermute | solution.py:357
  3.6 6.5 %collective-permute-start = (f32[9,8,128]{2,1,0:T(8,128)}, f32[9,8,128]{2,1,0:T(8,128)S(1)}, u32[]{:S(2)}, u32[]{:S(2)}) collective-permute-start(f32[9,8,128]{2,1,0:T(8,128)} %bitcast.21), channel_id=1, source_target_pairs={{0,4},{4,8},{8,12},{12,16},{16,20},{20,24},{24,28},{28,0},{1,5},{5... | collective-permute-start | bytes 110600 | tf_op jit(solution)/shard_map/ppermute | solution.py:357
  3.7 2.0 %copy-start = (bf16[1,1,3,768,768]{4,3,2,1,0:T(8,128)(2,1)S(1)}, bf16[1,1,3,768,768]{4,3,2,1,0:T(8,128)(2,1)}, u32[]{:S(2)}) copy-start(bf16[1,1,3,768,768]{4,3,2,1,0:T(8,128)(2,1)} %param.8) | copy-start | bytes 10616836
  5.7 0.8 %copy-start.3 = (bf16[1,1,3,8,768]{4,3,2,1,0:T(8,128)(2,1)S(1)}, bf16[1,1,3,8,768]{4,3,2,1,0:T(8,128)(2,1)}, u32[]{:S(2)}) copy-start(bf16[1,1,3,8,768]{4,3,2,1,0:T(8,128)(2,1)} %param.9) | copy-start | bytes 110596
  6.5 0.7 %copy-start.5 = (f32[24,96]{1,0:T(8,128)S(1)}, f32[24,96]{1,0:T(8,128)}, u32[]{:S(2)}) copy-start(f32[24,96]{1,0:T(8,128)} %factor_ref.1) | copy-start | bytes 27652
  7.2 0.7 copy-start.6
  7.9 0.7 copy-start.8
  11.5 4.1 %collective-permute-start.2 = (f32[11,8,128]{2,1,0:T(8,128)S(1)}, f32[11,8,128]{2,1,0:T(8,128)S(1)}, u32[]{:S(2)}, u32[]{:S(2)}) collective-permute-start(f32[11,8,128]{2,1,0:T(8,128)S(1)} %pad_maximum_fusion.1), channel_id=1, source_target_pairs={{0,1},{1,0},{2,3},{3,2},{4,5},{5,4},{6,7},{7,6},{8,9},{9,8},{10,11... | collective-permute-start | bytes 135176 | tf_op jit(solution)/shard_map/ppermute | solution.py:361
  15.6 5.3 %collective-permute-start.3 = (f32[14,8,128]{2,1,0:T(8,128)S(1)}, f32[14,8,128]{2,1,0:T(8,128)S(1)}, u32[]{:S(2)}, u32[]{:S(2)}) collective-permute-start(f32[14,8,128]{2,1,0:T(8,128)S(1)} %pad_maximum_fusion), channel_id=1, source_target_pairs={{0,3},{1,2},{2,1},{3,0},{4,7},{5,6},{6,5},{7,4},{8,11},{9,10},{10,... | collective-permute-start | bytes 172040 | tf_op jit(solution)/shard_map/ppermute | solution.py:361
  21.0 1.2 %collective-permute-start.4 = (f32[8,8,128]{2,1,0:T(8,128)S(1)}, f32[8,8,128]{2,1,0:T(8,128)S(1)}, u32[]{:S(2)}, u32[]{:S(2)}) collective-permute-start(f32[8,8,128]{2,1,0:T(8,128)S(1)} %pad_maximum_fusion.2), channel_id=1, source_target_pairs={{0,4},{4,0},{8,12},{12,8},{16,20},{20,16},{24,28},{28,24},{1,5},{5... | collective-permute-start | bytes 98312 | tf_op jit(solution)/shard_map/ppermute | solution.py:361
  22.2 5.1 %collective-permute-start.6 = (f32[8,8,128]{2,1,0:T(8,128)S(1)}, f32[8,8,128]{2,1,0:T(8,128)S(1)}, u32[]{:S(2)}, u32[]{:S(2)}) collective-permute-start(f32[8,8,128]{2,1,0:T(8,128)S(1)} %pad_maximum_fusion.3), channel_id=1, source_target_pairs={{0,28},{4,8},{8,4},{12,16},{16,12},{20,24},{24,20},{28,0},{1,29},{... | collective-permute-start | bytes 98312 | tf_op jit(solution)/shard_map/ppermute | solution.py:366
  25.4 5.9 %collective-permute-start.5 = (f32[1,8,128]{2,1,0:T(8,128)S(1)}, f32[1,8,128]{2,1,0:T(8,128)S(1)}, u32[]{:S(2)}, u32[]{:S(2)}) collective-permute-start(f32[1,8,128]{2,1,0:T(8,128)S(1)} %slice_add_fusion.6), channel_id=1, source_target_pairs={{0,16},{4,20},{8,24},{12,28},{16,0},{20,4},{24,8},{28,12},{1,17},{... | collective-permute-start | bytes 12296 | tf_op jit(solution)/shard_map/ppermute | solution.py:361
  27.3 4.0 %collective-permute-start.7 = (f32[1,8,128]{2,1,0:T(8,128)S(1)}, f32[1,8,128]{2,1,0:T(8,128)S(1)}, u32[]{:S(2)}, u32[]{:S(2)}) collective-permute-start(f32[1,8,128]{2,1,0:T(8,128)S(1)} %slice.112), channel_id=1, source_target_pairs={{0,4},{4,0},{8,12},{12,8},{16,20},{20,16},{24,28},{28,24},{1,5},{5... | collective-permute-start | bytes 12296 | tf_op jit(solution)/shard_map/ppermute | solution.py:361
  27.3 4.0 %copy-start.1 = (bf16[1,1,3,768,768]{4,3,2,1,0:T(8,128)(2,1)S(1)}, bf16[1,1,3,768,768]{4,3,2,1,0:T(8,128)(2,1)}, u32[]{:S(2)}) copy-start(bf16[1,1,3,768,768]{4,3,2,1,0:T(8,128)(2,1)} %param.8) | copy-start | bytes 10616836
  27.3 4.0 %copy-start.4 = (bf16[1,1,3,8,768]{4,3,2,1,0:T(8,128)(2,1)S(1)}, bf16[1,1,3,8,768]{4,3,2,1,0:T(8,128)(2,1)}, u32[]{:S(2)}) copy-start(bf16[1,1,3,8,768]{4,3,2,1,0:T(8,128)(2,1)} %param.9) | copy-start | bytes 110596
  27.4 4.0 %copy-start.7 = (s32[1,1,3,768]{3,1,2,0:T(1,128)S(1)}, s32[1,1,3,768]{3,1,2,0:T(1,128)}, u32[]{:S(2)}) copy-start(s32[1,1,3,768]{3,1,2,0:T(1,128)} %param.7) | copy-start | bytes 27652
  27.4 4.0 %copy-start.9 = (s32[1,1,3,8]{3,1,2,0:T(1,128)S(1)}, s32[1,1,3,8]{3,1,2,0:T(1,128)}, u32[]{:S(2)}) copy-start(s32[1,1,3,8]{3,1,2,0:T(1,128)} %param.10) | copy-start | bytes 292
  33.4 3.8 %collective-permute-start.8 = (f32[4,8,128]{2,1,0:T(8,128)S(1)}, f32[4,8,128]{2,1,0:T(8,128)S(1)}, u32[]{:S(2)}, u32[]{:S(2)}) collective-permute-start(f32[4,8,128]{2,1,0:T(8,128)S(1)} %pad_maximum_fusion.4), channel_id=1, source_target_pairs={{0,1},{1,0},{2,3},{3,2},{4,5},{5,4},{6,7},{7,6},{8,9},{9,8},{10,11... | collective-permute-start | bytes 49160 | tf_op jit(solution)/shard_map/ppermute | solution.py:361
  37.2 4.6 %collective-permute-start.9 = (f32[4,8,128]{2,1,0:T(8,128)S(1)}, f32[4,8,128]{2,1,0:T(8,128)S(1)}, u32[]{:S(2)}, u32[]{:S(2)}) collective-permute-start(f32[4,8,128]{2,1,0:T(8,128)S(1)} %pad_maximum_fusion.5), channel_id=1, source_target_pairs={{0,3},{1,2},{2,1},{3,0},{4,7},{5,6},{6,5},{7,4},{8,11},{9,10},{10,... | collective-permute-start | bytes 49160 | tf_op jit(solution)/shard_map/ppermute | solution.py:361
  41.9 1.2 %collective-permute-start.10 = (f32[4,8,128]{2,1,0:T(8,128)S(1)}, f32[4,8,128]{2,1,0:T(8,128)S(1)}, u32[]{:S(2)}, u32[]{:S(2)}) collective-permute-start(f32[4,8,128]{2,1,0:T(8,128)S(1)} %pad_maximum_fusion.6), channel_id=1, source_target_pairs={{0,4},{4,0},{8,12},{12,8},{16,20},{20,16},{24,28},{28,24},{1,5},{5... | collective-permute-start | bytes 49160 | tf_op jit(solution)/shard_map/ppermute | solution.py:361
  43.1 5.0 %collective-permute-start.12 = (f32[4,8,128]{2,1,0:T(8,128)S(1)}, f32[4,8,128]{2,1,0:T(8,128)S(1)}, u32[]{:S(2)}, u32[]{:S(2)}) collective-permute-start(f32[4,8,128]{2,1,0:T(8,128)S(1)} %pad_maximum_fusion.7), channel_id=1, source_target_pairs={{0,28},{4,8},{8,4},{12,16},{16,12},{20,24},{24,20},{28,0},{1,29},{... | collective-permute-start | bytes 49160 | tf_op jit(solution)/shard_map/ppermute | solution.py:366
  46.4 4.5 %collective-permute-start.11 = (f32[1,8,128]{2,1,0:T(8,128)S(1)}, f32[1,8,128]{2,1,0:T(8,128)S(1)}, u32[]{:S(2)}, u32[]{:S(2)}) collective-permute-start(f32[1,8,128]{2,1,0:T(8,128)S(1)} %slice_add_fusion.3), channel_id=1, source_target_pairs={{0,16},{4,20},{8,24},{12,28},{16,0},{20,4},{24,8},{28,12},{1,17},{... | collective-permute-start | bytes 12296 | tf_op jit(solution)/shard_map/ppermute | solution.py:361
  48.0 2.9 %collective-permute-start.13 = (f32[1,8,128]{2,1,0:T(8,128)S(1)}, f32[1,8,128]{2,1,0:T(8,128)S(1)}, u32[]{:S(2)}, u32[]{:S(2)}) collective-permute-start(f32[1,8,128]{2,1,0:T(8,128)S(1)} %slice.122), channel_id=1, source_target_pairs={{0,4},{4,0},{8,12},{12,8},{16,20},{20,16},{24,28},{28,24},{1,5},{5... | collective-permute-start | bytes 12296 | tf_op jit(solution)/shard_map/ppermute | solution.py:361
  52.9 3.8 %collective-permute-start.14 = (f32[4,8,128]{2,1,0:T(8,128)S(1)}, f32[4,8,128]{2,1,0:T(8,128)S(1)}, u32[]{:S(2)}, u32[]{:S(2)}) collective-permute-start(f32[4,8,128]{2,1,0:T(8,128)S(1)} %pad_maximum_fusion.8), channel_id=1, source_target_pairs={{0,1},{1,0},{2,3},{3,2},{4,5},{5,4},{6,7},{7,6},{8,9},{9,8},{10,11... | collective-permute-start | bytes 49160 | tf_op jit(solution)/shard_map/ppermute | solution.py:361
  56.7 4.6 %collective-permute-start.15 = (f32[4,8,128]{2,1,0:T(8,128)S(1)}, f32[4,8,128]{2,1,0:T(8,128)S(1)}, u32[]{:S(2)}, u32[]{:S(2)}) collective-permute-start(f32[4,8,128]{2,1,0:T(8,128)S(1)} %pad_maximum_fusion.9), channel_id=1, source_target_pairs={{0,3},{1,2},{2,1},{3,0},{4,7},{5,6},{6,5},{7,4},{8,11},{9,10},{10,... | collective-permute-start | bytes 49160 | tf_op jit(solution)/shard_map/ppermute | solution.py:361
  61.4 1.2 %collective-permute-start.16 = (f32[4,8,128]{2,1,0:T(8,128)S(1)}, f32[4,8,128]{2,1,0:T(8,128)S(1)}, u32[]{:S(2)}, u32[]{:S(2)}) collective-permute-start(f32[4,8,128]{2,1,0:T(8,128)S(1)} %pad_maximum_fusion.10), channel_id=1, source_target_pairs={{0,4},{4,0},{8,12},{12,8},{16,20},{20,16},{24,28},{28,24},{1,5},{5... | collective-permute-start | bytes 49160 | tf_op jit(solution)/shard_map/ppermute | solution.py:361
  62.5 5.0 %collective-permute-start.18 = (f32[4,8,128]{2,1,0:T(8,128)S(1)}, f32[4,8,128]{2,1,0:T(8,128)S(1)}, u32[]{:S(2)}, u32[]{:S(2)}) collective-permute-start(f32[4,8,128]{2,1,0:T(8,128)S(1)} %pad_maximum_fusion.11), channel_id=1, source_target_pairs={{0,28},{4,8},{8,4},{12,16},{16,12},{20,24},{24,20},{28,0},{1,29},{... | collective-permute-start | bytes 49160 | tf_op jit(solution)/shard_map/ppermute | solution.py:366
  63.9 4.5 %collective-permute-start.17 = (f32[1,8,128]{2,1,0:T(8,128)S(1)}, f32[1,8,128]{2,1,0:T(8,128)S(1)}, u32[]{:S(2)}, u32[]{:S(2)}) collective-permute-start(f32[1,8,128]{2,1,0:T(8,128)S(1)} %slice_add_fusion), channel_id=1, source_target_pairs={{0,16},{4,20},{8,24},{12,28},{16,0},{20,4},{24,8},{28,12},{1,17},{... | collective-permute-start | bytes 12296 | tf_op jit(solution)/shard_map/ppermute | solution.py:361
  67.5 1.2 %collective-permute-start.19 = (f32[1,8,128]{2,1,0:T(8,128)S(1)}, f32[1,8,128]{2,1,0:T(8,128)S(1)}, u32[]{:S(2)}, u32[]{:S(2)}) collective-permute-start(f32[1,8,128]{2,1,0:T(8,128)S(1)} %slice.130), channel_id=1, source_target_pairs={{0,4},{4,0},{8,12},{12,8},{16,20},{20,16},{24,28},{28,24},{1,5},{5... | collective-permute-start | bytes 12296 | tf_op jit(solution)/shard_map/ppermute | solution.py:361

commit v3 on v2

--- a/solution.py
+++ b/solution.py
@@ -13,6 +13,7 @@
 CORNERS = 8
 SIDES = 6
 BACK_X, AHEAD_X, BACK_Y, AHEAD_Y = range(4)
+PARITY, PLACE, CORNER = 0, 2, 3
 
 
 def lane_iota():
@@ -47,17 +48,27 @@
 
 
 def prepare_kernel(
-    nz, corners_ref, order_ref, response_ref, matrix_ref, factor_ref,
-    high_ref, low_ref, faces_ref, ids_ref, rows_ref,
+    nz, order_hbm, response_hbm, matrix_hbm, factor_hbm,
+    order_ref, response_ref, matrix_ref, high_ref, low_ref, faces_ref, rows_ref,
+    factor_ref, done,
 ):
-    if rows_ref is not None:
-        rows_ref[...] = jnp.zeros_like(rows_ref)
-        for at in range(rows_ref.shape[0]):
-            rows_ref[at, :, 0 : factor_ref.shape[1]] = factor_ref[at * 8 : (at + 1) * 8, :]
+    pairs = (
+        (order_hbm, order_ref),
+        (response_hbm, response_ref),
+        (matrix_hbm, matrix_ref),
+        (factor_hbm, factor_ref),
+    )
+    copies = [pltpu.make_async_copy(*pair, done.at[at]) for at, pair in enumerate(pairs)]
+    for copy in copies:
+        copy.start()
+    for at in (0, 1, 3):
+        copies[at].wait()
+    rows_ref[...] = jnp.zeros_like(rows_ref)
+    for at in range(rows_ref.shape[0]):
+        rows_ref[at, :, 0 : factor_ref.shape[1]] = factor_ref[at * 8 : (at + 1) * 8, :]
     response = response_ref[...].astype(F32)
     lane = lane_iota()
     lane_square = lax.broadcasted_iota(jnp.int32, (LANES, LANES), 1)
-    ids = jnp.zeros((8, LANES), jnp.int32)
     for z in range(nz):
         total = jnp.zeros((16, SIDES * LANES), F32)
         for block in range(SIDES):
@@ -80,9 +91,7 @@
             low_ref[z * SIDES + side] = low
             high_ref[z * SIDES + side] = high
             faces_ref[z * SIDES + side] = pick_lanes(own, high, low)
-        for corner in range(CORNERS):
-            ids = jnp.where(lane == z * CORNERS + corner, corners_ref[z, 0, corner], ids)
-    ids_ref[...] = ids
+    copies[2].wait()
 
 
 def factor_kernel(count, place_ref, *refs):
@@ -93,7 +102,7 @@
     square[...] = jnp.where(row == column, 1.0, 0.0)
     for mask, block in zip((0, 1, 3, 2), blocks):
         tall = block.shape[0] * 8
-        start = lax.bitwise_xor(place_ref[2], mask) * tall
+        start = lax.bitwise_xor(place_ref[PLACE], mask) * tall
         for at in range(block.shape[0]):
             square[pl.ds(pl.multiple_of(start + at * 8, 8), 8), :] = block[at]
     square[...] = jnp.where(row < count, square[...], jnp.where(row == column, 1.0, 0.0))
@@ -118,8 +127,8 @@
     inverse_ref[...] = jnp.where((row < count) & (column < count), both, 0.0)
 
 
-def send_side(nz, parity_ref, axis, faces, outs):
-    even = parity_ref[axis] == 0
+def send_side(nz, scalar_ref, axis, faces, outs):
+    even = scalar_ref[PARITY + axis] == 0
     first, second = outs
     for z in range(nz):
         up, down = faces[z * SIDES + 3 + axis], faces[z * SIDES + axis]
@@ -128,7 +137,7 @@
 
 
 def local_part(nz, ncoarse, residual, image, refs):
-    (order_ref, matrix_ref, response_ref, corners_ref, high_ref, low_ref, faces_ref, sums_ref) = refs
+    (order_ref, matrix_ref, response_ref, scalar_ref, high_ref, low_ref, faces_ref, sums_ref) = refs
     own, back = residual
     lane = lane_iota()
     energy = jnp.zeros((8, LANES), F32)
@@ -168,34 +177,41 @@
         if image is not None:
             cross += own[at] * image[at]
     numbers = (lane_sum(norm), lane_sum(cross), lane_sum(energy))
-    for block in range(sums_ref.shape[0]):
+    blocks = -(-(ncoarse + 3) // LANES)
+    for block in range(blocks):
         where = lane + block * LANES
         tile = jnp.zeros((8, LANES), F32)
         for z in range(nz):
             for corner in range(CORNERS):
-                tile += jnp.where(where == corners_ref[z, 0, corner], terms[z][:, corner : corner + 1], 0.0)
+                tile += jnp.where(where == scalar_ref[CORNER + z * CORNERS + corner], terms[z][:, corner : corner + 1], 0.0)
         for at, number in enumerate(numbers):
             tile += jnp.where(where == ncoarse + at, number, 0.0)
-        sums_ref[block] = tile
+        for copy in range(0, sums_ref.shape[0], blocks):
+            sums_ref[copy + block] = tile
     return faces
 
 
 def start_kernel(
-    nz, ncoarse, parity_ref, corners_ref, rhs_ref, back_x_ref, back_y_ref, order_ref, matrix_ref,
-    response_ref, high_ref, low_ref, response_faces_ref, ids_ref,
-    residual_ref, faces_ref, sums_ref, x_first, x_second, y_first, y_second,
+    nz, ncoarse, scalar_ref, rhs_ref, back_x_ref, back_y_ref, order_ref, matrix_ref,
+    response_ref, high_ref, low_ref, response_faces_ref,
+    residual_ref, ids_ref, faces_ref, sums_ref, x_first, x_second, y_first, y_second,
 ):
     own = [rhs_ref[at] for at in range(nz * 3)]
     back = [back_x_ref[z * 3] for z in range(nz)] + [back_y_ref[z * 3 + 1] for z in range(nz)]
     for at, tile in enumerate(own + back):
         residual_ref[at] = tile
-    refs = (order_ref, matrix_ref, response_ref, corners_ref, high_ref, low_ref, faces_ref, sums_ref)
+    refs = (order_ref, matrix_ref, response_ref, scalar_ref, high_ref, low_ref, faces_ref, sums_ref)
     faces = local_part(nz, ncoarse, (own, back), None, refs)
-    numbers = ids_ref[...].astype(F32)
+    lane = lane_iota()
+    ids = jnp.zeros((8, LANES), jnp.int32)
+    for at in range(nz * CORNERS):
+        ids = jnp.where(lane == at, scalar_ref[CORNER + at], ids)
+    ids_ref[...] = ids
+    numbers = ids.astype(F32)
     responses = [response_faces_ref[at] for at in range(nz * SIDES)]
     for axis, outs in ((0, (x_first, x_second)), (1, (y_first, y_second))):
-        send_side(nz, parity_ref, axis, faces, outs)
-        send_side(nz, parity_ref, axis, responses, [out.at[nz : 2 * nz] for out in outs])
+        send_side(nz, scalar_ref, axis, faces, outs)
+        send_side(nz, scalar_ref, axis, responses, [out.at[nz : 2 * nz] for out in outs])
         for out in outs:
             out[2 * nz] = numbers
 
@@ -208,8 +224,8 @@
         del refs[:count]
         return taken
 
-    parity_ref, corners_ref, sums_ref, inverse_ref = take(4)
-    received = take(4)
+    scalar_ref, sums_ref, inverse_ref = take(3)
+    received = take(2 if last else 4)
     faces_ref, response_faces_ref, residual_ref = take(3)
     if first:
         (ids_ref,) = take(1)
@@ -218,16 +234,18 @@
     if not last:
         order_ref, matrix_ref, response_ref, high_ref, low_ref = take(5)
         (out_residual, out_image, out_direction, out_multipliers, out_scalars, out_faces, out_sums) = take(7)
-        sends = take(4)
+        sends = take(len(refs) - (2 if first else 0))
         if first:
             out_ids, out_near = take(2)
     else:
         out_multipliers, out_residual = take(2)
 
-    even_x, even_y = parity_ref[0] == 0, parity_ref[1] == 0
+    even_x, even_y = scalar_ref[PARITY] == 0, scalar_ref[PARITY + 1] == 0
     lane = lane_iota()
 
     def ahead_and_back(at):
+        if last:
+            return {AHEAD_X: received[0][at], AHEAD_Y: received[1][at]}
         x_first, x_second, y_first, y_second = [ref[at] for ref in received]
         return {
             AHEAD_X: jnp.where(even_x, x_first, x_second),
@@ -254,10 +272,13 @@
     else:
         ids = ids_ref[...]
         for z in range(nz):
-            for side in range(4):
+            for side in (AHEAD_X, AHEAD_Y) if last else range(4):
                 near_responses[side, z] = near_ref[side * nz + z]
 
-    sums = [sums_ref[block] for block in range(sums_ref.shape[0])]
+    blocks = inverse_ref.shape[0] // LANES
+    sums = [sums_ref[block] for block in range(blocks)]
+    for copy in range(blocks, sums_ref.shape[0], blocks):
+        sums = [total + sums_ref[copy + block] for block, total in enumerate(sums)]
     coarse = jnp.dot(
         jnp.concatenate(sums, axis=1),
         inverse_ref[...],
@@ -328,23 +349,35 @@
         out_image[at] = image[at]
     out_scalars[0] = jnp.broadcast_to(norm, (8, LANES))
     out_scalars[1] = jnp.broadcast_to(curvature, (8, LANES))
-    refs = (order_ref, matrix_ref, response_ref, corners_ref, high_ref, low_ref, out_faces, out_sums)
+    refs = (order_ref, matrix_ref, response_ref, scalar_ref, high_ref, low_ref, out_faces, out_sums)
     faces = local_part(nz, ncoarse, (residual[: nz * 3], residual[nz * 3 :]), image, refs)
-    send_side(nz, parity_ref, 0, faces, sends[:2])
-    send_side(nz, parity_ref, 1, faces, sends[2:])
+    if len(sends) == 2:
+        for axis, out in enumerate(sends):
+            for z in range(nz):
+                out[z] = faces[z * SIDES + axis]
+    else:
+        send_side(nz, scalar_ref, 0, faces, sends[:2])
+        send_side(nz, scalar_ref, 1, faces, sends[2:])
 
 
 def tiles(count, kind=F32):
     return jax.ShapeDtypeStruct((count, 8, LANES), kind)
 
 
-def call(kernel, outs, operands, scalars, flops, scratch=()):
+def like(value):
+    return jax.ShapeDtypeStruct(value.shape, value.dtype)
+
+
+def call(kernel, outs, operands, first_space, flops, scratch=()):
     vmem = pl.BlockSpec(memory_space=pltpu.VMEM)
-    smem = pl.BlockSpec(memory_space=pltpu.SMEM)
+    specs = [pl.BlockSpec(memory_space=first_space)] + [vmem] * (len(operands) - 1)
+    if first_space == pltpu.HBM:
+        specs = [pl.BlockSpec(memory_space=pltpu.HBM)] * len(operands)
+        operands = [pltpu.with_memory_space_constraint(x, pltpu.HBM) for x in operands]
     return pl.pallas_call(
         kernel,
         out_shape=outs,
-        in_specs=[smem] * scalars + [vmem] * (len(operands) - scalars),
+        in_specs=specs,
         out_specs=[vmem] * len(outs),
         scratch_shapes=scratch,
         compiler_params=pltpu.CompilerParams(vmem_limit_bytes=48 * 2**20),
@@ -366,21 +399,18 @@
     return lax.ppermute(value, axis, [(i, (i + 1 if i % 2 else i - 1) % count) for i in range(count)])
 
 
-def exchange(sums, sends, rows=None):
+def exchange_first(sums, sends, rows):
     lead = sums.shape[0]
     x_first, x_second, y_first, y_second = sends
     near = x_first.shape[0]
     blocks = []
     if lax.axis_size("slab") == 4:
-        extra = [] if rows is None else [rows]
-        got = paired(jnp.concatenate([sums, y_first] + extra), "slab", 1)
-        sums, got_y_first = sums + got[:lead], got[lead : lead + near]
-        extra += [] if rows is None else [got[lead + near :]]
-        got = paired(jnp.concatenate([sums, y_second] + extra), "slab", 3)
-        sums, got_y_second = sums + got[:lead], got[lead : lead + near]
-        if rows is not None:
-            count = rows.shape[0]
-            blocks = extra + [got[lead + near : lead + near + count], got[lead + near + count :]]
+        first = paired(jnp.concatenate([sums, y_first, rows]), "slab", 1)
+        second = paired(jnp.concatenate([sums, y_second, rows]), "slab", 3)
+        other = paired(jnp.concatenate([sums, rows]), "slab", 2)
+        sums = sums + first[:lead] + (second[:lead] + other[:lead])
+        blocks = [rows, first[lead + near :], second[lead + near :], other[lead:]]
+        got_y_first, got_y_second = first[lead : lead + near], second[lead : lead + near]
     else:
         got_y_first, got_y_second = paired(y_first, "slab", 1), paired_other(y_second, "slab")
         sums = doubled(sums, "slab", 1)
@@ -396,6 +426,22 @@
     return sums, [got_x_first, got_x_second, got_y_first, got_y_second], blocks
 
 
+def exchange(sums, sends, spread):
+    if spread:
+        sums = lax.all_to_all(sums, ("sub", "slab"), 0, 0, tiled=True)
+    else:
+        sums = doubled(doubled(sums, "slab", 1), "sub", 1)
+    if len(sends) == 2:
+        return sums, [shifted(sends[0], "sub", -1), shifted(sends[1], "slab", -1)]
+    x_first, x_second, y_first, y_second = sends
+    return sums, [
+        paired(x_first, "sub", 1),
+        paired_other(x_second, "sub"),
+        paired(y_first, "slab", 1),
+        paired_other(y_second, "slab"),
+    ]
+
+
 def doubled(sums, axis, mask):
     while mask < lax.axis_size(axis):
         sums = sums + paired(sums, axis, mask)
@@ -423,58 +469,70 @@
     order = order.reshape(nz, 1, local_size)
     matrices = inverse_rr.reshape(nz, local_size, local_size)
     responses = corner_response.reshape(nz, CORNERS, local_size)
-    corners = corners.reshape(nz, 1, CORNERS)
     place = lax.axis_index("slab")
-    parity = jnp.stack([lax.axis_index("sub") % 2, place % 2, place]).astype(jnp.int32)
+    scalars = jnp.stack([lax.axis_index("sub") % 2, place % 2, place]).astype(jnp.int32)
+    scalars = jnp.concatenate([scalars, corners.reshape(nz * CORNERS)])
 
     back_x = shifted(rhs, "sub", 1)
     back_y = shifted(rhs, "slab", 1)
+    devices = lax.axis_size("sub") * lax.axis_size("slab")
     riding = blocks == 1 and lax.axis_size("slab") == 4 and coarse_factor.shape[0] % 8 == 0
+    spread = blocks * devices <= 64
+    copies = devices if spread else 1
     tables = nz * SIDES
     rows = coarse_factor.shape[0] // 8 if riding else 1
-    high, low, response_faces, ids, rows = call(
+    part = coarse_factor[: rows * 8, :LANES]
+    order, responses, matrices, high, low, response_faces, rows = call(
         functools.partial(prepare_kernel, nz),
-        [tiles(tables, jnp.int32), tiles(tables, jnp.int32), tiles(tables),
-         jax.ShapeDtypeStruct((8, LANES), jnp.int32), tiles(rows)],
-        [corners, order, responses, matrices, coarse_factor[: rows * 8, :LANES]],
-        1,
+        [like(order), like(responses), like(matrices), tiles(tables, jnp.int32),
+         tiles(tables, jnp.int32), tiles(tables), tiles(rows)],
+        [order, responses, matrices, part],
+        pltpu.HBM,
         2**30,
+        [pltpu.VMEM(part.shape, F32), pltpu.SemaphoreType.DMA((4,))],
     )
     own = [order, matrices, responses, high, low]
-    residual, faces, sums, *sends = call(
+    residual, ids, faces, sums, *sends = call(
         functools.partial(start_kernel, nz, ncoarse),
-        [tiles(nz * 5), tiles(tables), tiles(blocks)] + [tiles(2 * nz + 1)] * 4,
-        [parity, corners, rhs, back_x, back_y] + own + [response_faces, ids],
-        2,
+        [tiles(nz * 5), jax.ShapeDtypeStruct((8, LANES), jnp.int32), tiles(tables), tiles(blocks)]
+        + [tiles(2 * nz + 1)] * 4,
+        [scalars, rhs, back_x, back_y] + own + [response_faces],
+        pltpu.SMEM,
         2**30,
     )
     state = [residual, ids]
     for iteration in range(ITERS):
         first, last = iteration == 0, iteration == ITERS - 1
-        sums, received, factor = exchange(sums, sends, rows if first and riding else None)
+        if first:
+            sums, received, factor = exchange_first(sums, sends, rows)
+        else:
+            sums, received = exchange(sums, sends, spread)
         if first and riding:
             square = jax.ShapeDtypeStruct((LANES, LANES), F32)
             inverse = call(
-                functools.partial(factor_kernel, ncoarse), [square], [parity] + factor, 1, 3 * 2**30,
-                [pltpu.VMEM(square.shape, F32)],
+                functools.partial(factor_kernel, ncoarse), [square], [scalars] + factor,
+                pltpu.SMEM, 3 * 2**30, [pltpu.VMEM(square.shape, F32)],
             )[0]
         elif first:
             inverse = coarse_inverse(coarse_factor, blocks * LANES)
-        operands = [parity, corners, sums, inverse] + received + [faces, response_faces] + state
+        operands = [scalars, sums, inverse] + received + [faces, response_faces] + state
         kernel = functools.partial(step_kernel, first, last, nz, ncoarse)
         if last:
-            multipliers, residual = call(kernel, [tiles(nz * 3)] * 2, operands, 2, 2**30)
+            outs = [tiles(nz * 3)] * 2
+            multipliers, residual = call(kernel, outs, operands, pltpu.SMEM, 2**30)
             break
         outs = [tiles(nz * 5), tiles(nz * 5), tiles(nz * 3), tiles(nz * 3), tiles(2)]
-        outs += [tiles(tables), tiles(blocks)] + [tiles(nz)] * 4
+        outs += [tiles(tables), tiles(blocks * copies)]
+        sides = 2 if iteration == ITERS - 2 else 4
+        outs += [tiles(nz)] * sides
         if first:
             outs += [jax.ShapeDtypeStruct((8, LANES), jnp.int32), tiles(nz * 4)]
-        results = call(kernel, outs, operands + own, 2, 2**31)
-        residual, image, direction, multipliers, scalars, faces, sums = results[:7]
-        sends = results[7:11]
+        results = call(kernel, outs, operands + own, pltpu.SMEM, 2**31)
+        residual, image, direction, multipliers, step, faces, sums = results[:7]
+        sends = results[7 : 7 + sides]
         if first:
-            ids, near = results[11:]
-        state = [residual, ids, near, image, direction, multipliers, scalars]
+            ids, near = results[7 + sides :]
+        state = [residual, ids, near, image, direction, multipliers, step]
 
     def placed(value):
         value = value.reshape(interface_rhs.shape[:3] + (dirs, samples, face))

time: 70.7 us -> 61.2 us (0.87)
  waiting for transfers between devices: 32.3 us -> 15.2 us
  starting transfers between devices: 19.6 us -> 27 us
  local copies, waits for them, and re-layouts: 4.93 us -> 2.12 us
  Pallas kernels: 12.4 us -> 15 us
    ppermute x15 -> x8, waiting for transfers between devices: 25.2 us -> 5.17 us  [paired(): lax.ppermute(value, axis, [(i, i ^ mask) for i in range(lax.axis_size(axi...]
    all_to_all x0 -> x2, starting transfers between devices: none -> 5.97 us  [exchange(): sums = lax.all_to_all(sums, ('sub', 'slab'), 0, 0, tiled=True)]
    ppermute x2 -> x4, starting transfers between devices: 2.99 us -> 8.83 us  [shifted(): lax.ppermute(value, axis, [(i, (i + steps) % count) for i in range(count)])]
    ppermute x15 -> x8, starting transfers between devices: 8.67 us -> 5.49 us  [paired(): lax.ppermute(value, axis, [(i, i ^ mask) for i in range(lax.axis_size(axi...]
    ppermute x2 -> x4, waiting for transfers between devices: 0.01 us -> 3.09 us  [shifted(): lax.ppermute(value, axis, [(i, (i + steps) % count) for i in range(count)])]
    unnamed x20 -> x6, local copies, waits for them, and re-layouts: 4.88 us -> 2.01 us
    pallas_call x6, Pallas kernels: 12.4 us -> 15 us  [call(): pl.pallas_call(kernel, out_shape=outs, in_specs=specs, out_specs=[vmem] *...]
    ppermute x3, waiting for transfers between devices: 7.14 us -> 5.73 us  [paired_other(): lax.ppermute(value, axis, [(i, (i + 1 if i % 2 else i - 1) % count) for i...]
  transfers between devices with their start and end apart: 20 -> 17, of which waited for: 15 -> 8; matrix products, arithmetic and copies ran while one was open for 0% -> 1% of each run, Pallas kernels for 8% -> 11%
where the time goes in v3:
time: 61.2 us; the launch traced here: 60.8 us
  starting transfers between devices  27 us (44%)
  waiting for transfers between devices  15.2 us (25%)
  Pallas kernels  15 us (25%)
  local copies, waits for them, and re-layouts  2.12 us (3%)
  other arithmetic  0.82 us (1%)
  between operations  0.81 us (1%)
    pallas_call x6, Pallas kernels, call(): pl.pallas_call(kernel, out_shape=outs, in_specs=specs, out_specs=[vmem] *...  15 us
    ppermute x4, starting transfers between devices, shifted(): lax.ppermute(value, axis, [(i, (i + steps) % count) for i in range(count)])  8.83 us
    ppermute x3, starting transfers between devices, paired_other(): lax.ppermute(value, axis, [(i, (i + 1 if i % 2 else i - 1) % count) for i...  6.67 us
    all_to_all x2, starting transfers between devices, exchange(): sums = lax.all_to_all(sums, ('sub', 'slab'), 0, 0, tiled=True)  5.97 us
    ppermute x3, waiting for transfers between devices, paired_other(): lax.ppermute(value, axis, [(i, (i + 1 if i % 2 else i - 1) % count) for i...  5.73 us
    ppermute x8, starting transfers between devices, paired(): lax.ppermute(value, axis, [(i, i ^ mask) for i in range(lax.axis_size(axi...  5.49 us
    ppermute x8, waiting for transfers between devices, paired(): lax.ppermute(value, axis, [(i, i ^ mask) for i in range(lax.axis_size(axi...  5.17 us
    ppermute x4, waiting for transfers between devices, shifted(): lax.ppermute(value, axis, [(i, (i + steps) % count) for i in range(count)])  3.09 us
  transfers between devices with their start and end apart: 17, of which 8 were waited for; matrix products, arithmetic and copies ran while one was open for 1% of the time, Pallas kernels for 11%

profile of v3, /device:TPU:0, one launch (start us, length us, event | category | flops | bytes accessed | tf_op | source)
XLA Modules:
  0.0 60.8 jit_solution(10326150274404363845)
XLA Ops:
  0.6 0.0 copy-start
  0.6 3.0 %collective-permute-start.1 = (f32[9,8,128]{2,1,0:T(8,128)}, f32[9,8,128]{2,1,0:T(8,128)S(1)}, u32[]{:S(2)}, u32[]{:S(2)}) collective-permute-start(f32[9,8,128]{2,1,0:T(8,128)} %bitcast.15), channel_id=1, source_target_pairs={{0,1},{1,2},{2,3},{3,0},{4,5},{5,6},{6,7},{7,4},{8,9},{9,10},{10,1... | collective-permute-start | bytes 110600 | tf_op jit(solution)/shard_map/ppermute | solution.py:390
  3.6 0.0 collective-permute-start
  3.6 0.7 %reduce = s32[3,8]{1,0:T(4,128)S(1)} reduce(s32[1,1,3,8]{3,1,2,0:T(1,128)} %param.10, s32[]{:T(128)} %constant.22.clone.1), dimensions={0,1}, to_apply=%param.10.reduce_sub_computation | reduce | bytes 196 | tf_op args[4]
  4.3 0.1 reshape.25
  4.4 0.1 pad_add_fusion.scalar_ref.place_ref.refs_0_
  4.5 2.8 %shard_map.77 = (s32[3,1,768]{2,1,0:T(1,128)S(1)}, bf16[3,8,768]{2,1,0:T(8,128)(2,1)S(1)}, bf16[3,768,768]{2,1,0:T(8,128)(2,1)S(1)}, s32[18,8,128]{2,1,0:T(8,128...) custom-call(s32[3,1,768]{2,1,0:T(1,128)} %bitcast.20, ...), custom_call_target="tpu_custom_call" | custom-call | flops 1073741824 | bytes 1048576 | tf_op jit(solution)/shard_map/pallas_call | solution.py:377
  7.3 0.0 copy-start.1
  7.3 0.0 collective-permute-done.1.back_y_ref
  7.3 1.7 %collective-permute-done.back_x_ref = f32[9,8,128]{2,1,0:T(8,128)S(1)} collective-permute-done((f32[9,8,128]{2,1,0:T(8,128)}, f32[9,8,128]{2,1,0:T(8,128)S(1)}, u32[]{:S(2)}, u32[]{:S(2)}) %collective-permute-start) | collective-permute-done | bytes 36896 | tf_op jit(solution)/shard_map/ppermute | solution.py:390
  9.0 0.0 copy-done
  9.0 1.4 %shard_map.78 = (f32[15,8,128]{2,1,0:T(8,128)S(1)}, s32[8,128]{1,0:T(8,128)S(1)}, f32[18,8,128]{2,1,0:T(8,128)S(1)}, f32[1,8,128]{2,1,0:T(8,128)S(1)}, f32[7,8,1...) custom-call(s32[27]{0:T(128)S(1)} %pad_add_fusion.scalar_ref.place_ref.refs_0_,, ...), custom_call_target="tpu_custom_call" | custom-call | flops 1073741824 | bytes 1048576 | tf_op jit(solution)/shard_map/pallas_call | solution.py:377
  10.4 1.6 %collective-permute-start.2 = (f32[11,8,128]{2,1,0:T(8,128)S(1)}, f32[11,8,128]{2,1,0:T(8,128)S(1)}, u32[]{:S(2)}, u32[]{:S(2)}) collective-permute-start(f32[11,8,128]{2,1,0:T(8,128)S(1)} %get-tuple-element.80), channel_id=1, source_target_pairs={{0,1},{1,0},{2,3},{3,2},{4,5},{5,4},{6,7},{7,6},{8,9},{9,8},{10,11... | collective-permute-start | bytes 135176 | tf_op jit(solution)/shard_map/ppermute | solution.py:394
  12.0 1.5 %collective-permute-start.3 = (f32[11,8,128]{2,1,0:T(8,128)S(1)}, f32[11,8,128]{2,1,0:T(8,128)S(1)}, u32[]{:S(2)}, u32[]{:S(2)}) collective-permute-start(f32[11,8,128]{2,1,0:T(8,128)S(1)} %get-tuple-element.81), channel_id=1, source_target_pairs={{0,3},{1,2},{2,1},{3,0},{4,7},{5,6},{6,5},{7,4},{8,11},{9,10},{10,... | collective-permute-start | bytes 135176 | tf_op jit(solution)/shard_map/ppermute | solution.py:394
  13.5 0.5 collective-permute-start.4
  14.0 3.2 %collective-permute-done.4 = f32[4,8,128]{2,1,0:T(8,128)S(1)} collective-permute-done((f32[4,8,128]{2,1,0:T(8,128)S(1)}, f32[4,8,128]{2,1,0:T(8,128)S(1)}, u32[]{:S(2)}, u32[]{:S(2)}) %collective-permute-start.4) | collective-permute-done | bytes 16416 | tf_op jit(solution)/shard_map/ppermute | solution.py:394
  17.2 0.0 collective-permute-done.2
  17.2 0.0 collective-permute-done.3
  17.2 0.1 collective-permute-start.5
  17.3 1.2 %collective-permute-done.5 = f32[8,8,128]{2,1,0:T(8,128)S(1)} collective-permute-done((f32[8,8,128]{2,1,0:T(8,128)S(1)}, f32[8,8,128]{2,1,0:T(8,128)S(1)}, u32[]{:S(2)}, u32[]{:S(2)}) %collective-permute-start.5) | collective-permute-done | bytes 32800 | tf_op jit(solution)/shard_map/ppermute | solution.py:394
  18.5 1.7 %collective-permute-start.7 = (f32[8,8,128]{2,1,0:T(8,128)S(1)}, f32[8,8,128]{2,1,0:T(8,128)S(1)}, u32[]{:S(2)}, u32[]{:S(2)}) collective-permute-start(f32[8,8,128]{2,1,0:T(8,128)S(1)} %pad_maximum_fusion.5), channel_id=1, source_target_pairs={{0,28},{4,8},{8,4},{12,16},{16,12},{20,24},{24,20},{28,0},{1,29},{... | collective-permute-start | bytes 98312 | tf_op jit(solution)/shard_map/ppermute | solution.py:399
  20.2 0.1 collective-permute-start.6
  20.3 3.3 %collective-permute-done.7 = f32[8,8,128]{2,1,0:T(8,128)S(1)} collective-permute-done((f32[8,8,128]{2,1,0:T(8,128)S(1)}, f32[8,8,128]{2,1,0:T(8,128)S(1)}, u32[]{:S(2)}, u32[]{:S(2)}) %collective-permute-start.7) | collective-permute-done | bytes 32800 | tf_op jit(solution)/shard_map/ppermute | solution.py:399
  23.6 0.0 collective-permute-start.8
  23.7 3.9 %shard_map.79.refs_2_ = f32[128,128]{1,0:T(8,128)S(1)} custom-call(s32[27]{0:T(128)S(1)} %pad_add_fusion.scalar_ref.place_ref.refs_0_, f32[3,8,128]{2,1,0:T(8,128)S(1)} %get-tuple-element.49.refs_0_, f32[3,8,128]{2,1,0:T(8,128)S(1)} %slice.53.refs_1_, f32[3,8,128]{2,1,0:T(8,128)S(1)} %slice.54.refs_2_, f32[3,8,128]{2,1,0:T(8,128)S(1)} %slice.55.refs_3_), custom_call_target="tpu_custom_call" | custom-call | flops 3221225472 | bytes 1048576 | tf_op jit(solution)/shard_map/pallas_call | solution.py:377
  27.6 0.0 collective-permute-done.6
  27.6 0.0 collective-permute-done.8
  27.6 0.0 copy-done.1
  27.6 2.6 %shard_map.80 = (f32[15,8,128]{2,1,0:T(8,128)S(1)}, f32[15,8,128]{2,1,0:T(8,128)S(1)}, f32[9,8,128]{2,1,0:T(8,128)S(1)}, f32[9,8,128]{2,1,0:T(8,128)S(1)}, f32[2...) custom-call(s32[27]{0:T(128)S(1)} %pad_add_fusion.scalar_ref.place_r, ...), custom_call_target="tpu_custom_call" | custom-call | flops 2147483648 | bytes 1048576 | tf_op jit(solution)/shard_map/pallas_call | solution.py:377
  30.3 3.4 %all-to-all-start = ((f32[32,8,128]{2,1,0:T(8,128)}), f32[32,8,128]{2,1,0:T(8,128)S(1)}, u32[]{:S(2)}, u32[]{:S(2)}) async-start(f32[32,8,128]{2,1,0:T(8,128)} %get-tuple-element.56), calls=%async_computation | async-start | bytes 262144 | tf_op jit(solution)/shard_map/all_to_all | solution.py:431
  33.7 0.3 collective-permute-start.9
  34.0 3.5 %collective-permute-start.10 = (f32[3,8,128]{2,1,0:T(8,128)S(1)}, f32[3,8,128]{2,1,0:T(8,128)S(1)}, u32[]{:S(2)}, u32[]{:S(2)}) collective-permute-start(f32[3,8,128]{2,1,0:T(8,128)S(1)} %get-tuple-element.58), channel_id=1, source_target_pairs={{0,28},{4,8},{8,4},{12,16},{16,12},{20,24},{24,20},{28,0},{1,29},{... | collective-permute-start | bytes 36872 | tf_op jit(solution)/shard_map/ppermute | solution.py:399
  37.5 1.5 %collective-permute-start.11 = (f32[3,8,128]{2,1,0:T(8,128)S(1)}, f32[3,8,128]{2,1,0:T(8,128)S(1)}, u32[]{:S(2)}, u32[]{:S(2)}) collective-permute-start(f32[3,8,128]{2,1,0:T(8,128)S(1)} %get-tuple-element.59), channel_id=1, source_target_pairs={{0,1},{1,0},{2,3},{3,2},{4,5},{5,4},{6,7},{7,6},{8,9},{9,8},{10,11... | collective-permute-start | bytes 36872 | tf_op jit(solution)/shard_map/ppermute | solution.py:394
  39.0 1.5 %collective-permute-start.12 = (f32[3,8,128]{2,1,0:T(8,128)S(1)}, f32[3,8,128]{2,1,0:T(8,128)S(1)}, u32[]{:S(2)}, u32[]{:S(2)}) collective-permute-start(f32[3,8,128]{2,1,0:T(8,128)S(1)} %get-tuple-element.60), channel_id=1, source_target_pairs={{0,3},{1,2},{2,1},{3,0},{4,7},{5,6},{6,5},{7,4},{8,11},{9,10},{10,... | collective-permute-start | bytes 36872 | tf_op jit(solution)/shard_map/ppermute | solution.py:399
  40.5 0.0 collective-permute-done.9.refs_3_
  40.5 0.0 collective-permute-done.10.refs_4_
  40.5 0.7 %collective-permute-done.11.refs_5_ = f32[3,8,128]{2,1,0:T(8,128)S(1)} collective-permute-done((f32[3,8,128]{2,1,0:T(8,128)S(1)}, f32[3,8,128]{2,1,0:T(8,128)S(1)}, u32[]{:S(2)}, u32[]{:S(2)}) %collective-permute-start.11) | collective-permute-done | bytes 12320 | tf_op jit(solution)/shard_map/ppermute | solution.py:394
  41.2 2.4 %collective-permute-done.12.refs_6_ = f32[3,8,128]{2,1,0:T(8,128)S(1)} collective-permute-done((f32[3,8,128]{2,1,0:T(8,128)S(1)}, f32[3,8,128]{2,1,0:T(8,128)S(1)}, u32[]{:S(2)}, u32[]{:S(2)}) %collective-permute-start.12) | collective-permute-done | bytes 12320 | tf_op jit(solution)/shard_map/ppermute | solution.py:399
  43.6 0.0 all-to-all-done.refs_1_
  43.6 2.0 %copy-done.2 = bf16[3,768,768]{2,1,0:T(8,128)(2,1)S(1)} copy-done((bf16[3,768,768]{2,1,0:T(8,128)(2,1)S(1)}, bf16[3,768,768]{2,1,0:T(8,128)(2,1)}, u32[]{:S(2)}) %copy-start.2) | copy-done | bytes 3538968
  45.6 2.6 %shard_map.81 = (f32[15,8,128]{2,1,0:T(8,128)S(1)}, f32[15,8,128]{2,1,0:T(8,128)S(1)}, f32[9,8,128]{2,1,0:T(8,128)S(1)}, f32[9,8,128]{2,1,0:T(8,128)S(1)}, f32[2...) custom-call(s32[27]{0:T(128)S(1)} %pad_add_fusion.scalar_ref.place_r, ...), custom_call_target="tpu_custom_call" | custom-call | flops 2147483648 | bytes 1048576 | tf_op jit(solution)/shard_map/pallas_call | solution.py:377
  48.2 2.6 %all-to-all-start.1 = ((f32[32,8,128]{2,1,0:T(8,128)}), f32[32,8,128]{2,1,0:T(8,128)S(1)}, u32[]{:S(2)}, u32[]{:S(2)}) async-start(f32[32,8,128]{2,1,0:T(8,128)} %get-tuple-element.69), calls=%async_computation.1 | async-start | bytes 262144 | tf_op jit(solution)/shard_map/all_to_all | solution.py:431
  50.8 3.4 %collective-permute-start.13 = (f32[3,8,128]{2,1,0:T(8,128)S(1)}, f32[3,8,128]{2,1,0:T(8,128)S(1)}, u32[]{:S(2)}, u32[]{:S(2)}) collective-permute-start(f32[3,8,128]{2,1,0:T(8,128)S(1)} %get-tuple-element.70), channel_id=1, source_target_pairs={{0,28},{4,0},{8,4},{12,8},{16,12},{20,16},{24,20},{28,24},{1,29},{... | collective-permute-start | bytes 36872 | tf_op jit(solution)/shard_map/ppermute | solution.py:390
  54.2 2.4 %collective-permute-start.14 = (f32[3,8,128]{2,1,0:T(8,128)S(1)}, f32[3,8,128]{2,1,0:T(8,128)S(1)}, u32[]{:S(2)}, u32[]{:S(2)}) collective-permute-start(f32[3,8,128]{2,1,0:T(8,128)S(1)} %get-tuple-element.71), channel_id=1, source_target_pairs={{0,3},{1,0},{2,1},{3,2},{4,7},{5,4},{6,5},{7,6},{8,11},{9,8},{10,9... | collective-permute-start | bytes 36872 | tf_op jit(solution)/shard_map/ppermute | solution.py:390
  56.6 0.0 collective-permute-done.13.refs_3_
  56.6 1.4 %collective-permute-done.14.refs_4_ = f32[3,8,128]{2,1,0:T(8,128)S(1)} collective-permute-done((f32[3,8,128]{2,1,0:T(8,128)S(1)}, f32[3,8,128]{2,1,0:T(8,128)S(1)}, u32[]{:S(2)}, u32[]{:S(2)}) %collective-permute-start.14) | collective-permute-done | bytes 12320 | tf_op jit(solution)/shard_map/ppermute | solution.py:390
  58.0 1.2 %all-to-all-done.1.refs_1_ = f32[32,8,128]{2,1,0:T(8,128)S(1)} async-done(((f32[32,8,128]{2,1,0:T(8,128)}), f32[32,8,128]{2,1,0:T(8,128)S(1)}, u32[]{:S(2)}, u32[]{:S(2)}) %all-to-all-start.1) | async-done | bytes 131104 | tf_op jit(solution)/shard_map/all_to_all | solution.py:431
  59.2 1.7 %shard_map.82 = (f32[9,8,128]{2,1,0:T(8,128)}, f32[9,8,128]{2,1,0:T(8,128)}) custom-call(s32[27]{0:T(128)S(1)} %pad_add_fusion.scalar_ref.place_ref.refs_0_, f32[32,8,128]{2,1,0:T(8,128)S(1)} %all-to-all-done.1.refs_1_, f32[128,128]{1,0:T(8,128)S(1)} %shard_map.79.refs_2_, f32[3,8,128]{2,1,0:T(8,128)S(1)} %collective-permute-done.13.refs_3_, ...), custom_call_target="tpu_custom_call" | custom-call | flops 1073741824 | bytes 1048576 | tf_op jit(solution)/shard_map/pallas_call | solution.py:377
  (16 shorter events, 0.1 us)
Async XLA Ops:
  0.6 8.4 %copy-start = (f32[1,1,3,8,3,128]{5,3,4,2,1,0:T(8,128)S(1)}, f32[1,1,3,8,3,128]{5,3,4,2,1,0:T(8,128)}, u32[]{:S(2)}) copy-start(f32[1,1,3,8,3,128]{5,3,4,2,1,0:T(8,128)} %param.6) | copy-start | bytes 110596
  0.6 6.7 %collective-permute-start.1 = (f32[9,8,128]{2,1,0:T(8,128)}, f32[9,8,128]{2,1,0:T(8,128)S(1)}, u32[]{:S(2)}, u32[]{:S(2)}) collective-permute-start(f32[9,8,128]{2,1,0:T(8,128)} %bitcast.15), channel_id=1, source_target_pairs={{0,1},{1,2},{2,3},{3,0},{4,5},{5,6},{6,7},{7,4},{8,9},{9,10},{10,1... | collective-permute-start | bytes 110600 | tf_op jit(solution)/shard_map/ppermute | solution.py:390
  3.6 5.4 %collective-permute-start = (f32[9,8,128]{2,1,0:T(8,128)}, f32[9,8,128]{2,1,0:T(8,128)S(1)}, u32[]{:S(2)}, u32[]{:S(2)}) collective-permute-start(f32[9,8,128]{2,1,0:T(8,128)} %bitcast.16), channel_id=1, source_target_pairs={{0,4},{4,8},{8,12},{12,16},{16,20},{20,24},{24,28},{28,0},{1,5},{5... | collective-permute-start | bytes 110600 | tf_op jit(solution)/shard_map/ppermute | solution.py:390
  7.3 20.3 %copy-start.1 = (bf16[3,768,768]{2,1,0:T(8,128)(2,1)}, bf16[3,768,768]{2,1,0:T(8,128)(2,1)S(1)}, u32[]{:S(2)}) copy-start(bf16[3,768,768]{2,1,0:T(8,128)(2,1)S(1)} %get-tuple-element.42.matrix_ref.refs_12_.refs_17_) | copy-start | bytes 10616836
  10.4 6.8 %collective-permute-start.2 = (f32[11,8,128]{2,1,0:T(8,128)S(1)}, f32[11,8,128]{2,1,0:T(8,128)S(1)}, u32[]{:S(2)}, u32[]{:S(2)}) collective-permute-start(f32[11,8,128]{2,1,0:T(8,128)S(1)} %get-tuple-element.80), channel_id=1, source_target_pairs={{0,1},{1,0},{2,3},{3,2},{4,5},{5,4},{6,7},{7,6},{8,9},{9,8},{10,11... | collective-permute-start | bytes 135176 | tf_op jit(solution)/shard_map/ppermute | solution.py:394
  12.0 5.2 %collective-permute-start.3 = (f32[11,8,128]{2,1,0:T(8,128)S(1)}, f32[11,8,128]{2,1,0:T(8,128)S(1)}, u32[]{:S(2)}, u32[]{:S(2)}) collective-permute-start(f32[11,8,128]{2,1,0:T(8,128)S(1)} %get-tuple-element.81), channel_id=1, source_target_pairs={{0,3},{1,2},{2,1},{3,0},{4,7},{5,6},{6,5},{7,4},{8,11},{9,10},{10,... | collective-permute-start | bytes 135176 | tf_op jit(solution)/shard_map/ppermute | solution.py:394
  13.5 3.7 %collective-permute-start.4 = (f32[4,8,128]{2,1,0:T(8,128)S(1)}, f32[4,8,128]{2,1,0:T(8,128)S(1)}, u32[]{:S(2)}, u32[]{:S(2)}) collective-permute-start(f32[4,8,128]{2,1,0:T(8,128)S(1)} %pad_maximum_fusion.6), channel_id=1, source_target_pairs={{0,2},{1,3},{2,0},{3,1},{4,6},{5,7},{6,4},{7,5},{8,10},{9,11},{10,... | collective-permute-start | bytes 49160 | tf_op jit(solution)/shard_map/ppermute | solution.py:394
  17.2 1.3 %collective-permute-start.5 = (f32[8,8,128]{2,1,0:T(8,128)S(1)}, f32[8,8,128]{2,1,0:T(8,128)S(1)}, u32[]{:S(2)}, u32[]{:S(2)}) collective-permute-start(f32[8,8,128]{2,1,0:T(8,128)S(1)} %pad_maximum_fusion.4), channel_id=1, source_target_pairs={{0,4},{4,0},{8,12},{12,8},{16,20},{20,16},{24,28},{28,24},{1,5},{5... | collective-permute-start | bytes 98312 | tf_op jit(solution)/shard_map/ppermute | solution.py:394
  18.5 5.1 %collective-permute-start.7 = (f32[8,8,128]{2,1,0:T(8,128)S(1)}, f32[8,8,128]{2,1,0:T(8,128)S(1)}, u32[]{:S(2)}, u32[]{:S(2)}) collective-permute-start(f32[8,8,128]{2,1,0:T(8,128)S(1)} %pad_maximum_fusion.5), channel_id=1, source_target_pairs={{0,28},{4,8},{8,4},{12,16},{16,12},{20,24},{24,20},{28,0},{1,29},{... | collective-permute-start | bytes 98312 | tf_op jit(solution)/shard_map/ppermute | solution.py:399
  20.2 7.4 %collective-permute-start.6 = (f32[1,8,128]{2,1,0:T(8,128)S(1)}, f32[1,8,128]{2,1,0:T(8,128)S(1)}, u32[]{:S(2)}, u32[]{:S(2)}) collective-permute-start(f32[1,8,128]{2,1,0:T(8,128)S(1)} %slice_add_fusion), channel_id=1, source_target_pairs={{0,16},{4,20},{8,24},{12,28},{16,0},{20,4},{24,8},{28,12},{1,17},{... | collective-permute-start | bytes 12296 | tf_op jit(solution)/shard_map/ppermute | solution.py:394
  23.6 4.0 %collective-permute-start.8 = (f32[1,8,128]{2,1,0:T(8,128)S(1)}, f32[1,8,128]{2,1,0:T(8,128)S(1)}, u32[]{:S(2)}, u32[]{:S(2)}) collective-permute-start(f32[1,8,128]{2,1,0:T(8,128)S(1)} %slice.52), channel_id=1, source_target_pairs={{0,4},{4,0},{8,12},{12,8},{16,20},{20,16},{24,28},{28,24},{1,5},{5... | collective-permute-start | bytes 12296 | tf_op jit(solution)/shard_map/ppermute | solution.py:394
  30.3 13.3 %all-to-all-start = ((f32[32,8,128]{2,1,0:T(8,128)}), f32[32,8,128]{2,1,0:T(8,128)S(1)}, u32[]{:S(2)}, u32[]{:S(2)}) async-start(f32[32,8,128]{2,1,0:T(8,128)} %get-tuple-element.56), calls=%async_computation | async-start | bytes 262144 | tf_op jit(solution)/shard_map/all_to_all | solution.py:431
  33.7 6.8 %collective-permute-start.9 = (f32[3,8,128]{2,1,0:T(8,128)S(1)}, f32[3,8,128]{2,1,0:T(8,128)S(1)}, u32[]{:S(2)}, u32[]{:S(2)}) collective-permute-start(f32[3,8,128]{2,1,0:T(8,128)S(1)} %get-tuple-element.57), channel_id=1, source_target_pairs={{0,4},{4,0},{8,12},{12,8},{16,20},{20,16},{24,28},{28,24},{1,5},{5... | collective-permute-start | bytes 36872 | tf_op jit(solution)/shard_map/ppermute | solution.py:394
  34.0 6.4 %collective-permute-start.10 = (f32[3,8,128]{2,1,0:T(8,128)S(1)}, f32[3,8,128]{2,1,0:T(8,128)S(1)}, u32[]{:S(2)}, u32[]{:S(2)}) collective-permute-start(f32[3,8,128]{2,1,0:T(8,128)S(1)} %get-tuple-element.58), channel_id=1, source_target_pairs={{0,28},{4,8},{8,4},{12,16},{16,12},{20,24},{24,20},{28,0},{1,29},{... | collective-permute-start | bytes 36872 | tf_op jit(solution)/shard_map/ppermute | solution.py:399
  37.5 3.7 %collective-permute-start.11 = (f32[3,8,128]{2,1,0:T(8,128)S(1)}, f32[3,8,128]{2,1,0:T(8,128)S(1)}, u32[]{:S(2)}, u32[]{:S(2)}) collective-permute-start(f32[3,8,128]{2,1,0:T(8,128)S(1)} %get-tuple-element.59), channel_id=1, source_target_pairs={{0,1},{1,0},{2,3},{3,2},{4,5},{5,4},{6,7},{7,6},{8,9},{9,8},{10,11... | collective-permute-start | bytes 36872 | tf_op jit(solution)/shard_map/ppermute | solution.py:394
  39.0 4.6 %collective-permute-start.12 = (f32[3,8,128]{2,1,0:T(8,128)S(1)}, f32[3,8,128]{2,1,0:T(8,128)S(1)}, u32[]{:S(2)}, u32[]{:S(2)}) collective-permute-start(f32[3,8,128]{2,1,0:T(8,128)S(1)} %get-tuple-element.60), channel_id=1, source_target_pairs={{0,3},{1,2},{2,1},{3,0},{4,7},{5,6},{6,5},{7,4},{8,11},{9,10},{10,... | collective-permute-start | bytes 36872 | tf_op jit(solution)/shard_map/ppermute | solution.py:399
  43.6 2.0 %copy-start.2 = (bf16[3,768,768]{2,1,0:T(8,128)(2,1)S(1)}, bf16[3,768,768]{2,1,0:T(8,128)(2,1)}, u32[]{:S(2)}) copy-start(bf16[3,768,768]{2,1,0:T(8,128)(2,1)} %copy-done.1) | copy-start | bytes 10616836
  48.2 11.0 %all-to-all-start.1 = ((f32[32,8,128]{2,1,0:T(8,128)}), f32[32,8,128]{2,1,0:T(8,128)S(1)}, u32[]{:S(2)}, u32[]{:S(2)}) async-start(f32[32,8,128]{2,1,0:T(8,128)} %get-tuple-element.69), calls=%async_computation.1 | async-start | bytes 262144 | tf_op jit(solution)/shard_map/all_to_all | solution.py:431
  50.8 5.8 %collective-permute-start.13 = (f32[3,8,128]{2,1,0:T(8,128)S(1)}, f32[3,8,128]{2,1,0:T(8,128)S(1)}, u32[]{:S(2)}, u32[]{:S(2)}) collective-permute-start(f32[3,8,128]{2,1,0:T(8,128)S(1)} %get-tuple-element.70), channel_id=1, source_target_pairs={{0,28},{4,0},{8,4},{12,8},{16,12},{20,16},{24,20},{28,24},{1,29},{... | collective-permute-start | bytes 36872 | tf_op jit(solution)/shard_map/ppermute | solution.py:390
  54.2 3.8 %collective-permute-start.14 = (f32[3,8,128]{2,1,0:T(8,128)S(1)}, f32[3,8,128]{2,1,0:T(8,128)S(1)}, u32[]{:S(2)}, u32[]{:S(2)}) collective-permute-start(f32[3,8,128]{2,1,0:T(8,128)S(1)} %get-tuple-element.71), channel_id=1, source_target_pairs={{0,3},{1,0},{2,1},{3,2},{4,7},{5,4},{6,5},{7,6},{8,11},{9,8},{10,9... | collective-permute-start | bytes 36872 | tf_op jit(solution)/shard_map/ppermute | solution.py:390

commit v4 on v3

v4 whole, which is shorter than its diff:
```python
import functools

import jax
import jax.numpy as jnp
from jax import lax
from jax.experimental import pallas as pl
from jax.experimental.pallas import tpu as pltpu
from jax.sharding import PartitionSpec as P

ITERS = 3
F32 = jnp.float32
LANES = 128
CORNERS = 8
WIDE = 256
SIDES = 6
BACK_X, AHEAD_X, BACK_Y, AHEAD_Y = range(4)
PARITY, PLACE = 0, 2


def upper_blocks(size):
    return [(i, j) for i in range(size // WIDE) for j in range(i, size // WIDE)]


def symmetric_dot(vector, matrix_ref, z):
    size = vector.shape[1]
    kept = upper_blocks(size)
    parts = [vector[:, at : at + WIDE] for at in range(0, size, WIDE)]
    outs = [None] * len(parts)
    for at, (i, j) in enumerate(kept):
        block = matrix_ref[z * len(kept) + at]
        terms = [(j, jnp.dot(parts[i], block, preferred_element_type=F32))]
        if i != j:
            turned = (((1,), (1,)), ((), ()))
            terms.append((i, lax.dot_general(parts[j], block, turned, preferred_element_type=F32)))
        for to, term in terms:
            outs[to] = term if outs[to] is None else outs[to] + term
    return jnp.concatenate(outs, axis=1)


def lane_iota():
    return lax.broadcasted_iota(jnp.int32, (8, LANES), 1)


def pick_lanes(tiles, high, low):
    out = None
    for number, tile in enumerate(tiles):
        moved = jnp.take_along_axis(tile, low, axis=1, mode="promise_in_bounds")
        out = moved if out is None else jnp.where(high == number, moved, out)
    return out


def two_parts(value):
    upper = value.astype(jnp.bfloat16)
    lower = (value - upper.astype(F32)).astype(jnp.bfloat16)
    return jnp.concatenate([upper, lower], axis=0)


def lane_sum(tile):
    return jnp.sum(tile, axis=1, keepdims=True)


def order_tiles(order_ref, z):
    high, low = [], []
    for block in range(SIDES):
        row = jnp.broadcast_to(order_ref[z, :, block * LANES : (block + 1) * LANES], (8, LANES))
        high.append(lax.shift_right_logical(row, 7))
        low.append(lax.bitwise_and(row, LANES - 1))
    return high, low


def prepare_kernel(
    nz, order_hbm, response_hbm, factor_hbm, corners_hbm, matrix_hbm,
    order_ref, slots_ref, vertex_ref, ids_ref, matrix_ref, place_ref, faces_ref, rows_ref,
    response_ref, factor_ref, corners_ref, done,
):
    pairs = [(order_hbm, order_ref), (response_hbm, response_ref), (factor_hbm, factor_ref)]
    pairs.append((corners_hbm, corners_ref))
    small = len(pairs)
    for z in range(nz):
        for i, j in upper_blocks(matrix_hbm.shape[1]):
            block = matrix_hbm.at[z, pl.ds(i * WIDE, WIDE), pl.ds(j * WIDE, WIDE)]
            pairs.append((block, matrix_ref.at[len(pairs) - small]))
    copies = [pltpu.make_async_copy(*pair, done.at[at]) for at, pair in enumerate(pairs)]
    for copy in copies:
        copy.start()
    for copy in copies[:small]:
        copy.wait()
    rows_ref[...] = jnp.zeros_like(rows_ref)
    for at in range(rows_ref.shape[0]):
        rows_ref[at, :, 0 : factor_ref.shape[1]] = factor_ref[at * 8 : (at + 1) * 8, :]
    response = response_ref[...].astype(F32)
    lane = lane_iota()
    lane_square = lax.broadcasted_iota(jnp.int32, (LANES, LANES), 1)
    ids_ref[...] = jnp.zeros_like(ids_ref)
    for z in range(nz):
        ids_ref[:, z * CORNERS : (z + 1) * CORNERS] = jnp.broadcast_to(corners_ref[z], (8, CORNERS))
    slots = slots_ref.shape[0]
    column = jnp.broadcast_to(ids_ref[0:1, :], (LANES, LANES)).T[:slots]
    for at in range(0, vertex_ref.shape[1], LANES):
        hot = jnp.where(column == lane_square[:slots] + at, 1.0, 0.0)
        vertex_ref[:, at : at + LANES] = hot.astype(jnp.bfloat16)
    pieces = [response[z] for z in range(nz)]
    if slots > nz * CORNERS:
        pieces.append(jnp.zeros((slots - nz * CORNERS, response.shape[2]), F32))
    slots_ref[...] = jnp.concatenate(pieces, axis=0).astype(jnp.bfloat16)
    for z in range(nz):
        total = jnp.zeros((16, SIDES * LANES), F32)
        for block in range(SIDES):
            row = order_ref[z, :, block * LANES : (block + 1) * LANES]
            column = jnp.broadcast_to(row, (LANES, LANES)).T
            hot = jnp.concatenate(
                [
                    jnp.where(column == lane_square + side * LANES, 1.0, 0.0).astype(jnp.bfloat16)
                    for side in range(SIDES)
                ],
                axis=1,
            )
            places = jnp.concatenate([lane.astype(F32), jnp.full((8, LANES), block, F32)], axis=0)
            total += jnp.dot(places.astype(jnp.bfloat16), hot, preferred_element_type=F32)
        own = [response[z][:, side * LANES : (side + 1) * LANES] for side in range(SIDES)]
        for side in range(SIDES):
            span = slice(side * LANES, (side + 1) * LANES)
            low = total[:8, span].astype(jnp.int32)
            high = total[8:, span].astype(jnp.int32)
            place_ref[z, :, span] = (high * LANES + low)[0:1]
            faces_ref[z * SIDES + side] = pick_lanes(own, high, low)
    for copy in copies[small:]:
        copy.wait()


def factor_kernel(count, mark_ref, *refs):
    *blocks, inverse_ref, square = refs
    size = square.shape[0]
    row = lax.broadcasted_iota(jnp.int32, (size, size), 0)
    column = lax.broadcasted_iota(jnp.int32, (size, size), 1)
    place = mark_ref[PLACE]
    tall = blocks[0].shape[0]
    for at in range(4 * tall):
        tile = blocks[0][at % tall]
        for mask, block in zip((1, 3, 2), blocks[1:]):
            tile = jnp.where(lax.bitwise_xor(place, mask) == at // tall, block[at % tall], tile)
        square[at * 8 : (at + 1) * 8, :] = tile
    square[4 * tall * 8 :, :] = jnp.zeros((size - 4 * tall * 8, LANES), F32)
    square[...] = jnp.where(row < count, square[...], jnp.where(row == column, 1.0, 0.0))
    factor = square[...]
    lane = lane_iota()
    sub = lax.broadcasted_iota(jnp.int32, (8, LANES), 0)
    corner = lax.bitwise_and(lane, LANES - 8)
    tile = jnp.zeros((8, LANES), F32)
    for at in range(0, size, 8):
        tile = jnp.where(corner == at, factor[at : at + 8, :], tile)
    solved = jnp.where(lane - corner == sub, 1.0, 0.0)
    for q in range(8):
        wide = jnp.take_along_axis(tile, corner + q, axis=1, mode="promise_in_bounds")
        row_q = solved[q : q + 1, :] / wide[q : q + 1, :]
        solved = jnp.where(sub > q, solved - wide * row_q, jnp.where(sub == q, row_q, solved))
    inverse = jnp.concatenate(
        [jnp.where(corner == at, solved, 0.0) for at in range(0, size, 8)], axis=0
    )
    width = 8
    while width < count:
        lower = [
            slice(at, at + width) for at in range(width, size, 2 * width)
        ]
        below = jnp.where(
            (row // (2 * width) == column // (2 * width)) & (row // width > column // width), factor, 0.0
        )
        part = jnp.concatenate([below[rows] for rows in lower], axis=0)
        inner = jnp.dot(part, inverse, precision=lax.Precision.HIGHEST, preferred_element_type=F32)
        left = jnp.concatenate([inverse[rows] for rows in lower], axis=0)
        none = jnp.zeros((width, size), F32)
        spread = []
        for at in range(len(lower)):
            spread += [none, inner[at * width : (at + 1) * width]]
        change = jnp.dot(
            left, jnp.concatenate(spread, axis=0),
            precision=lax.Precision.HIGHEST, preferred_element_type=F32,
        )
        pieces = []
        for at, rows in enumerate(lower):
            pieces += [
                inverse[rows.start - width : rows.start],
                inverse[rows] - change[at * width : (at + 1) * width],
            ]
        inverse = jnp.concatenate(pieces, axis=0)
        width *= 2
    both = lax.dot_general(
        inverse,
        inverse,
        (((0,), (0,)), ((), ())),
        precision=lax.Precision.HIGHEST,
        preferred_element_type=F32,
    )
    inverse_ref[...] = jnp.where((row < count) & (column < count), both, 0.0)


def send_side(nz, mark_ref, axis, faces, outs):
    even = mark_ref[PARITY + axis] == 0
    first, second = outs
    for z in range(nz):
        up, down = faces[z * SIDES + 3 + axis], faces[z * SIDES + axis]
        first[z] = jnp.where(even, up, down)
        second[z] = jnp.where(even, down, up)


def local_part(nz, ncoarse, residual, image, refs):
    (order_ref, matrix_ref, slots_ref, vertex_ref, place_ref, faces_ref) = refs[:6]
    sums_hbm, sums_ref, done = refs[6:]
    own, back = residual
    lane = lane_iota()
    norm = jnp.zeros((8, LANES), F32)
    cross = jnp.zeros((8, LANES), F32)
    for at in range(nz * 3):
        norm += own[at] * own[at]
        if image is not None:
            cross += own[at] * image[at]
    energy = jnp.zeros((8, LANES), F32)
    parts, results = [], []
    for z in range(nz):
        sides = [
            -back[z],
            -back[nz + z],
            -own[((z - 1) % nz) * 3 + 2],
            own[z * 3],
            own[z * 3 + 1],
            own[z * 3 + 2],
        ]
        high, low = order_tiles(order_ref, z)
        vector = jnp.concatenate([pick_lanes(sides, high[s], low[s]) for s in range(SIDES)], axis=1)
        parts.append(two_parts(vector))
        solved = symmetric_dot(parts[z], matrix_ref, z)
        solved = solved[:8] + solved[8:]
        results.append([solved[:, s * LANES : (s + 1) * LANES] for s in range(SIDES)])
        for s in range(SIDES):
            energy += results[z][s] * vector[:, s * LANES : (s + 1) * LANES]
    numbers = (lane_sum(norm), lane_sum(cross), lane_sum(energy))
    products = lax.dot_general(
        jnp.concatenate(parts, axis=0), slots_ref[...], (((1,), (1,)), ((), ())),
        preferred_element_type=F32,
    )
    slot = lax.broadcasted_iota(jnp.int32, (8, products.shape[1]), 1)
    terms = jnp.zeros(slot.shape, F32)
    for z in range(nz):
        both = products[z * 16 : z * 16 + 8] + products[z * 16 + 8 : z * 16 + 16]
        terms = jnp.where(lax.shift_right_logical(slot, 3) == z, both, terms)
    by_vertex = jnp.dot(two_parts(terms), vertex_ref[...], preferred_element_type=F32)
    by_vertex = by_vertex[:8] + by_vertex[8:]
    blocks = vertex_ref.shape[1] // LANES
    for block in range(blocks):
        where = lane + block * LANES
        tile = by_vertex[:, block * LANES : (block + 1) * LANES]
        for at, number in enumerate(numbers):
            tile += jnp.where(where == ncoarse + at, number, 0.0)
        for copy in range(0, sums_ref.shape[0], blocks):
            sums_ref[copy + block] = tile
    leaving = pltpu.make_async_copy(sums_ref, sums_hbm, done)
    leaving.start()
    faces = []
    for z in range(nz):
        high, low = order_tiles(place_ref, z)
        for s in range(SIDES):
            at = z * SIDES + s
            faces.append(pick_lanes(results[z], high[s], low[s]))
            faces_ref[at] = faces[at]
    return faces, leaving


def start_kernel(
    nz, ncoarse, mark_ref, rhs_ref, back_x_ref, back_y_ref, order_ref, matrix_ref,
    slots_ref, vertex_ref, place_ref, ids_ref, response_faces_ref,
    residual_ref, faces_ref, sums_hbm, x_first, x_second, y_first, y_second, sums_ref, done,
):
    own = [rhs_ref[at] for at in range(nz * 3)]
    back = [back_x_ref[z * 3] for z in range(nz)] + [back_y_ref[z * 3 + 1] for z in range(nz)]
    for at, tile in enumerate(own + back):
        residual_ref[at] = tile
    refs = (order_ref, matrix_ref, slots_ref, vertex_ref, place_ref, faces_ref)
    refs += (sums_hbm, sums_ref, done)
    faces, leaving = local_part(nz, ncoarse, (own, back), None, refs)
    numbers = ids_ref[...].astype(F32)
    responses = [response_faces_ref[at] for at in range(nz * SIDES)]
    for axis, outs in ((0, (x_first, x_second)), (1, (y_first, y_second))):
        send_side(nz, mark_ref, axis, faces, outs)
        send_side(nz, mark_ref, axis, responses, [out.at[nz : 2 * nz] for out in outs])
        for out in outs:
            out[2 * nz] = numbers
    leaving.wait()


def step_kernel(first, last, nz, ncoarse, *refs):
    refs = list(refs)

    def take(count):
        taken = refs[:count]
        del refs[:count]
        return taken

    mark_ref, sums_ref, inverse_ref = take(3)
    received = take(2 if last else 4)[::-1]
    faces_ref, response_faces_ref, residual_ref = take(3)
    if first:
        (ids_ref,) = take(1)
    else:
        ids_ref, near_ref, image_ref, direction_ref, multipliers_ref, scalars_ref = take(6)
    if not last:
        order_ref, matrix_ref, slots_ref, vertex_ref, place_ref = take(5)
        (out_residual, out_image, out_direction, out_multipliers, out_scalars, out_faces, out_sums) = take(7)
        sends = take(len(refs) - (4 if first else 2))
        if first:
            out_ids, out_near = take(2)
        sums_scratch, done = take(2)
    else:
        out_multipliers, out_residual = take(2)

    even_x, even_y = mark_ref[PARITY] == 0, mark_ref[PARITY + 1] == 0
    lane = lane_iota()

    def ahead_and_back(at):
        if last:
            return {AHEAD_X: received[0][at], AHEAD_Y: received[1][at]}
        x_first, x_second, y_first, y_second = [ref[at] for ref in received]
        return {
            AHEAD_X: jnp.where(even_x, x_first, x_second),
            BACK_X: jnp.where(even_x, x_second, x_first),
            AHEAD_Y: jnp.where(even_y, y_first, y_second),
            BACK_Y: jnp.where(even_y, y_second, y_first),
        }

    near_faces, near_responses = {}, {}
    for z in range(nz):
        for side, tile in ahead_and_back(z).items():
            near_faces[side, z] = tile
    if first:
        ids = ids_ref[...]
        for side, tile in ahead_and_back(2 * nz).items():
            shift = nz * CORNERS * (side + 1)
            moved = pltpu.roll(tile, shift, axis=1).astype(jnp.int32)
            ids = jnp.where((lane >= shift) & (lane < shift + nz * CORNERS), moved, ids)
        out_ids[...] = ids
        for z in range(nz):
            for side, tile in ahead_and_back(nz + z).items():
                near_responses[side, z] = tile
                out_near[side * nz + z] = tile
    else:
        ids = ids_ref[...]
        for z in range(nz):
            for side in (AHEAD_X, AHEAD_Y) if last else range(4):
                near_responses[side, z] = near_ref[side * nz + z]

    blocks = inverse_ref.shape[0] // LANES
    sums = [sums_ref[block] for block in range(blocks)]
    for copy in range(blocks, sums_ref.shape[0], blocks):
        sums = [total + sums_ref[copy + block] for block, total in enumerate(sums)]
    coarse = jnp.dot(
        jnp.concatenate(sums, axis=1),
        inverse_ref[...],
        precision=lax.Precision.HIGHEST,
        preferred_element_type=F32,
    )
    coarse = [coarse[:, b * LANES : (b + 1) * LANES] for b in range(coarse.shape[1] // LANES)]
    energy = sum(lane_sum(a * b) for a, b in zip(sums, coarse))

    def number(at):
        block, place = divmod(ncoarse + at, LANES)
        return sums[block][:, place : place + 1]

    norm, cross, energy = number(0), number(1), energy + number(2)
    if first:
        curvature = energy
    else:
        last_norm, last_curvature = scalars_ref[0][:, 0:1], scalars_ref[1][:, 0:1]
        ratio = norm / last_norm
        curvature = energy + 2.0 * ratio * cross + ratio * ratio * last_curvature
    step = norm / curvature

    picked = pick_lanes(coarse, lax.shift_right_logical(ids, 7), lax.bitwise_and(ids, LANES - 1))

    wide = {}

    def lifted(tile, response, slot):
        for corner in range(CORNERS):
            at = slot * CORNERS + corner
            if at not in wide:
                wide[at] = jnp.broadcast_to(picked[:, at : at + 1], (8, LANES))
            tile = tile + wide[at] * response[corner : corner + 1, :]
        return tile

    def own_side(z, side):
        at = z * SIDES + side
        return lifted(faces_ref[at], response_faces_ref[at], z)

    def near_side(side, z):
        return lifted(near_faces[side, z], near_responses[side, z], nz * (side + 1) + z)

    fresh = [None] * (nz * 5)
    third_down = [own_side(z, 2) for z in range(nz)]
    for z in range(nz):
        fresh[z * 3] = own_side(z, 3) - near_side(AHEAD_X, z)
        fresh[z * 3 + 1] = own_side(z, 4) - near_side(AHEAD_Y, z)
        fresh[z * 3 + 2] = own_side(z, 5) - third_down[(z + 1) % nz]
        if not last:
            fresh[nz * 3 + z] = near_side(BACK_X, z) - own_side(z, 0)
            fresh[nz * 4 + z] = near_side(BACK_Y, z) - own_side(z, 1)

    count = nz * 3 if last else nz * 5
    residual, image = [], []
    for at in range(count):
        new_image = fresh[at] if first else fresh[at] + ratio * image_ref[at]
        old_residual = residual_ref[at]
        residual.append(old_residual - step * new_image)
        image.append(new_image)
        if at < nz * 3:
            direction = old_residual if first else old_residual + ratio * direction_ref[at]
            multipliers = step * direction if first else multipliers_ref[at] + step * direction
            if last:
                out_multipliers[at] = multipliers
                out_residual[at] = residual[at]
            else:
                out_direction[at] = direction
                out_multipliers[at] = multipliers
    if last:
        return
    for at in range(count):
        out_residual[at] = residual[at]
        out_image[at] = image[at]
    out_scalars[0] = jnp.broadcast_to(norm, (8, LANES))
    out_scalars[1] = jnp.broadcast_to(curvature, (8, LANES))
    refs = (order_ref, matrix_ref, slots_ref, vertex_ref, place_ref, out_faces)
    refs += (out_sums, sums_scratch, done)
    faces, leaving = local_part(nz, ncoarse, (residual[: nz * 3], residual[nz * 3 :]), image, refs)
    if len(sends) == 2:
        for axis, out in enumerate(sends):
            for z in range(nz):
                out[z] = faces[z * SIDES + axis]
    else:
        send_side(nz, mark_ref, 0, faces, sends[:2])
        send_side(nz, mark_ref, 1, faces, sends[2:])
    leaving.wait()


def tiles(count, kind=F32):
    return jax.ShapeDtypeStruct((count, 8, LANES), kind)


def like(value):
    return jax.ShapeDtypeStruct(value.shape, value.dtype)


def call(kernel, outs, operands, first_space, flops, scratch=(), hbm=(), hbm_out=None):
    limit = 16 * 2**20 if max(x.size for x in operands) < 2**21 else 48 * 2**20
    vmem = pl.BlockSpec(memory_space=pltpu.VMEM)
    specs = [pl.BlockSpec(memory_space=first_space)] + [vmem] * (len(operands) - 1)
    operands = list(operands)
    for at in hbm:
        specs[at] = pl.BlockSpec(memory_space=pltpu.HBM)
        operands[at] = pltpu.with_memory_space_constraint(operands[at], pltpu.HBM)
    return pl.pallas_call(
        kernel,
        out_shape=outs,
        in_specs=specs,
        out_specs=[
            pl.BlockSpec(memory_space=pltpu.HBM) if at == hbm_out else vmem for at in range(len(outs))
        ],
        scratch_shapes=scratch,
        compiler_params=pltpu.CompilerParams(vmem_limit_bytes=limit),
        cost_estimate=pl.CostEstimate(flops=flops, bytes_accessed=2**20, transcendentals=0),
    )(*operands)


def shifted(value, axis, steps):
    count = lax.axis_size(axis)
    return lax.ppermute(value, axis, [(i, (i + steps) % count) for i in range(count)])


def paired(value, axis, mask):
    return lax.ppermute(value, axis, [(i, i ^ mask) for i in range(lax.axis_size(axis))])


def paired_other(value, axis):
    count = lax.axis_size(axis)
    return lax.ppermute(value, axis, [(i, (i + 1 if i % 2 else i - 1) % count) for i in range(count)])


def summed(sums, spread):
    if spread:
        return lax.all_to_all(sums, ("sub", "slab"), 0, 0, tiled=True)
    return doubled(doubled(sums, "slab", 1), "sub", 1)


def exchange(sums, sends, spread, rows=None):
    x_first, x_second, y_first, y_second = sends
    near = y_first.shape[0]
    blocks = []
    if rows is not None:
        y_first, y_second = jnp.concatenate([y_first, rows]), jnp.concatenate([y_second, rows])
    sums = summed(sums, spread)
    got_y_second, got_y_first = paired_other(y_second, "slab"), paired(y_first, "slab", 1)
    if rows is not None:
        blocks = [rows, got_y_first[near:], got_y_second[near:], paired(rows, "slab", 2)]
        got_y_first, got_y_second = got_y_first[:near], got_y_second[:near]
    got_x_second, got_x_first = paired_other(x_second, "sub"), paired(x_first, "sub", 1)
    return sums, [got_x_first, got_x_second, got_y_first, got_y_second], blocks


def exchange_last(sums, sends, spread):
    sums = summed(sums, spread)
    return sums, [shifted(sends[0], "sub", -1), shifted(sends[1], "slab", -1)]


def doubled(sums, axis, mask):
    while mask < lax.axis_size(axis):
        sums = sums + paired(sums, axis, mask)
        mask *= 2
    return sums


def coarse_inverse(coarse_factor, width):
    factor = lax.all_gather(coarse_factor, "slab", axis=0, tiled=True)
    count = factor.shape[0]
    inverse = lax.linalg.triangular_solve(
        factor, jnp.eye(count, dtype=F32), left_side=True, lower=True
    )
    both = jnp.dot(inverse.T, inverse, precision=lax.Precision.HIGHEST)
    columns = -(-count // LANES) * LANES
    return jnp.pad(both, ((0, width - count), (0, columns - count)))


def local(interface_rhs, order, inverse_rr, corner_response, corners, coarse_factor):
    nz, samples, dirs, face = interface_rhs.shape[2:]
    ncoarse = coarse_factor.shape[1]
    local_size = SIDES * face
    blocks = -(-(ncoarse + 3) // LANES)
    rhs = interface_rhs.transpose(0, 1, 2, 4, 3, 5).reshape(nz * dirs, samples, face)
    order = order.reshape(nz, 1, local_size)
    matrices = inverse_rr.reshape(nz, local_size, local_size)
    responses = corner_response.reshape(nz, CORNERS, local_size)
    place = lax.axis_index("slab")
    marks = jnp.stack([lax.axis_index("sub") % 2, place % 2, place]).astype(jnp.int32)
    marks = jnp.broadcast_to(marks[:, None, None], (3, 8, LANES))

    back_x = shifted(rhs, "sub", 1)
    back_y = shifted(rhs, "slab", 1)
    devices = lax.axis_size("sub") * lax.axis_size("slab")
    riding = blocks == 1 and lax.axis_size("slab") == 4 and coarse_factor.shape[0] % 8 == 0
    spread = blocks * devices <= 64
    copies = devices if spread else 1
    tables = nz * SIDES
    rows = coarse_factor.shape[0] // 8 if riding else 1
    part = coarse_factor[: rows * 8, :LANES]
    kept = nz * len(upper_blocks(local_size))
    kept = jax.ShapeDtypeStruct((kept, WIDE, WIDE), matrices.dtype)
    slots = -(-nz * CORNERS // 16) * 16
    order, slots, vertex, ids, matrices, unorder, response_faces, rows = call(
        functools.partial(prepare_kernel, nz),
        [like(order), jax.ShapeDtypeStruct((slots, local_size), jnp.bfloat16),
         jax.ShapeDtypeStruct((slots, blocks * LANES), jnp.bfloat16),
         jax.ShapeDtypeStruct((8, LANES), jnp.int32), kept, like(order), tiles(tables), tiles(rows)],
        [order, responses, part, corners.reshape(nz, 1, CORNERS), matrices],
        pltpu.HBM,
        2**30,
        [pltpu.VMEM(responses.shape, responses.dtype), pltpu.VMEM(part.shape, F32),
         pltpu.VMEM((nz, 1, CORNERS), jnp.int32), pltpu.SemaphoreType.DMA((4 + kept.shape[0],))],
        range(5),
    )
    own = [order, matrices, slots, vertex, unorder]
    leaving = [pltpu.VMEM((blocks * copies, 8, LANES), F32), pltpu.SemaphoreType.DMA]
    residual, faces, sums, *sends = call(
        functools.partial(start_kernel, nz, ncoarse),
        [tiles(nz * 5), tiles(tables), tiles(blocks * copies)]
        + [tiles(2 * nz + 1)] * 4,
        [marks, rhs, back_x, back_y] + own + [ids, response_faces],
        pltpu.VMEM,
        2**30,
        leaving,
        hbm_out=2,
    )
    state = [residual, ids]

    def invert(factor):
        if not riding:
            return coarse_inverse(coarse_factor, blocks * LANES)
        square = jax.ShapeDtypeStruct((LANES, LANES), F32)
        return call(
            functools.partial(factor_kernel, ncoarse), [square], [marks] + factor,
            pltpu.VMEM, 3 * 2**30, [pltpu.VMEM(square.shape, F32)],
        )[0]

    for iteration in range(ITERS):
        first, last = iteration == 0, iteration == ITERS - 1
        if last:
            sums, received = exchange_last(sums, sends, spread)
        else:
            ride = rows if first and riding else None
            sums, received, factor = exchange(sums, sends, spread, ride)
        if first:
            inverse = invert(factor)
        operands = [marks, sums, inverse] + received[::-1] + [faces, response_faces] + state
        kernel = functools.partial(step_kernel, first, last, nz, ncoarse)
        if last:
            outs = [tiles(nz * 3)] * 2
            multipliers, residual = call(kernel, outs, operands, pltpu.VMEM, 2**30)
            break
        outs = [tiles(nz * 5), tiles(nz * 5), tiles(nz * 3), tiles(nz * 3), tiles(2)]
        sides = 2 if iteration == ITERS - 2 else 4
        outs += [tiles(tables), tiles(blocks * copies)]
        outs += [tiles(nz)] * sides
        if first:
            outs += [jax.ShapeDtypeStruct((8, LANES), jnp.int32), tiles(nz * 4)]
        results = call(kernel, outs, operands + own, pltpu.VMEM, 2**31, leaving, hbm_out=6)
        residual, image, direction, multipliers, step, faces, sums = results[:7]
        sends = results[7 : 7 + sides]
        if first:
            ids, near = results[7 + sides :]
        state = [residual, ids, near, image, direction, multipliers, step]

    def placed(value):
        value = value.reshape(interface_rhs.shape[:3] + (dirs, samples, face))
        return value.transpose(0, 1, 2, 4, 3, 5)

    return placed(multipliers), placed(residual)


def solution(mesh):
    in_specs = (
        P("sub", "slab", None, None, None, None),
        P("sub", "slab", None, None),
        P("sub", "slab", None, None, None),
        P("sub", "slab", None, None, None),
        P("sub", "slab", None, None),
        P("slab", None),
    )
    out_specs = (P("sub", "slab", None, None, None, None), P("sub", "slab", None, None, None, None))
    return jax.shard_map(local, mesh=mesh, in_specs=in_specs, out_specs=out_specs, check_vma=False)
```

time: 61.2 us -> 54.8 us (0.90)
  Pallas kernels: 15 us -> 11.2 us
  starting transfers between devices: 27 us -> 30.8 us
  waiting for transfers between devices: 15.2 us -> 11.6 us
  local copies, waits for them, and re-layouts: 2.12 us -> 0.09 us
  other arithmetic: 0.82 us -> 0.09 us
    ppermute x8 -> x5, waiting for transfers between devices: 5.17 us -> 0.54 us  [paired(): lax.ppermute(value, axis, [(i, i ^ mask) for i in range(lax.axis_size(axi...]
    pallas_call x6, Pallas kernels: 15 us -> 11.2 us  [call(): pl.pallas_call(kernel, out_shape=outs, in_specs=specs, out_specs=[pl.Bloc...]
    all_to_all x2 -> x3, starting transfers between devices: 5.97 us -> 9.37 us  [summed(): return lax.all_to_all(sums, ('sub', 'slab'), 0, 0, tiled=True)]
    ppermute x3 -> x4, starting transfers between devices: 6.67 us -> 9.81 us  [paired_other(): lax.ppermute(value, axis, [(i, (i + 1 if i % 2 else i - 1) % count) for i...]
    ppermute x3 -> x4, waiting for transfers between devices: 5.73 us -> 3.1 us  [paired_other(): lax.ppermute(value, axis, [(i, (i + 1 if i % 2 else i - 1) % count) for i...]
    ppermute x8 -> x5, starting transfers between devices: 5.49 us -> 3.02 us  [paired(): lax.ppermute(value, axis, [(i, i ^ mask) for i in range(lax.axis_size(axi...]
    all_to_all x2 -> x3, waiting for transfers between devices: 1.16 us -> 3.4 us  [summed(): return lax.all_to_all(sums, ('sub', 'slab'), 0, 0, tiled=True)]
    unnamed x6 -> x2, local copies, waits for them, and re-layouts: 2.01 us -> 0.01 us
  transfers between devices with their start and end apart: 17 -> 16, of which waited for: 8 -> 9; matrix products, arithmetic and copies ran while one was open for 1% -> 0% of each run, Pallas kernels for 11% -> 8%
where the time goes in v4:
time: 54.8 us; the launch traced here: 54.5 us
  starting transfers between devices  30.8 us (56%)
  waiting for transfers between devices  11.6 us (21%)
  Pallas kernels  11.2 us (20%)
  between operations  0.76 us (1%)
    pallas_call x6, Pallas kernels, call(): pl.pallas_call(kernel, out_shape=outs, in_specs=specs, out_specs=[pl.Bloc...  11.2 us
    ppermute x4, starting transfers between devices, paired_other(): lax.ppermute(value, axis, [(i, (i + 1 if i % 2 else i - 1) % count) for i...  9.81 us
    all_to_all x3, starting transfers between devices, summed(): return lax.all_to_all(sums, ('sub', 'slab'), 0, 0, tiled=True)  9.37 us
    ppermute x4, starting transfers between devices, shifted(): lax.ppermute(value, axis, [(i, (i + steps) % count) for i in range(count)])  8.55 us
    ppermute x4, waiting for transfers between devices, shifted(): lax.ppermute(value, axis, [(i, (i + steps) % count) for i in range(count)])  4.57 us
    all_to_all x3, waiting for transfers between devices, summed(): return lax.all_to_all(sums, ('sub', 'slab'), 0, 0, tiled=True)  3.4 us
    ppermute x4, waiting for transfers between devices, paired_other(): lax.ppermute(value, axis, [(i, (i + 1 if i % 2 else i - 1) % count) for i...  3.1 us
    ppermute x5, starting transfers between devices, paired(): lax.ppermute(value, axis, [(i, i ^ mask) for i in range(lax.axis_size(axi...  3.02 us
  transfers between devices with their start and end apart: 16, of which 9 were waited for; matrix products, arithmetic and copies ran while one was open for 0% of the time, Pallas kernels for 8%

profile of v4, /device:TPU:0, one launch (start us, length us, event | category | flops | bytes accessed | tf_op | source)
XLA Modules:
  0.0 54.5 jit_solution(12856344264943898271)
XLA Ops:
  0.6 0.0 copy-start
  0.6 3.0 %collective-permute-start.1 = (f32[9,8,128]{2,1,0:T(8,128)}, f32[9,8,128]{2,1,0:T(8,128)S(1)}, u32[]{:S(2)}, u32[]{:S(2)}) collective-permute-start(f32[9,8,128]{2,1,0:T(8,128)} %bitcast.16), channel_id=1, source_target_pairs={{0,1},{1,2},{2,3},{3,0},{4,5},{5,6},{6,7},{7,4},{8,9},{9,10},{10,1... | collective-permute-start | bytes 110600 | tf_op jit(solution)/shard_map/ppermute | solution.py:472
  3.6 0.0 collective-permute-start
  3.6 0.1 pad_add_fusion
  3.7 2.1 %shard_map.77 = (s32[3,1,768]{2,1,0:T(1,128)S(1)}, bf16[32,768]{1,0:T(8,128)(2,1)S(1)}, bf16[32,128]{1,0:T(8,128)(2,1)S(1)}, s32[8,128]{1,0:T(8,128)S(1)}, bf16[...) custom-call(s32[3,1,768]{2,1,0:T(1,128)} %bitcast.21, ...), custom_call_target="tpu_custom_call" | custom-call | flops 1073741824 | bytes 1048576 | tf_op jit(solution)/shard_map/pallas_call | solution.py:457
  5.9 0.9 %collective-permute-done.1.back_y_ref = f32[9,8,128]{2,1,0:T(8,128)S(1)} collective-permute-done((f32[9,8,128]{2,1,0:T(8,128)}, f32[9,8,128]{2,1,0:T(8,128)S(1)}, u32[]{:S(2)}, u32[]{:S(2)}) %collective-permute-start.1) | collective-permute-done | bytes 36896 | tf_op jit(solution)/shard_map/ppermute | solution.py:472
  6.7 2.3 %collective-permute-done.back_x_ref = f32[9,8,128]{2,1,0:T(8,128)S(1)} collective-permute-done((f32[9,8,128]{2,1,0:T(8,128)}, f32[9,8,128]{2,1,0:T(8,128)S(1)}, u32[]{:S(2)}, u32[]{:S(2)}) %collective-permute-start) | collective-permute-done | bytes 36896 | tf_op jit(solution)/shard_map/ppermute | solution.py:472
  9.0 0.1 broadcast_in_dim.2.mark_ref.refs_0_
  9.1 0.0 copy-done
  9.1 1.6 %shard_map.78 = (f32[15,8,128]{2,1,0:T(8,128)S(1)}, f32[18,8,128]{2,1,0:T(8,128)S(1)}, f32[32,8,128]{2,1,0:T(8,128)}, f32[7,8,128]{2,1,0:T(8,128)S(1)}, f32[7,8,...) custom-call(s32[3,8,128]{2,1,0:T(8,128)S(1)} %broadcast_in_dim.2.mark_ref.refs_0_, ...), custom_call_target="tpu_custom_call" | custom-call | flops 1073741824 | bytes 1048576 | tf_op jit(solution)/shard_map/pallas_call | solution.py:457
  10.7 1.1 %collective-permute-start.3 = (f32[10,8,128]{2,1,0:T(8,128)S(1)}, f32[10,8,128]{2,1,0:T(8,128)S(1)}, u32[]{:S(2)}, u32[]{:S(2)}) collective-permute-start(f32[10,8,128]{2,1,0:T(8,128)S(1)} %get-tuple-element.80), channel_id=1, source_target_pairs={{0,3},{1,2},{2,1},{3,0},{4,7},{5,6},{6,5},{7,4},{8,11},{9,10},{10,... | collective-permute-start | bytes 122888 | tf_op jit(solution)/shard_map/ppermute | solution.py:481
  11.8 2.0 %collective-permute-start.2 = (f32[10,8,128]{2,1,0:T(8,128)S(1)}, f32[10,8,128]{2,1,0:T(8,128)S(1)}, u32[]{:S(2)}, u32[]{:S(2)}) collective-permute-start(f32[10,8,128]{2,1,0:T(8,128)S(1)} %get-tuple-element.81), channel_id=1, source_target_pairs={{0,1},{1,0},{2,3},{3,2},{4,5},{5,4},{6,7},{7,6},{8,9},{9,8},{10,11... | collective-permute-start | bytes 122888 | tf_op jit(solution)/shard_map/ppermute | solution.py:476
  13.8 0.5 collective-permute-start.4
  14.3 3.1 %all-to-all-start = ((f32[32,8,128]{2,1,0:T(8,128)}), f32[32,8,128]{2,1,0:T(8,128)S(1)}, u32[]{:S(2)}, u32[]{:S(2)}) async-start(f32[32,8,128]{2,1,0:T(8,128)} %get-tuple-element.48), calls=%async_computation | async-start | bytes 262144 | tf_op jit(solution)/shard_map/all_to_all | solution.py:486
  17.4 3.4 %collective-permute-start.5 = (f32[7,8,128]{2,1,0:T(8,128)S(1)}, f32[7,8,128]{2,1,0:T(8,128)S(1)}, u32[]{:S(2)}, u32[]{:S(2)}) collective-permute-start(f32[7,8,128]{2,1,0:T(8,128)S(1)} %get-tuple-element.52), channel_id=1, source_target_pairs={{0,28},{4,8},{8,4},{12,16},{16,12},{20,24},{24,20},{28,0},{1,29},{... | collective-permute-start | bytes 86024 | tf_op jit(solution)/shard_map/ppermute | solution.py:481
  20.9 0.0 collective-permute-start.6
  20.9 0.0 collective-permute-done.3
  20.9 0.0 collective-permute-done.2
  20.9 0.0 collective-permute-done.4.refs_3_
  20.9 2.1 %shard_map.79.refs_2_ = f32[128,128]{1,0:T(8,128)S(1)} custom-call(s32[3,8,128]{2,1,0:T(8,128)S(1)} %broadcast_in_dim.2.mark_ref.refs_0_, f32[3,8,128]{2,1,0:T(8,128)S(1)} %get-tuple-element.49.refs_0_, f32[3,8,128]{2,1,0:T(8,128)S(1)} %slice.16.refs_1_, f32[3,8,128]{2,1,0:T(8,128)S(1)} %slice.17.refs_2_, f32[3,8,128]{2,1,0:T(8,128)S(1)} %collective-permute-done.4.refs_3_), custom_call_target="tpu_custom_call" | custom-call | flops 3221225472 | bytes 1048576 | tf_op jit(solution)/shard_map/pallas_call | solution.py:457
  23.0 1.4 %collective-permute-done.5.refs_5_ = f32[7,8,128]{2,1,0:T(8,128)S(1)} collective-permute-done((f32[7,8,128]{2,1,0:T(8,128)S(1)}, f32[7,8,128]{2,1,0:T(8,128)S(1)}, u32[]{:S(2)}, u32[]{:S(2)}) %collective-permute-start.5) | collective-permute-done | bytes 28704 | tf_op jit(solution)/shard_map/ppermute | solution.py:481
  24.4 0.0 collective-permute-done.6.refs_6_
  24.4 1.7 %all-to-all-done.refs_1_ = f32[32,8,128]{2,1,0:T(8,128)S(1)} async-done(((f32[32,8,128]{2,1,0:T(8,128)}), f32[32,8,128]{2,1,0:T(8,128)S(1)}, u32[]{:S(2)}, u32[]{:S(2)}) %all-to-all-start) | async-done | bytes 131104 | tf_op jit(solution)/shard_map/all_to_all | solution.py:486
  26.1 2.2 %shard_map.80 = (f32[15,8,128]{2,1,0:T(8,128)S(1)}, f32[15,8,128]{2,1,0:T(8,128)S(1)}, f32[9,8,128]{2,1,0:T(8,128)S(1)}, f32[9,8,128]{2,1,0:T(8,128)S(1)}, f32[2...) custom-call(s32[3,8,128]{2,1,0:T(8,128)S(1)} %broadcast_in_dim.2.mar, ...), custom_call_target="tpu_custom_call" | custom-call | flops 2147483648 | bytes 1048576 | tf_op jit(solution)/shard_map/pallas_call | solution.py:457
  28.2 2.6 %all-to-all-start.1 = ((f32[32,8,128]{2,1,0:T(8,128)}), f32[32,8,128]{2,1,0:T(8,128)S(1)}, u32[]{:S(2)}, u32[]{:S(2)}) async-start(f32[32,8,128]{2,1,0:T(8,128)} %get-tuple-element.56), calls=%async_computation.1 | async-start | bytes 262144 | tf_op jit(solution)/shard_map/all_to_all | solution.py:486
  30.8 2.6 %collective-permute-start.7 = (f32[3,8,128]{2,1,0:T(8,128)S(1)}, f32[3,8,128]{2,1,0:T(8,128)S(1)}, u32[]{:S(2)}, u32[]{:S(2)}) collective-permute-start(f32[3,8,128]{2,1,0:T(8,128)S(1)} %get-tuple-element.57), channel_id=1, source_target_pairs={{0,3},{1,2},{2,1},{3,0},{4,7},{5,6},{6,5},{7,4},{8,11},{9,10},{10,... | collective-permute-start | bytes 36872 | tf_op jit(solution)/shard_map/ppermute | solution.py:481
  33.5 0.5 %collective-permute-start.8 = (f32[3,8,128]{2,1,0:T(8,128)S(1)}, f32[3,8,128]{2,1,0:T(8,128)S(1)}, u32[]{:S(2)}, u32[]{:S(2)}) collective-permute-start(f32[3,8,128]{2,1,0:T(8,128)S(1)} %get-tuple-element.58), channel_id=1, source_target_pairs={{0,1},{1,0},{2,3},{3,2},{4,5},{5,4},{6,7},{7,6},{8,9},{9,8},{10,11... | collective-permute-start | bytes 36872 | tf_op jit(solution)/shard_map/ppermute | solution.py:476
  34.0 2.7 %collective-permute-start.9 = (f32[3,8,128]{2,1,0:T(8,128)S(1)}, f32[3,8,128]{2,1,0:T(8,128)S(1)}, u32[]{:S(2)}, u32[]{:S(2)}) collective-permute-start(f32[3,8,128]{2,1,0:T(8,128)S(1)} %get-tuple-element.59), channel_id=1, source_target_pairs={{0,28},{4,8},{8,4},{12,16},{16,12},{20,24},{24,20},{28,0},{1,29},{... | collective-permute-start | bytes 36872 | tf_op jit(solution)/shard_map/ppermute | solution.py:481
  36.7 0.0 collective-permute-start.10
  36.7 0.0 collective-permute-done.7.refs_3_
  36.7 0.5 collective-permute-done.8.refs_4_
  37.2 1.7 %collective-permute-done.9.refs_5_ = f32[3,8,128]{2,1,0:T(8,128)S(1)} collective-permute-done((f32[3,8,128]{2,1,0:T(8,128)S(1)}, f32[3,8,128]{2,1,0:T(8,128)S(1)}, u32[]{:S(2)}, u32[]{:S(2)}) %collective-permute-start.9) | collective-permute-done | bytes 12320 | tf_op jit(solution)/shard_map/ppermute | solution.py:481
  38.9 0.0 collective-permute-done.10.refs_6_
  38.9 0.3 all-to-all-done.1.refs_1_
  39.2 2.1 %shard_map.81 = (f32[15,8,128]{2,1,0:T(8,128)S(1)}, f32[15,8,128]{2,1,0:T(8,128)S(1)}, f32[9,8,128]{2,1,0:T(8,128)S(1)}, f32[9,8,128]{2,1,0:T(8,128)S(1)}, f32[2...) custom-call(s32[3,8,128]{2,1,0:T(8,128)S(1)} %broadcast_in_dim.2.mar, ...), custom_call_target="tpu_custom_call" | custom-call | flops 2147483648 | bytes 1048576 | tf_op jit(solution)/shard_map/pallas_call | solution.py:457
  41.4 3.6 %all-to-all-start.2 = ((f32[32,8,128]{2,1,0:T(8,128)}), f32[32,8,128]{2,1,0:T(8,128)S(1)}, u32[]{:S(2)}, u32[]{:S(2)}) async-start(f32[32,8,128]{2,1,0:T(8,128)} %get-tuple-element.69), calls=%async_computation.2 | async-start | bytes 262144 | tf_op jit(solution)/shard_map/all_to_all | solution.py:486
  45.0 2.7 %collective-permute-start.11 = (f32[3,8,128]{2,1,0:T(8,128)S(1)}, f32[3,8,128]{2,1,0:T(8,128)S(1)}, u32[]{:S(2)}, u32[]{:S(2)}) collective-permute-start(f32[3,8,128]{2,1,0:T(8,128)S(1)} %get-tuple-element.70), channel_id=1, source_target_pairs={{0,3},{1,0},{2,1},{3,2},{4,7},{5,4},{6,5},{7,6},{8,11},{9,8},{10,9... | collective-permute-start | bytes 36872 | tf_op jit(solution)/shard_map/ppermute | solution.py:472
  47.7 2.8 %collective-permute-start.12 = (f32[3,8,128]{2,1,0:T(8,128)S(1)}, f32[3,8,128]{2,1,0:T(8,128)S(1)}, u32[]{:S(2)}, u32[]{:S(2)}) collective-permute-start(f32[3,8,128]{2,1,0:T(8,128)S(1)} %get-tuple-element.71), channel_id=1, source_target_pairs={{0,28},{4,0},{8,4},{12,8},{16,12},{20,16},{24,20},{28,24},{1,29},{... | collective-permute-start | bytes 36872 | tf_op jit(solution)/shard_map/ppermute | solution.py:472
  50.6 0.0 collective-permute-done.11.refs_3_
  50.6 1.4 %collective-permute-done.12.refs_4_ = f32[3,8,128]{2,1,0:T(8,128)S(1)} collective-permute-done((f32[3,8,128]{2,1,0:T(8,128)S(1)}, f32[3,8,128]{2,1,0:T(8,128)S(1)}, u32[]{:S(2)}, u32[]{:S(2)}) %collective-permute-start.12) | collective-permute-done | bytes 12320 | tf_op jit(solution)/shard_map/ppermute | solution.py:472
  52.0 1.4 %all-to-all-done.2.refs_1_ = f32[32,8,128]{2,1,0:T(8,128)S(1)} async-done(((f32[32,8,128]{2,1,0:T(8,128)}), f32[32,8,128]{2,1,0:T(8,128)S(1)}, u32[]{:S(2)}, u32[]{:S(2)}) %all-to-all-start.2) | async-done | bytes 131104 | tf_op jit(solution)/shard_map/all_to_all | solution.py:486
  53.4 1.1 %shard_map.82 = (f32[9,8,128]{2,1,0:T(8,128)}, f32[9,8,128]{2,1,0:T(8,128)}) custom-call(s32[3,8,128]{2,1,0:T(8,128)S(1)} %broadcast_in_dim.2.mark_ref.refs_0_, f32[32,8,128]{2,1,0:T(8,128)S(1)} %all-to-all-done.2.refs_1_, f32[128,128]{1,0:T(8,128)S(1)} %shard_map.79.refs_2_, f32[3,8,128]{2,1,0:T(8,128)S(1)} %collective-permute-done.11.refs_3_, ...), custom_call_target="tpu_custom_call" | custom-call | flops 1073741824 | bytes 1048576 | tf_op jit(solution)/shard_map/pallas_call | solution.py:457
  (5 shorter events, 0.0 us)
Async XLA Ops:
  0.6 8.5 %copy-start = (f32[1,1,3,8,3,128]{5,3,4,2,1,0:T(8,128)S(1)}, f32[1,1,3,8,3,128]{5,3,4,2,1,0:T(8,128)}, u32[]{:S(2)}) copy-start(f32[1,1,3,8,3,128]{5,3,4,2,1,0:T(8,128)} %param.6) | copy-start | bytes 110596
  0.6 6.1 %collective-permute-start.1 = (f32[9,8,128]{2,1,0:T(8,128)}, f32[9,8,128]{2,1,0:T(8,128)S(1)}, u32[]{:S(2)}, u32[]{:S(2)}) collective-permute-start(f32[9,8,128]{2,1,0:T(8,128)} %bitcast.16), channel_id=1, source_target_pairs={{0,1},{1,2},{2,3},{3,0},{4,5},{5,6},{6,7},{7,4},{8,9},{9,10},{10,1... | collective-permute-start | bytes 110600 | tf_op jit(solution)/shard_map/ppermute | solution.py:472
  3.6 5.4 %collective-permute-start = (f32[9,8,128]{2,1,0:T(8,128)}, f32[9,8,128]{2,1,0:T(8,128)S(1)}, u32[]{:S(2)}, u32[]{:S(2)}) collective-permute-start(f32[9,8,128]{2,1,0:T(8,128)} %bitcast.17), channel_id=1, source_target_pairs={{0,4},{4,8},{8,12},{12,16},{16,20},{20,24},{24,28},{28,0},{1,5},{5... | collective-permute-start | bytes 110600 | tf_op jit(solution)/shard_map/ppermute | solution.py:472
  10.7 10.1 %collective-permute-start.3 = (f32[10,8,128]{2,1,0:T(8,128)S(1)}, f32[10,8,128]{2,1,0:T(8,128)S(1)}, u32[]{:S(2)}, u32[]{:S(2)}) collective-permute-start(f32[10,8,128]{2,1,0:T(8,128)S(1)} %get-tuple-element.80), channel_id=1, source_target_pairs={{0,3},{1,2},{2,1},{3,0},{4,7},{5,6},{6,5},{7,4},{8,11},{9,10},{10,... | collective-permute-start | bytes 122888 | tf_op jit(solution)/shard_map/ppermute | solution.py:481
  11.8 9.1 %collective-permute-start.2 = (f32[10,8,128]{2,1,0:T(8,128)S(1)}, f32[10,8,128]{2,1,0:T(8,128)S(1)}, u32[]{:S(2)}, u32[]{:S(2)}) collective-permute-start(f32[10,8,128]{2,1,0:T(8,128)S(1)} %get-tuple-element.81), channel_id=1, source_target_pairs={{0,1},{1,0},{2,3},{3,2},{4,5},{5,4},{6,7},{7,6},{8,9},{9,8},{10,11... | collective-permute-start | bytes 122888 | tf_op jit(solution)/shard_map/ppermute | solution.py:476
  13.8 7.1 %collective-permute-start.4 = (f32[3,8,128]{2,1,0:T(8,128)S(1)}, f32[3,8,128]{2,1,0:T(8,128)S(1)}, u32[]{:S(2)}, u32[]{:S(2)}) collective-permute-start(f32[3,8,128]{2,1,0:T(8,128)S(1)} %get-tuple-element.49.refs_0_), channel_id=1, source_target_pairs={{0,2},{1,3},{2,0},{3,1},{4,6},{5,7},{6,4},{7,5},{8,10},{9,11},{10,... | collective-permute-start | bytes 36872 | tf_op jit(solution)/shard_map/ppermute | solution.py:476
  14.3 11.8 %all-to-all-start = ((f32[32,8,128]{2,1,0:T(8,128)}), f32[32,8,128]{2,1,0:T(8,128)S(1)}, u32[]{:S(2)}, u32[]{:S(2)}) async-start(f32[32,8,128]{2,1,0:T(8,128)} %get-tuple-element.48), calls=%async_computation | async-start | bytes 262144 | tf_op jit(solution)/shard_map/all_to_all | solution.py:486
  17.4 7.0 %collective-permute-start.5 = (f32[7,8,128]{2,1,0:T(8,128)S(1)}, f32[7,8,128]{2,1,0:T(8,128)S(1)}, u32[]{:S(2)}, u32[]{:S(2)}) collective-permute-start(f32[7,8,128]{2,1,0:T(8,128)S(1)} %get-tuple-element.52), channel_id=1, source_target_pairs={{0,28},{4,8},{8,4},{12,16},{16,12},{20,24},{24,20},{28,0},{1,29},{... | collective-permute-start | bytes 86024 | tf_op jit(solution)/shard_map/ppermute | solution.py:481
  20.9 3.5 %collective-permute-start.6 = (f32[7,8,128]{2,1,0:T(8,128)S(1)}, f32[7,8,128]{2,1,0:T(8,128)S(1)}, u32[]{:S(2)}, u32[]{:S(2)}) collective-permute-start(f32[7,8,128]{2,1,0:T(8,128)S(1)} %get-tuple-element.53), channel_id=1, source_target_pairs={{0,4},{4,0},{8,12},{12,8},{16,20},{20,16},{24,28},{28,24},{1,5},{5... | collective-permute-start | bytes 86024 | tf_op jit(solution)/shard_map/ppermute | solution.py:476
  28.2 11.0 %all-to-all-start.1 = ((f32[32,8,128]{2,1,0:T(8,128)}), f32[32,8,128]{2,1,0:T(8,128)S(1)}, u32[]{:S(2)}, u32[]{:S(2)}) async-start(f32[32,8,128]{2,1,0:T(8,128)} %get-tuple-element.56), calls=%async_computation.1 | async-start | bytes 262144 | tf_op jit(solution)/shard_map/all_to_all | solution.py:486
  30.8 5.8 %collective-permute-start.7 = (f32[3,8,128]{2,1,0:T(8,128)S(1)}, f32[3,8,128]{2,1,0:T(8,128)S(1)}, u32[]{:S(2)}, u32[]{:S(2)}) collective-permute-start(f32[3,8,128]{2,1,0:T(8,128)S(1)} %get-tuple-element.57), channel_id=1, source_target_pairs={{0,3},{1,2},{2,1},{3,0},{4,7},{5,6},{6,5},{7,4},{8,11},{9,10},{10,... | collective-permute-start | bytes 36872 | tf_op jit(solution)/shard_map/ppermute | solution.py:481
  33.5 3.7 %collective-permute-start.8 = (f32[3,8,128]{2,1,0:T(8,128)S(1)}, f32[3,8,128]{2,1,0:T(8,128)S(1)}, u32[]{:S(2)}, u32[]{:S(2)}) collective-permute-start(f32[3,8,128]{2,1,0:T(8,128)S(1)} %get-tuple-element.58), channel_id=1, source_target_pairs={{0,1},{1,0},{2,3},{3,2},{4,5},{5,4},{6,7},{7,6},{8,9},{9,8},{10,11... | collective-permute-start | bytes 36872 | tf_op jit(solution)/shard_map/ppermute | solution.py:476
  34.0 4.9 %collective-permute-start.9 = (f32[3,8,128]{2,1,0:T(8,128)S(1)}, f32[3,8,128]{2,1,0:T(8,128)S(1)}, u32[]{:S(2)}, u32[]{:S(2)}) collective-permute-start(f32[3,8,128]{2,1,0:T(8,128)S(1)} %get-tuple-element.59), channel_id=1, source_target_pairs={{0,28},{4,8},{8,4},{12,16},{16,12},{20,24},{24,20},{28,0},{1,29},{... | collective-permute-start | bytes 36872 | tf_op jit(solution)/shard_map/ppermute | solution.py:481
  36.7 2.3 %collective-permute-start.10 = (f32[3,8,128]{2,1,0:T(8,128)S(1)}, f32[3,8,128]{2,1,0:T(8,128)S(1)}, u32[]{:S(2)}, u32[]{:S(2)}) collective-permute-start(f32[3,8,128]{2,1,0:T(8,128)S(1)} %get-tuple-element.60), channel_id=1, source_target_pairs={{0,4},{4,0},{8,12},{12,8},{16,20},{20,16},{24,28},{28,24},{1,5},{5... | collective-permute-start | bytes 36872 | tf_op jit(solution)/shard_map/ppermute | solution.py:476
  41.4 12.1 %all-to-all-start.2 = ((f32[32,8,128]{2,1,0:T(8,128)}), f32[32,8,128]{2,1,0:T(8,128)S(1)}, u32[]{:S(2)}, u32[]{:S(2)}) async-start(f32[32,8,128]{2,1,0:T(8,128)} %get-tuple-element.69), calls=%async_computation.2 | async-start | bytes 262144 | tf_op jit(solution)/shard_map/all_to_all | solution.py:486
  45.0 5.6 %collective-permute-start.11 = (f32[3,8,128]{2,1,0:T(8,128)S(1)}, f32[3,8,128]{2,1,0:T(8,128)S(1)}, u32[]{:S(2)}, u32[]{:S(2)}) collective-permute-start(f32[3,8,128]{2,1,0:T(8,128)S(1)} %get-tuple-element.70), channel_id=1, source_target_pairs={{0,3},{1,0},{2,1},{3,2},{4,7},{5,4},{6,5},{7,6},{8,11},{9,8},{10,9... | collective-permute-start | bytes 36872 | tf_op jit(solution)/shard_map/ppermute | solution.py:472
  47.7 4.2 %collective-permute-start.12 = (f32[3,8,128]{2,1,0:T(8,128)S(1)}, f32[3,8,128]{2,1,0:T(8,128)S(1)}, u32[]{:S(2)}, u32[]{:S(2)}) collective-permute-start(f32[3,8,128]{2,1,0:T(8,128)S(1)} %get-tuple-element.71), channel_id=1, source_target_pairs={{0,28},{4,0},{8,4},{12,8},{16,12},{20,16},{24,20},{28,24},{1,29},{... | collective-permute-start | bytes 36872 | tf_op jit(solution)/shard_map/ppermute | solution.py:472

commit v5 on v4

--- a/solution.py
+++ b/solution.py
@@ -204,8 +204,7 @@
 
 
 def local_part(nz, ncoarse, residual, image, refs):
-    (order_ref, matrix_ref, slots_ref, vertex_ref, place_ref, faces_ref) = refs[:6]
-    sums_hbm, sums_ref, done = refs[6:]
+    (order_ref, matrix_ref, slots_ref, vertex_ref, place_ref, faces_ref, sums_ref) = refs
     own, back = residual
     lane = lane_iota()
     norm = jnp.zeros((8, LANES), F32)
@@ -253,8 +252,6 @@
             tile += jnp.where(where == ncoarse + at, number, 0.0)
         for copy in range(0, sums_ref.shape[0], blocks):
             sums_ref[copy + block] = tile
-    leaving = pltpu.make_async_copy(sums_ref, sums_hbm, done)
-    leaving.start()
     faces = []
     for z in range(nz):
         high, low = order_tiles(place_ref, z)
@@ -262,21 +259,20 @@
             at = z * SIDES + s
             faces.append(pick_lanes(results[z], high[s], low[s]))
             faces_ref[at] = faces[at]
-    return faces, leaving
+    return faces
 
 
 def start_kernel(
     nz, ncoarse, mark_ref, rhs_ref, back_x_ref, back_y_ref, order_ref, matrix_ref,
     slots_ref, vertex_ref, place_ref, ids_ref, response_faces_ref,
-    residual_ref, faces_ref, sums_hbm, x_first, x_second, y_first, y_second, sums_ref, done,
+    residual_ref, faces_ref, sums_ref, x_first, x_second, y_first, y_second,
 ):
     own = [rhs_ref[at] for at in range(nz * 3)]
     back = [back_x_ref[z * 3] for z in range(nz)] + [back_y_ref[z * 3 + 1] for z in range(nz)]
     for at, tile in enumerate(own + back):
         residual_ref[at] = tile
-    refs = (order_ref, matrix_ref, slots_ref, vertex_ref, place_ref, faces_ref)
-    refs += (sums_hbm, sums_ref, done)
-    faces, leaving = local_part(nz, ncoarse, (own, back), None, refs)
+    refs = (order_ref, matrix_ref, slots_ref, vertex_ref, place_ref, faces_ref, sums_ref)
+    faces = local_part(nz, ncoarse, (own, back), None, refs)
     numbers = ids_ref[...].astype(F32)
     responses = [response_faces_ref[at] for at in range(nz * SIDES)]
     for axis, outs in ((0, (x_first, x_second)), (1, (y_first, y_second))):
@@ -284,7 +280,6 @@
         send_side(nz, mark_ref, axis, responses, [out.at[nz : 2 * nz] for out in outs])
         for out in outs:
             out[2 * nz] = numbers
-    leaving.wait()
 
 
 def step_kernel(first, last, nz, ncoarse, *refs):
@@ -305,10 +300,9 @@
     if not last:
         order_ref, matrix_ref, slots_ref, vertex_ref, place_ref = take(5)
         (out_residual, out_image, out_direction, out_multipliers, out_scalars, out_faces, out_sums) = take(7)
-        sends = take(len(refs) - (4 if first else 2))
+        sends = take(len(refs) - (2 if first else 0))
         if first:
             out_ids, out_near = take(2)
-        sums_scratch, done = take(2)
     else:
         out_multipliers, out_residual = take(2)
 
@@ -425,9 +419,8 @@
         out_image[at] = image[at]
     out_scalars[0] = jnp.broadcast_to(norm, (8, LANES))
     out_scalars[1] = jnp.broadcast_to(curvature, (8, LANES))
-    refs = (order_ref, matrix_ref, slots_ref, vertex_ref, place_ref, out_faces)
-    refs += (out_sums, sums_scratch, done)
-    faces, leaving = local_part(nz, ncoarse, (residual[: nz * 3], residual[nz * 3 :]), image, refs)
+    refs = (order_ref, matrix_ref, slots_ref, vertex_ref, place_ref, out_faces, out_sums)
+    faces = local_part(nz, ncoarse, (residual[: nz * 3], residual[nz * 3 :]), image, refs)
     if len(sends) == 2:
         for axis, out in enumerate(sends):
             for z in range(nz):
@@ -435,7 +428,6 @@
     else:
         send_side(nz, mark_ref, 0, faces, sends[:2])
         send_side(nz, mark_ref, 1, faces, sends[2:])
-    leaving.wait()
 
 
 def tiles(count, kind=F32):
@@ -446,7 +438,7 @@
     return jax.ShapeDtypeStruct(value.shape, value.dtype)
 
 
-def call(kernel, outs, operands, first_space, flops, scratch=(), hbm=(), hbm_out=None):
+def call(kernel, outs, operands, first_space, flops, scratch=(), hbm=()):
     limit = 16 * 2**20 if max(x.size for x in operands) < 2**21 else 48 * 2**20
     vmem = pl.BlockSpec(memory_space=pltpu.VMEM)
     specs = [pl.BlockSpec(memory_space=first_space)] + [vmem] * (len(operands) - 1)
@@ -458,9 +450,7 @@
         kernel,
         out_shape=outs,
         in_specs=specs,
-        out_specs=[
-            pl.BlockSpec(memory_space=pltpu.HBM) if at == hbm_out else vmem for at in range(len(outs))
-        ],
+        out_specs=[vmem] * len(outs),
         scratch_shapes=scratch,
         compiler_params=pltpu.CompilerParams(vmem_limit_bytes=limit),
         cost_estimate=pl.CostEstimate(flops=flops, bytes_accessed=2**20, transcendentals=0),
@@ -563,7 +553,6 @@
         range(5),
     )
     own = [order, matrices, slots, vertex, unorder]
-    leaving = [pltpu.VMEM((blocks * copies, 8, LANES), F32), pltpu.SemaphoreType.DMA]
     residual, faces, sums, *sends = call(
         functools.partial(start_kernel, nz, ncoarse),
         [tiles(nz * 5), tiles(tables), tiles(blocks * copies)]
@@ -571,8 +560,6 @@
         [marks, rhs, back_x, back_y] + own + [ids, response_faces],
         pltpu.VMEM,
         2**30,
-        leaving,
-        hbm_out=2,
     )
     state = [residual, ids]
 
@@ -582,7 +569,7 @@
         square = jax.ShapeDtypeStruct((LANES, LANES), F32)
         return call(
             functools.partial(factor_kernel, ncoarse), [square], [marks] + factor,
-            pltpu.VMEM, 3 * 2**30, [pltpu.VMEM(square.shape, F32)],
+            pltpu.VMEM, 2**29, [pltpu.VMEM(square.shape, F32)],
         )[0]
 
     for iteration in range(ITERS):
@@ -606,7 +593,7 @@
         outs += [tiles(nz)] * sides
         if first:
             outs += [jax.ShapeDtypeStruct((8, LANES), jnp.int32), tiles(nz * 4)]
-        results = call(kernel, outs, operands + own, pltpu.VMEM, 2**31, leaving, hbm_out=6)
+        results = call(kernel, outs, operands + own, pltpu.VMEM, 2**31)
         residual, image, direction, multipliers, step, faces, sums = results[:7]
         sends = results[7 : 7 + sides]
         if first:

time: 54.8 us -> 53.8 us (0.982)
  waiting for transfers between devices: 11.6 us -> 9.45 us
  starting transfers between devices: 30.8 us -> 31.9 us
    all_to_all x3, starting transfers between devices: 9.37 us -> 11.4 us  [summed(): return lax.all_to_all(sums, ('sub', 'slab'), 0, 0, tiled=True)]
    all_to_all x3, waiting for transfers between devices: 3.4 us -> 1.6 us  [summed(): return lax.all_to_all(sums, ('sub', 'slab'), 0, 0, tiled=True)]
    ppermute x5, starting transfers between devices: 3.02 us -> 1.39 us  [paired(): lax.ppermute(value, axis, [(i, i ^ mask) for i in range(lax.axis_size(axi...]
    ppermute x4, waiting for transfers between devices: 3.1 us -> 1.82 us  [paired_other(): lax.ppermute(value, axis, [(i, (i + 1 if i % 2 else i - 1) % count) for i...]
    ppermute x5, waiting for transfers between devices: 0.54 us -> 1.46 us  [paired(): lax.ppermute(value, axis, [(i, i ^ mask) for i in range(lax.axis_size(axi...]
    ppermute x4, starting transfers between devices: 9.81 us -> 10.5 us  [paired_other(): lax.ppermute(value, axis, [(i, (i + 1 if i % 2 else i - 1) % count) for i...]
where the time goes in v5:
time: 53.8 us; the launch traced here: 53.5 us
  starting transfers between devices  31.9 us (59%)
  Pallas kernels  11.2 us (21%)
  waiting for transfers between devices  9.45 us (18%)
  between operations  0.73 us (1%)
    all_to_all x3, starting transfers between devices, summed(): return lax.all_to_all(sums, ('sub', 'slab'), 0, 0, tiled=True)  11.4 us
    pallas_call x6, Pallas kernels, call(): pl.pallas_call(kernel, out_shape=outs, in_specs=specs, out_specs=[vmem] *...  11.2 us
    ppermute x4, starting transfers between devices, paired_other(): lax.ppermute(value, axis, [(i, (i + 1 if i % 2 else i - 1) % count) for i...  10.5 us
    ppermute x4, starting transfers between devices, shifted(): lax.ppermute(value, axis, [(i, (i + steps) % count) for i in range(count)])  8.55 us
    ppermute x4, waiting for transfers between devices, shifted(): lax.ppermute(value, axis, [(i, (i + steps) % count) for i in range(count)])  4.57 us
    ppermute x4, waiting for transfers between devices, paired_other(): lax.ppermute(value, axis, [(i, (i + 1 if i % 2 else i - 1) % count) for i...  1.82 us
    all_to_all x3, waiting for transfers between devices, summed(): return lax.all_to_all(sums, ('sub', 'slab'), 0, 0, tiled=True)  1.6 us
    ppermute x5, waiting for transfers between devices, paired(): lax.ppermute(value, axis, [(i, i ^ mask) for i in range(lax.axis_size(axi...  1.46 us
  transfers between devices with their start and end apart: 16, of which 9 were waited for; matrix products, arithmetic and copies ran while one was open for 0% of the time, Pallas kernels for 8%

profile of v5, /device:TPU:0, one launch (start us, length us, event | category | flops | bytes accessed | tf_op | source)
XLA Modules:
  0.0 53.5 jit_solution(17884071092220980350)
XLA Ops:
  0.6 0.0 copy-start
  0.6 3.0 %collective-permute-start.1 = (f32[9,8,128]{2,1,0:T(8,128)}, f32[9,8,128]{2,1,0:T(8,128)S(1)}, u32[]{:S(2)}, u32[]{:S(2)}) collective-permute-start(f32[9,8,128]{2,1,0:T(8,128)} %bitcast.16), channel_id=1, source_target_pairs={{0,1},{1,2},{2,3},{3,0},{4,5},{5,6},{6,7},{7,4},{8,9},{9,10},{10,1... | collective-permute-start | bytes 110600 | tf_op jit(solution)/shard_map/ppermute | solution.py:462
  3.6 0.0 collective-permute-start
  3.6 0.1 pad_add_fusion
  3.7 2.1 %shard_map.77 = (s32[3,1,768]{2,1,0:T(1,128)S(1)}, bf16[32,768]{1,0:T(8,128)(2,1)S(1)}, bf16[32,128]{1,0:T(8,128)(2,1)S(1)}, s32[8,128]{1,0:T(8,128)S(1)}, bf16[...) custom-call(s32[3,1,768]{2,1,0:T(1,128)} %bitcast.21, ...), custom_call_target="tpu_custom_call" | custom-call | flops 1073741824 | bytes 1048576 | tf_op jit(solution)/shard_map/pallas_call | solution.py:449
  5.9 0.9 %collective-permute-done.1.back_y_ref = f32[9,8,128]{2,1,0:T(8,128)S(1)} collective-permute-done((f32[9,8,128]{2,1,0:T(8,128)}, f32[9,8,128]{2,1,0:T(8,128)S(1)}, u32[]{:S(2)}, u32[]{:S(2)}) %collective-permute-start.1) | collective-permute-done | bytes 36896 | tf_op jit(solution)/shard_map/ppermute | solution.py:462
  6.7 2.3 %collective-permute-done.back_x_ref = f32[9,8,128]{2,1,0:T(8,128)S(1)} collective-permute-done((f32[9,8,128]{2,1,0:T(8,128)}, f32[9,8,128]{2,1,0:T(8,128)S(1)}, u32[]{:S(2)}, u32[]{:S(2)}) %collective-permute-start) | collective-permute-done | bytes 36896 | tf_op jit(solution)/shard_map/ppermute | solution.py:462
  9.0 0.1 broadcast_in_dim.2.mark_ref.refs_0_
  9.1 0.0 copy-done
  9.1 1.6 %shard_map.78 = (f32[15,8,128]{2,1,0:T(8,128)S(1)}, f32[18,8,128]{2,1,0:T(8,128)S(1)}, f32[32,8,128]{2,1,0:T(8,128)}, f32[7,8,128]{2,1,0:T(8,128)S(1)}, f32[7,8,...) custom-call(s32[3,8,128]{2,1,0:T(8,128)S(1)} %broadcast_in_dim.2.mark_ref.refs_0_, ...), custom_call_target="tpu_custom_call" | custom-call | flops 1073741824 | bytes 1048576 | tf_op jit(solution)/shard_map/pallas_call | solution.py:449
  10.7 3.1 %all-to-all-start = ((f32[32,8,128]{2,1,0:T(8,128)}), f32[32,8,128]{2,1,0:T(8,128)S(1)}, u32[]{:S(2)}, u32[]{:S(2)}) async-start(f32[32,8,128]{2,1,0:T(8,128)} %get-tuple-element.48), calls=%async_computation | async-start | bytes 262144 | tf_op jit(solution)/shard_map/all_to_all | solution.py:476
  13.9 2.7 %collective-permute-start.3 = (f32[10,8,128]{2,1,0:T(8,128)S(1)}, f32[10,8,128]{2,1,0:T(8,128)S(1)}, u32[]{:S(2)}, u32[]{:S(2)}) collective-permute-start(f32[10,8,128]{2,1,0:T(8,128)S(1)} %get-tuple-element.80), channel_id=1, source_target_pairs={{0,3},{1,2},{2,1},{3,0},{4,7},{5,6},{6,5},{7,4},{8,11},{9,10},{10,... | collective-permute-start | bytes 122888 | tf_op jit(solution)/shard_map/ppermute | solution.py:471
  16.6 0.6 %collective-permute-start.2 = (f32[10,8,128]{2,1,0:T(8,128)S(1)}, f32[10,8,128]{2,1,0:T(8,128)S(1)}, u32[]{:S(2)}, u32[]{:S(2)}) collective-permute-start(f32[10,8,128]{2,1,0:T(8,128)S(1)} %get-tuple-element.81), channel_id=1, source_target_pairs={{0,1},{1,0},{2,3},{3,2},{4,5},{5,4},{6,7},{7,6},{8,9},{9,8},{10,11... | collective-permute-start | bytes 122888 | tf_op jit(solution)/shard_map/ppermute | solution.py:466
  17.2 0.3 collective-permute-start.4
  17.4 2.5 %collective-permute-start.5 = (f32[7,8,128]{2,1,0:T(8,128)S(1)}, f32[7,8,128]{2,1,0:T(8,128)S(1)}, u32[]{:S(2)}, u32[]{:S(2)}) collective-permute-start(f32[7,8,128]{2,1,0:T(8,128)S(1)} %get-tuple-element.52), channel_id=1, source_target_pairs={{0,28},{4,8},{8,4},{12,16},{16,12},{20,24},{24,20},{28,0},{1,29},{... | collective-permute-start | bytes 86024 | tf_op jit(solution)/shard_map/ppermute | solution.py:471
  20.0 0.0 collective-permute-start.6
  20.0 0.0 collective-permute-done.3
  20.0 0.8 %collective-permute-done.2 = f32[10,8,128]{2,1,0:T(8,128)S(1)} collective-permute-done((f32[10,8,128]{2,1,0:T(8,128)S(1)}, f32[10,8,128]{2,1,0:T(8,128)S(1)}, u32[]{:S(2)}, u32[]{:S(2)}) %collective-permute-start.2) | collective-permute-done | bytes 40992 | tf_op jit(solution)/shard_map/ppermute | solution.py:466
  20.7 0.1 collective-permute-done.4.refs_3_
  20.9 2.1 %shard_map.79.refs_2_ = f32[128,128]{1,0:T(8,128)S(1)} custom-call(s32[3,8,128]{2,1,0:T(8,128)S(1)} %broadcast_in_dim.2.mark_ref.refs_0_, f32[3,8,128]{2,1,0:T(8,128)S(1)} %get-tuple-element.49.refs_0_, f32[3,8,128]{2,1,0:T(8,128)S(1)} %slice.16.refs_1_, f32[3,8,128]{2,1,0:T(8,128)S(1)} %slice.17.refs_2_, f32[3,8,128]{2,1,0:T(8,128)S(1)} %collective-permute-done.4.refs_3_), custom_call_target="tpu_custom_call" | custom-call | flops 536870912 | bytes 1048576 | tf_op jit(solution)/shard_map/pallas_call | solution.py:449
  22.9 0.0 collective-permute-done.5.refs_5_
  23.0 0.0 collective-permute-done.6.refs_6_
  23.0 0.0 all-to-all-done.refs_1_
  23.0 2.2 %shard_map.80 = (f32[15,8,128]{2,1,0:T(8,128)S(1)}, f32[15,8,128]{2,1,0:T(8,128)S(1)}, f32[9,8,128]{2,1,0:T(8,128)S(1)}, f32[9,8,128]{2,1,0:T(8,128)S(1)}, f32[2...) custom-call(s32[3,8,128]{2,1,0:T(8,128)S(1)} %broadcast_in_dim.2.mar, ...), custom_call_target="tpu_custom_call" | custom-call | flops 2147483648 | bytes 1048576 | tf_op jit(solution)/shard_map/pallas_call | solution.py:449
  25.1 4.6 %all-to-all-start.1 = ((f32[32,8,128]{2,1,0:T(8,128)}), f32[32,8,128]{2,1,0:T(8,128)S(1)}, u32[]{:S(2)}, u32[]{:S(2)}) async-start(f32[32,8,128]{2,1,0:T(8,128)} %get-tuple-element.56), calls=%async_computation.1 | async-start | bytes 262144 | tf_op jit(solution)/shard_map/all_to_all | solution.py:476
  29.8 2.7 %collective-permute-start.7 = (f32[3,8,128]{2,1,0:T(8,128)S(1)}, f32[3,8,128]{2,1,0:T(8,128)S(1)}, u32[]{:S(2)}, u32[]{:S(2)}) collective-permute-start(f32[3,8,128]{2,1,0:T(8,128)S(1)} %get-tuple-element.57), channel_id=1, source_target_pairs={{0,3},{1,2},{2,1},{3,0},{4,7},{5,6},{6,5},{7,4},{8,11},{9,10},{10,... | collective-permute-start | bytes 36872 | tf_op jit(solution)/shard_map/ppermute | solution.py:471
  32.5 0.6 %collective-permute-start.8 = (f32[3,8,128]{2,1,0:T(8,128)S(1)}, f32[3,8,128]{2,1,0:T(8,128)S(1)}, u32[]{:S(2)}, u32[]{:S(2)}) collective-permute-start(f32[3,8,128]{2,1,0:T(8,128)S(1)} %get-tuple-element.58), channel_id=1, source_target_pairs={{0,1},{1,0},{2,3},{3,2},{4,5},{5,4},{6,7},{7,6},{8,9},{9,8},{10,11... | collective-permute-start | bytes 36872 | tf_op jit(solution)/shard_map/ppermute | solution.py:466
  33.1 2.5 %collective-permute-start.9 = (f32[3,8,128]{2,1,0:T(8,128)S(1)}, f32[3,8,128]{2,1,0:T(8,128)S(1)}, u32[]{:S(2)}, u32[]{:S(2)}) collective-permute-start(f32[3,8,128]{2,1,0:T(8,128)S(1)} %get-tuple-element.59), channel_id=1, source_target_pairs={{0,28},{4,8},{8,4},{12,16},{16,12},{20,24},{24,20},{28,0},{1,29},{... | collective-permute-start | bytes 36872 | tf_op jit(solution)/shard_map/ppermute | solution.py:471
  35.6 0.0 collective-permute-start.10
  35.6 0.0 collective-permute-done.7.refs_3_
  35.6 0.6 %collective-permute-done.8.refs_4_ = f32[3,8,128]{2,1,0:T(8,128)S(1)} collective-permute-done((f32[3,8,128]{2,1,0:T(8,128)S(1)}, f32[3,8,128]{2,1,0:T(8,128)S(1)}, u32[]{:S(2)}, u32[]{:S(2)}) %collective-permute-start.8) | collective-permute-done | bytes 12320 | tf_op jit(solution)/shard_map/ppermute | solution.py:466
  36.2 1.8 %collective-permute-done.9.refs_5_ = f32[3,8,128]{2,1,0:T(8,128)S(1)} collective-permute-done((f32[3,8,128]{2,1,0:T(8,128)S(1)}, f32[3,8,128]{2,1,0:T(8,128)S(1)}, u32[]{:S(2)}, u32[]{:S(2)}) %collective-permute-start.9) | collective-permute-done | bytes 12320 | tf_op jit(solution)/shard_map/ppermute | solution.py:471
  38.0 0.0 collective-permute-done.10.refs_6_
  38.0 0.2 all-to-all-done.1.refs_1_
  38.2 2.1 %shard_map.81 = (f32[15,8,128]{2,1,0:T(8,128)S(1)}, f32[15,8,128]{2,1,0:T(8,128)S(1)}, f32[9,8,128]{2,1,0:T(8,128)S(1)}, f32[9,8,128]{2,1,0:T(8,128)S(1)}, f32[2...) custom-call(s32[3,8,128]{2,1,0:T(8,128)S(1)} %broadcast_in_dim.2.mar, ...), custom_call_target="tpu_custom_call" | custom-call | flops 2147483648 | bytes 1048576 | tf_op jit(solution)/shard_map/pallas_call | solution.py:449
  40.3 3.6 %all-to-all-start.2 = ((f32[32,8,128]{2,1,0:T(8,128)}), f32[32,8,128]{2,1,0:T(8,128)S(1)}, u32[]{:S(2)}, u32[]{:S(2)}) async-start(f32[32,8,128]{2,1,0:T(8,128)} %get-tuple-element.69), calls=%async_computation.2 | async-start | bytes 262144 | tf_op jit(solution)/shard_map/all_to_all | solution.py:476
  43.9 2.7 %collective-permute-start.11 = (f32[3,8,128]{2,1,0:T(8,128)S(1)}, f32[3,8,128]{2,1,0:T(8,128)S(1)}, u32[]{:S(2)}, u32[]{:S(2)}) collective-permute-start(f32[3,8,128]{2,1,0:T(8,128)S(1)} %get-tuple-element.70), channel_id=1, source_target_pairs={{0,3},{1,0},{2,1},{3,2},{4,7},{5,4},{6,5},{7,6},{8,11},{9,8},{10,9... | collective-permute-start | bytes 36872 | tf_op jit(solution)/shard_map/ppermute | solution.py:462
  46.7 2.8 %collective-permute-start.12 = (f32[3,8,128]{2,1,0:T(8,128)S(1)}, f32[3,8,128]{2,1,0:T(8,128)S(1)}, u32[]{:S(2)}, u32[]{:S(2)}) collective-permute-start(f32[3,8,128]{2,1,0:T(8,128)S(1)} %get-tuple-element.71), channel_id=1, source_target_pairs={{0,28},{4,0},{8,4},{12,8},{16,12},{20,16},{24,20},{28,24},{1,29},{... | collective-permute-start | bytes 36872 | tf_op jit(solution)/shard_map/ppermute | solution.py:462
  49.5 0.0 collective-permute-done.11.refs_3_
  49.5 1.4 %collective-permute-done.12.refs_4_ = f32[3,8,128]{2,1,0:T(8,128)S(1)} collective-permute-done((f32[3,8,128]{2,1,0:T(8,128)S(1)}, f32[3,8,128]{2,1,0:T(8,128)S(1)}, u32[]{:S(2)}, u32[]{:S(2)}) %collective-permute-start.12) | collective-permute-done | bytes 12320 | tf_op jit(solution)/shard_map/ppermute | solution.py:462
  50.9 1.4 %all-to-all-done.2.refs_1_ = f32[32,8,128]{2,1,0:T(8,128)S(1)} async-done(((f32[32,8,128]{2,1,0:T(8,128)}), f32[32,8,128]{2,1,0:T(8,128)S(1)}, u32[]{:S(2)}, u32[]{:S(2)}) %all-to-all-start.2) | async-done | bytes 131104 | tf_op jit(solution)/shard_map/all_to_all | solution.py:476
  52.3 1.1 %shard_map.82 = (f32[9,8,128]{2,1,0:T(8,128)}, f32[9,8,128]{2,1,0:T(8,128)}) custom-call(s32[3,8,128]{2,1,0:T(8,128)S(1)} %broadcast_in_dim.2.mark_ref.refs_0_, f32[32,8,128]{2,1,0:T(8,128)S(1)} %all-to-all-done.2.refs_1_, f32[128,128]{1,0:T(8,128)S(1)} %shard_map.79.refs_2_, f32[3,8,128]{2,1,0:T(8,128)S(1)} %collective-permute-done.11.refs_3_, ...), custom_call_target="tpu_custom_call" | custom-call | flops 1073741824 | bytes 1048576 | tf_op jit(solution)/shard_map/pallas_call | solution.py:449
  (5 shorter events, 0.0 us)
Async XLA Ops:
  0.6 8.5 %copy-start = (f32[1,1,3,8,3,128]{5,3,4,2,1,0:T(8,128)S(1)}, f32[1,1,3,8,3,128]{5,3,4,2,1,0:T(8,128)}, u32[]{:S(2)}) copy-start(f32[1,1,3,8,3,128]{5,3,4,2,1,0:T(8,128)} %param.6) | copy-start | bytes 110596
  0.6 6.1 %collective-permute-start.1 = (f32[9,8,128]{2,1,0:T(8,128)}, f32[9,8,128]{2,1,0:T(8,128)S(1)}, u32[]{:S(2)}, u32[]{:S(2)}) collective-permute-start(f32[9,8,128]{2,1,0:T(8,128)} %bitcast.16), channel_id=1, source_target_pairs={{0,1},{1,2},{2,3},{3,0},{4,5},{5,6},{6,7},{7,4},{8,9},{9,10},{10,1... | collective-permute-start | bytes 110600 | tf_op jit(solution)/shard_map/ppermute | solution.py:462
  3.6 5.4 %collective-permute-start = (f32[9,8,128]{2,1,0:T(8,128)}, f32[9,8,128]{2,1,0:T(8,128)S(1)}, u32[]{:S(2)}, u32[]{:S(2)}) collective-permute-start(f32[9,8,128]{2,1,0:T(8,128)} %bitcast.17), channel_id=1, source_target_pairs={{0,4},{4,8},{8,12},{12,16},{16,20},{20,24},{24,28},{28,0},{1,5},{5... | collective-permute-start | bytes 110600 | tf_op jit(solution)/shard_map/ppermute | solution.py:462
  10.7 12.3 %all-to-all-start = ((f32[32,8,128]{2,1,0:T(8,128)}), f32[32,8,128]{2,1,0:T(8,128)S(1)}, u32[]{:S(2)}, u32[]{:S(2)}) async-start(f32[32,8,128]{2,1,0:T(8,128)} %get-tuple-element.48), calls=%async_computation | async-start | bytes 262144 | tf_op jit(solution)/shard_map/all_to_all | solution.py:476
  13.9 6.1 %collective-permute-start.3 = (f32[10,8,128]{2,1,0:T(8,128)S(1)}, f32[10,8,128]{2,1,0:T(8,128)S(1)}, u32[]{:S(2)}, u32[]{:S(2)}) collective-permute-start(f32[10,8,128]{2,1,0:T(8,128)S(1)} %get-tuple-element.80), channel_id=1, source_target_pairs={{0,3},{1,2},{2,1},{3,0},{4,7},{5,6},{6,5},{7,4},{8,11},{9,10},{10,... | collective-permute-start | bytes 122888 | tf_op jit(solution)/shard_map/ppermute | solution.py:471
  16.6 4.1 %collective-permute-start.2 = (f32[10,8,128]{2,1,0:T(8,128)S(1)}, f32[10,8,128]{2,1,0:T(8,128)S(1)}, u32[]{:S(2)}, u32[]{:S(2)}) collective-permute-start(f32[10,8,128]{2,1,0:T(8,128)S(1)} %get-tuple-element.81), channel_id=1, source_target_pairs={{0,1},{1,0},{2,3},{3,2},{4,5},{5,4},{6,7},{7,6},{8,9},{9,8},{10,11... | collective-permute-start | bytes 122888 | tf_op jit(solution)/shard_map/ppermute | solution.py:466
  17.2 3.7 %collective-permute-start.4 = (f32[3,8,128]{2,1,0:T(8,128)S(1)}, f32[3,8,128]{2,1,0:T(8,128)S(1)}, u32[]{:S(2)}, u32[]{:S(2)}) collective-permute-start(f32[3,8,128]{2,1,0:T(8,128)S(1)} %get-tuple-element.49.refs_0_), channel_id=1, source_target_pairs={{0,2},{1,3},{2,0},{3,1},{4,6},{5,7},{6,4},{7,5},{8,10},{9,11},{10,... | collective-permute-start | bytes 36872 | tf_op jit(solution)/shard_map/ppermute | solution.py:466
  17.4 5.5 %collective-permute-start.5 = (f32[7,8,128]{2,1,0:T(8,128)S(1)}, f32[7,8,128]{2,1,0:T(8,128)S(1)}, u32[]{:S(2)}, u32[]{:S(2)}) collective-permute-start(f32[7,8,128]{2,1,0:T(8,128)S(1)} %get-tuple-element.52), channel_id=1, source_target_pairs={{0,28},{4,8},{8,4},{12,16},{16,12},{20,24},{24,20},{28,0},{1,29},{... | collective-permute-start | bytes 86024 | tf_op jit(solution)/shard_map/ppermute | solution.py:471
  20.0 3.0 %collective-permute-start.6 = (f32[7,8,128]{2,1,0:T(8,128)S(1)}, f32[7,8,128]{2,1,0:T(8,128)S(1)}, u32[]{:S(2)}, u32[]{:S(2)}) collective-permute-start(f32[7,8,128]{2,1,0:T(8,128)S(1)} %get-tuple-element.53), channel_id=1, source_target_pairs={{0,4},{4,0},{8,12},{12,8},{16,20},{20,16},{24,28},{28,24},{1,5},{5... | collective-permute-start | bytes 86024 | tf_op jit(solution)/shard_map/ppermute | solution.py:466
  25.1 13.0 %all-to-all-start.1 = ((f32[32,8,128]{2,1,0:T(8,128)}), f32[32,8,128]{2,1,0:T(8,128)S(1)}, u32[]{:S(2)}, u32[]{:S(2)}) async-start(f32[32,8,128]{2,1,0:T(8,128)} %get-tuple-element.56), calls=%async_computation.1 | async-start | bytes 262144 | tf_op jit(solution)/shard_map/all_to_all | solution.py:476
  29.8 5.8 %collective-permute-start.7 = (f32[3,8,128]{2,1,0:T(8,128)S(1)}, f32[3,8,128]{2,1,0:T(8,128)S(1)}, u32[]{:S(2)}, u32[]{:S(2)}) collective-permute-start(f32[3,8,128]{2,1,0:T(8,128)S(1)} %get-tuple-element.57), channel_id=1, source_target_pairs={{0,3},{1,2},{2,1},{3,0},{4,7},{5,6},{6,5},{7,4},{8,11},{9,10},{10,... | collective-permute-start | bytes 36872 | tf_op jit(solution)/shard_map/ppermute | solution.py:471
  32.5 3.7 %collective-permute-start.8 = (f32[3,8,128]{2,1,0:T(8,128)S(1)}, f32[3,8,128]{2,1,0:T(8,128)S(1)}, u32[]{:S(2)}, u32[]{:S(2)}) collective-permute-start(f32[3,8,128]{2,1,0:T(8,128)S(1)} %get-tuple-element.58), channel_id=1, source_target_pairs={{0,1},{1,0},{2,3},{3,2},{4,5},{5,4},{6,7},{7,6},{8,9},{9,8},{10,11... | collective-permute-start | bytes 36872 | tf_op jit(solution)/shard_map/ppermute | solution.py:466
  33.1 4.9 %collective-permute-start.9 = (f32[3,8,128]{2,1,0:T(8,128)S(1)}, f32[3,8,128]{2,1,0:T(8,128)S(1)}, u32[]{:S(2)}, u32[]{:S(2)}) collective-permute-start(f32[3,8,128]{2,1,0:T(8,128)S(1)} %get-tuple-element.59), channel_id=1, source_target_pairs={{0,28},{4,8},{8,4},{12,16},{16,12},{20,24},{24,20},{28,0},{1,29},{... | collective-permute-start | bytes 36872 | tf_op jit(solution)/shard_map/ppermute | solution.py:471
  35.6 2.4 %collective-permute-start.10 = (f32[3,8,128]{2,1,0:T(8,128)S(1)}, f32[3,8,128]{2,1,0:T(8,128)S(1)}, u32[]{:S(2)}, u32[]{:S(2)}) collective-permute-start(f32[3,8,128]{2,1,0:T(8,128)S(1)} %get-tuple-element.60), channel_id=1, source_target_pairs={{0,4},{4,0},{8,12},{12,8},{16,20},{20,16},{24,28},{28,24},{1,5},{5... | collective-permute-start | bytes 36872 | tf_op jit(solution)/shard_map/ppermute | solution.py:466
  40.3 12.1 %all-to-all-start.2 = ((f32[32,8,128]{2,1,0:T(8,128)}), f32[32,8,128]{2,1,0:T(8,128)S(1)}, u32[]{:S(2)}, u32[]{:S(2)}) async-start(f32[32,8,128]{2,1,0:T(8,128)} %get-tuple-element.69), calls=%async_computation.2 | async-start | bytes 262144 | tf_op jit(solution)/shard_map/all_to_all | solution.py:476
  43.9 5.6 %collective-permute-start.11 = (f32[3,8,128]{2,1,0:T(8,128)S(1)}, f32[3,8,128]{2,1,0:T(8,128)S(1)}, u32[]{:S(2)}, u32[]{:S(2)}) collective-permute-start(f32[3,8,128]{2,1,0:T(8,128)S(1)} %get-tuple-element.70), channel_id=1, source_target_pairs={{0,3},{1,0},{2,1},{3,2},{4,7},{5,4},{6,5},{7,6},{8,11},{9,8},{10,9... | collective-permute-start | bytes 36872 | tf_op jit(solution)/shard_map/ppermute | solution.py:462
  46.7 4.2 %collective-permute-start.12 = (f32[3,8,128]{2,1,0:T(8,128)S(1)}, f32[3,8,128]{2,1,0:T(8,128)S(1)}, u32[]{:S(2)}, u32[]{:S(2)}) collective-permute-start(f32[3,8,128]{2,1,0:T(8,128)S(1)} %get-tuple-element.71), channel_id=1, source_target_pairs={{0,28},{4,0},{8,4},{12,8},{16,12},{20,16},{24,20},{28,24},{1,29},{... | collective-permute-start | bytes 36872 | tf_op jit(solution)/shard_map/ppermute | solution.py:462

commit v6 on v5

--- a/solution.py
+++ b/solution.py
@@ -15,6 +15,8 @@
 SIDES = 6
 BACK_X, AHEAD_X, BACK_Y, AHEAD_Y = range(4)
 PARITY, PLACE = 0, 2
+PACK = 16
+NUMBERS = 3
 
 
 def upper_blocks(size):
@@ -47,6 +49,75 @@
         moved = jnp.take_along_axis(tile, low, axis=1, mode="promise_in_bounds")
         out = moved if out is None else jnp.where(high == number, moved, out)
     return out
+
+
+def bf16_parts(value, count):
+    parts = []
+    for _ in range(count):
+        parts.append(value.astype(jnp.bfloat16))
+        value = value - parts[-1].astype(F32)
+    return jnp.concatenate(parts, axis=0)
+
+
+def pack_sums(nz, terms, numbers):
+    slot = lax.broadcasted_iota(jnp.int32, (terms.shape[1], LANES), 0)
+    lane = lax.broadcasted_iota(jnp.int32, slot.shape, 1)
+    level = lax.shift_right_logical(slot, 3) + lax.bitwise_and(slot, 1)
+    level = jnp.where(level >= nz, level - nz, level)
+    vertex = level * 4 + lax.bitwise_and(lax.shift_right_logical(slot, 1), 3)
+    hot = (lax.bitwise_and(lane, PACK - 1) == vertex) & (slot < nz * CORNERS)
+    wide = jnp.dot(
+        two_parts(terms), jnp.where(hot, 1.0, 0.0).astype(jnp.bfloat16), preferred_element_type=F32
+    )
+    wide = wide[:8] + wide[8:]
+    lane = lane_iota()
+    for at, number in enumerate(numbers):
+        wide = jnp.where(lax.bitwise_and(lane, PACK - 1) == nz * 4 + at, number, wide)
+    sample = lax.broadcasted_iota(jnp.int32, (8, LANES), 0)
+    return jnp.sum(jnp.where(lane // PACK == sample, wide, 0.0), axis=0, keepdims=True)
+
+
+def unpack_sums(sums_ref, spread_ref):
+    lane = lane_iota()
+    place = lax.broadcasted_iota(jnp.int32, (8, LANES), 0) * PACK + lax.bitwise_and(lane, PACK - 1)
+    group = LANES // PACK
+    tiles = []
+    for first in range(0, sums_ref.shape[0], group):
+        tile = jnp.zeros((8, LANES), F32)
+        for at in range(group):
+            row = jnp.broadcast_to(sums_ref[first + at], (8, LANES))
+            row = jnp.take_along_axis(row, place, axis=1, mode="promise_in_bounds")
+            tile = jnp.where(lane // PACK == at, row, tile)
+        tiles.append(tile)
+    parts = bf16_parts(jnp.concatenate(tiles, axis=1), 3)
+    total = jnp.dot(parts, spread_ref[...], preferred_element_type=F32)
+    return total[:8] + (total[8:16] + total[16:])
+
+
+def own_vertices(nz, ncoarse, ids):
+    at = lane_iota() - ncoarse - NUMBERS
+    inside = (at >= 0) & (at < PACK)
+    at = jnp.where(inside, at, 0)
+    slot = jnp.where(at < nz * 4, (at // 4) * CORNERS + lax.bitwise_and(at, 3) * 2, 0)
+    vertex = jnp.take_along_axis(ids, slot, axis=1, mode="promise_in_bounds")
+    vertex = jnp.where(at < nz * 4, vertex, ncoarse + at - nz * 4)
+    vertex = jnp.where(at < nz * 4 + NUMBERS, vertex, -1)
+    return jnp.where(inside, vertex.astype(F32), 0.0)
+
+
+def spread_kernel(ncoarse, sums_ref, spread_ref):
+    lane = lane_iota()
+    lane_square = lax.broadcasted_iota(jnp.int32, (LANES, LANES), 1)
+    place = ncoarse + NUMBERS + lax.bitwise_and(lane, PACK - 1)
+    group = LANES // PACK
+    for first in range(0, sums_ref.shape[0], group):
+        line = jnp.zeros((8, LANES), F32)
+        for at in range(group):
+            row = jnp.take_along_axis(sums_ref[first + at], place, axis=1, mode="promise_in_bounds")
+            line = jnp.where(lane // PACK == at, row, line)
+        column = jnp.broadcast_to(line[0:1].astype(jnp.int32), (LANES, LANES)).T
+        hot = jnp.where(column == lane_square, 1.0, 0.0).astype(jnp.bfloat16)
+        spread_ref[first * PACK : (first + group) * PACK, :] = hot
 
 
 def two_parts(value):
@@ -128,6 +199,16 @@
         copy.wait()
 
 
+def apart(value, slices, size):
+    pieces, at, used = [], 0, 0
+    for rows in slices:
+        pieces += [jnp.zeros((rows.start - at, size), F32), value[used : used + rows.stop - rows.start]]
+        at, used = rows.stop, used + rows.stop - rows.start
+    if at < size:
+        pieces.append(jnp.zeros((size - at, size), F32))
+    return jnp.concatenate(pieces, axis=0)
+
+
 def factor_kernel(count, mark_ref, *refs):
     *blocks, inverse_ref, square = refs
     size = square.shape[0]
@@ -143,46 +224,35 @@
     square[4 * tall * 8 :, :] = jnp.zeros((size - 4 * tall * 8, LANES), F32)
     square[...] = jnp.where(row < count, square[...], jnp.where(row == column, 1.0, 0.0))
     factor = square[...]
-    lane = lane_iota()
-    sub = lax.broadcasted_iota(jnp.int32, (8, LANES), 0)
-    corner = lax.bitwise_and(lane, LANES - 8)
-    tile = jnp.zeros((8, LANES), F32)
-    for at in range(0, size, 8):
-        tile = jnp.where(corner == at, factor[at : at + 8, :], tile)
-    solved = jnp.where(lane - corner == sub, 1.0, 0.0)
-    for q in range(8):
+    least = 16
+    lane = lax.broadcasted_iota(jnp.int32, (least, LANES), 1)
+    sub = lax.broadcasted_iota(jnp.int32, (least, LANES), 0)
+    corner = lax.bitwise_and(lane, LANES - least)
+    tile = jnp.zeros((least, LANES), F32)
+    for at in range(0, size, least):
+        tile = jnp.where(corner == at, factor[at : at + least, :], tile)
+    diagonal = jnp.take_along_axis(tile, corner + sub, axis=1, mode="promise_in_bounds")
+    solved = jnp.where(lane - corner == sub, 1.0 / diagonal, 0.0)
+    tile = tile / diagonal
+    for q in range(least - 1):
         wide = jnp.take_along_axis(tile, corner + q, axis=1, mode="promise_in_bounds")
-        row_q = solved[q : q + 1, :] / wide[q : q + 1, :]
-        solved = jnp.where(sub > q, solved - wide * row_q, jnp.where(sub == q, row_q, solved))
+        solved = jnp.where(sub > q, solved - wide * solved[q : q + 1, :], solved)
     inverse = jnp.concatenate(
-        [jnp.where(corner == at, solved, 0.0) for at in range(0, size, 8)], axis=0
-    )
-    width = 8
+        [jnp.where(corner == at, solved, 0.0) for at in range(0, size, least)], axis=0
+    )
+    width = least
     while width < count:
-        lower = [
-            slice(at, at + width) for at in range(width, size, 2 * width)
-        ]
+        lower = [slice(at, min(at + width, -(-count // 8) * 8)) for at in range(width, count, 2 * width)]
         below = jnp.where(
             (row // (2 * width) == column // (2 * width)) & (row // width > column // width), factor, 0.0
         )
         part = jnp.concatenate([below[rows] for rows in lower], axis=0)
+        left = jnp.concatenate([inverse[rows] for rows in lower], axis=0)
         inner = jnp.dot(part, inverse, precision=lax.Precision.HIGHEST, preferred_element_type=F32)
-        left = jnp.concatenate([inverse[rows] for rows in lower], axis=0)
-        none = jnp.zeros((width, size), F32)
-        spread = []
-        for at in range(len(lower)):
-            spread += [none, inner[at * width : (at + 1) * width]]
         change = jnp.dot(
-            left, jnp.concatenate(spread, axis=0),
-            precision=lax.Precision.HIGHEST, preferred_element_type=F32,
+            left, apart(inner, lower, size), precision=lax.Precision.HIGHEST, preferred_element_type=F32
         )
-        pieces = []
-        for at, rows in enumerate(lower):
-            pieces += [
-                inverse[rows.start - width : rows.start],
-                inverse[rows] - change[at * width : (at + 1) * width],
-            ]
-        inverse = jnp.concatenate(pieces, axis=0)
+        inverse = inverse - apart(change, lower, size)
         width *= 2
     both = lax.dot_general(
         inverse,
@@ -203,7 +273,7 @@
         second[z] = jnp.where(even, down, up)
 
 
-def local_part(nz, ncoarse, residual, image, refs):
+def local_part(nz, ncoarse, residual, image, refs, ids=None):
     (order_ref, matrix_ref, slots_ref, vertex_ref, place_ref, faces_ref, sums_ref) = refs
     own, back = residual
     lane = lane_iota()
@@ -242,16 +312,23 @@
     for z in range(nz):
         both = products[z * 16 : z * 16 + 8] + products[z * 16 + 8 : z * 16 + 16]
         terms = jnp.where(lax.shift_right_logical(slot, 3) == z, both, terms)
-    by_vertex = jnp.dot(two_parts(terms), vertex_ref[...], preferred_element_type=F32)
-    by_vertex = by_vertex[:8] + by_vertex[8:]
-    blocks = vertex_ref.shape[1] // LANES
-    for block in range(blocks):
-        where = lane + block * LANES
-        tile = by_vertex[:, block * LANES : (block + 1) * LANES]
-        for at, number in enumerate(numbers):
-            tile += jnp.where(where == ncoarse + at, number, 0.0)
-        for copy in range(0, sums_ref.shape[0], blocks):
-            sums_ref[copy + block] = tile
+    if sums_ref.shape[1] == 1:
+        row = pack_sums(nz, terms, numbers)
+        for copy in range(sums_ref.shape[0]):
+            sums_ref[copy] = row
+    else:
+        by_vertex = jnp.dot(two_parts(terms), vertex_ref[...], preferred_element_type=F32)
+        by_vertex = by_vertex[:8] + by_vertex[8:]
+        blocks = vertex_ref.shape[1] // LANES
+        for block in range(blocks):
+            where = lane + block * LANES
+            tile = by_vertex[:, block * LANES : (block + 1) * LANES]
+            for at, number in enumerate(numbers):
+                tile += jnp.where(where == ncoarse + at, number, 0.0)
+            if ids is not None:
+                tile += own_vertices(nz, ncoarse, ids)
+            for copy in range(0, sums_ref.shape[0], blocks):
+                sums_ref[copy + block] = tile
     faces = []
     for z in range(nz):
         high, low = order_tiles(place_ref, z)
@@ -263,7 +340,7 @@
 
 
 def start_kernel(
-    nz, ncoarse, mark_ref, rhs_ref, back_x_ref, back_y_ref, order_ref, matrix_ref,
+    packed, nz, ncoarse, mark_ref, rhs_ref, back_x_ref, back_y_ref, order_ref, matrix_ref,
     slots_ref, vertex_ref, place_ref, ids_ref, response_faces_ref,
     residual_ref, faces_ref, sums_ref, x_first, x_second, y_first, y_second,
 ):
@@ -272,7 +349,7 @@
     for at, tile in enumerate(own + back):
         residual_ref[at] = tile
     refs = (order_ref, matrix_ref, slots_ref, vertex_ref, place_ref, faces_ref, sums_ref)
-    faces = local_part(nz, ncoarse, (own, back), None, refs)
+    faces = local_part(nz, ncoarse, (own, back), None, refs, ids_ref[...] if packed else None)
     numbers = ids_ref[...].astype(F32)
     responses = [response_faces_ref[at] for at in range(nz * SIDES)]
     for axis, outs in ((0, (x_first, x_second)), (1, (y_first, y_second))):
@@ -291,6 +368,9 @@
         return taken
 
     mark_ref, sums_ref, inverse_ref = take(3)
+    packed = sums_ref.shape[1] == 1
+    if packed:
+        (spread_ref,) = take(1)
     received = take(2 if last else 4)[::-1]
     faces_ref, response_faces_ref, residual_ref = take(3)
     if first:
@@ -342,9 +422,12 @@
                 near_responses[side, z] = near_ref[side * nz + z]
 
     blocks = inverse_ref.shape[0] // LANES
-    sums = [sums_ref[block] for block in range(blocks)]
-    for copy in range(blocks, sums_ref.shape[0], blocks):
-        sums = [total + sums_ref[copy + block] for block, total in enumerate(sums)]
+    if packed:
+        sums = [unpack_sums(sums_ref, spread_ref)]
+    else:
+        sums = [sums_ref[block] for block in range(blocks)]
+        for copy in range(blocks, sums_ref.shape[0], blocks):
+            sums = [total + sums_ref[copy + block] for block, total in enumerate(sums)]
     coarse = jnp.dot(
         jnp.concatenate(sums, axis=1),
         inverse_ref[...],
@@ -519,7 +602,7 @@
     nz, samples, dirs, face = interface_rhs.shape[2:]
     ncoarse = coarse_factor.shape[1]
     local_size = SIDES * face
-    blocks = -(-(ncoarse + 3) // LANES)
+    blocks = -(-(ncoarse + NUMBERS) // LANES)
     rhs = interface_rhs.transpose(0, 1, 2, 4, 3, 5).reshape(nz * dirs, samples, face)
     order = order.reshape(nz, 1, local_size)
     matrices = inverse_rr.reshape(nz, local_size, local_size)
@@ -534,6 +617,8 @@
     riding = blocks == 1 and lax.axis_size("slab") == 4 and coarse_factor.shape[0] % 8 == 0
     spread = blocks * devices <= 64
     copies = devices if spread else 1
+    packed = spread and riding and devices % (LANES // PACK) == 0
+    packed = packed and nz * 4 + NUMBERS <= PACK and ncoarse + NUMBERS + PACK <= LANES
     tables = nz * SIDES
     rows = coarse_factor.shape[0] // 8 if riding else 1
     part = coarse_factor[: rows * 8, :LANES]
@@ -554,7 +639,7 @@
     )
     own = [order, matrices, slots, vertex, unorder]
     residual, faces, sums, *sends = call(
-        functools.partial(start_kernel, nz, ncoarse),
+        functools.partial(start_kernel, packed, nz, ncoarse),
         [tiles(nz * 5), tiles(tables), tiles(blocks * copies)]
         + [tiles(2 * nz + 1)] * 4,
         [marks, rhs, back_x, back_y] + own + [ids, response_faces],
@@ -581,7 +666,13 @@
             sums, received, factor = exchange(sums, sends, spread, ride)
         if first:
             inverse = invert(factor)
-        operands = [marks, sums, inverse] + received[::-1] + [faces, response_faces] + state
+        if first and packed:
+            wide = jax.ShapeDtypeStruct((devices * PACK, LANES), jnp.bfloat16)
+            scatter = call(
+                functools.partial(spread_kernel, ncoarse), [wide], [sums], pltpu.VMEM, 2**26
+            )
+        rows_at = list(scatter) if packed and not first else []
+        operands = [marks, sums, inverse] + rows_at + received[::-1] + [faces, response_faces] + state
         kernel = functools.partial(step_kernel, first, last, nz, ncoarse)
         if last:
             outs = [tiles(nz * 3)] * 2
@@ -589,7 +680,7 @@
             break
         outs = [tiles(nz * 5), tiles(nz * 5), tiles(nz * 3), tiles(nz * 3), tiles(2)]
         sides = 2 if iteration == ITERS - 2 else 4
-        outs += [tiles(tables), tiles(blocks * copies)]
+        outs += [tiles(tables), jax.ShapeDtypeStruct((copies, 1, LANES), F32) if packed else tiles(blocks * copies)]
         outs += [tiles(nz)] * sides
         if first:
             outs += [jax.ShapeDtypeStruct((8, LANES), jnp.int32), tiles(nz * 4)]

time: 53.8 us -> 52.8 us (0.981)
  waiting for transfers between devices: 9.45 us -> 5.52 us
  starting transfers between devices: 31.9 us -> 34.8 us
    all_to_all x3, starting transfers between devices: 11.4 us -> 13.9 us  [summed(): return lax.all_to_all(sums, ('sub', 'slab'), 0, 0, tiled=True)]
    ppermute x4, waiting for transfers between devices: 4.57 us -> 2.53 us  [shifted(): lax.ppermute(value, axis, [(i, (i + steps) % count) for i in range(count)])]
    all_to_all x3, waiting for transfers between devices: 1.6 us -> 0.14 us  [summed(): return lax.all_to_all(sums, ('sub', 'slab'), 0, 0, tiled=True)]
    pallas_call x6 -> x7, Pallas kernels: 11.2 us -> 11.4 us  [call(): pl.pallas_call(kernel, out_shape=outs, in_specs=specs, out_specs=[vmem] *...]
  transfers between devices with their start and end apart: 16 -> 16, of which waited for: 9 -> 7; matrix products, arithmetic and copies ran while one was open for 0% -> 0% of each run, Pallas kernels for 8% -> 8%
where the time goes in v6:
time: 52.8 us; the launch traced here: 52.6 us
  starting transfers between devices  34.8 us (66%)
  Pallas kernels  11.4 us (22%)
  waiting for transfers between devices  5.52 us (10%)
  between operations  0.74 us (1%)
    all_to_all x3, starting transfers between devices, summed(): return lax.all_to_all(sums, ('sub', 'slab'), 0, 0, tiled=True)  13.9 us
    pallas_call x7, Pallas kernels, call(): pl.pallas_call(kernel, out_shape=outs, in_specs=specs, out_specs=[vmem] *...  11.4 us
    ppermute x4, starting transfers between devices, paired_other(): lax.ppermute(value, axis, [(i, (i + 1 if i % 2 else i - 1) % count) for i...  10.6 us
    ppermute x4, starting transfers between devices, shifted(): lax.ppermute(value, axis, [(i, (i + steps) % count) for i in range(count)])  8.61 us
    ppermute x4, waiting for transfers between devices, shifted(): lax.ppermute(value, axis, [(i, (i + steps) % count) for i in range(count)])  2.53 us
    ppermute x4, waiting for transfers between devices, paired_other(): lax.ppermute(value, axis, [(i, (i + 1 if i % 2 else i - 1) % count) for i...  1.84 us
    ppermute x5, starting transfers between devices, paired(): lax.ppermute(value, axis, [(i, i ^ mask) for i in range(lax.axis_size(axi...  1.7 us
  transfers between devices with their start and end apart: 16, of which 7 were waited for; matrix products, arithmetic and copies ran while one was open for 0% of the time, Pallas kernels for 8%

profile of v6, /device:TPU:0, one launch (start us, length us, event | category | flops | bytes accessed | tf_op | source)
XLA Modules:
  0.0 52.6 jit_solution(15401918024731059639)
XLA Ops:
  0.6 0.0 copy-start
  0.6 0.5 collective-permute-start
  1.1 2.6 %collective-permute-start.1 = (f32[9,8,128]{2,1,0:T(8,128)}, f32[9,8,128]{2,1,0:T(8,128)S(1)}, u32[]{:S(2)}, u32[]{:S(2)}) collective-permute-start(f32[9,8,128]{2,1,0:T(8,128)} %bitcast.17), channel_id=1, source_target_pairs={{0,1},{1,2},{2,3},{3,0},{4,5},{5,6},{6,7},{7,4},{8,9},{9,10},{10,1... | collective-permute-start | bytes 110600 | tf_op jit(solution)/shard_map/ppermute | solution.py:545
  3.7 0.1 pad_add_fusion
  3.8 2.1 %shard_map.77 = (s32[3,1,768]{2,1,0:T(1,128)S(1)}, bf16[32,768]{1,0:T(8,128)(2,1)S(1)}, bf16[32,128]{1,0:T(8,128)(2,1)S(1)}, s32[8,128]{1,0:T(8,128)S(1)}, bf16[...) custom-call(s32[3,1,768]{2,1,0:T(1,128)} %bitcast.21, ...), custom_call_target="tpu_custom_call" | custom-call | flops 1073741824 | bytes 1048576 | tf_op jit(solution)/shard_map/pallas_call | solution.py:532
  5.9 1.1 %collective-permute-done.back_x_ref = f32[9,8,128]{2,1,0:T(8,128)S(1)} collective-permute-done((f32[9,8,128]{2,1,0:T(8,128)}, f32[9,8,128]{2,1,0:T(8,128)S(1)}, u32[]{:S(2)}, u32[]{:S(2)}) %collective-permute-start) | collective-permute-done | bytes 36896 | tf_op jit(solution)/shard_map/ppermute | solution.py:545
  7.0 0.0 collective-permute-done.1.back_y_ref
  7.0 0.1 broadcast_in_dim.2.mark_ref.refs_0_
  7.1 0.0 copy-done
  7.1 1.6 %shard_map.78 = (f32[15,8,128]{2,1,0:T(8,128)S(1)}, f32[18,8,128]{2,1,0:T(8,128)S(1)}, f32[32,8,128]{2,1,0:T(8,128)}, f32[7,8,128]{2,1,0:T(8,128)S(1)}, f32[7,8,...) custom-call(s32[3,8,128]{2,1,0:T(8,128)S(1)} %broadcast_in_dim.2.mark_ref.refs_0_, ...), custom_call_target="tpu_custom_call" | custom-call | flops 1073741824 | bytes 1048576 | tf_op jit(solution)/shard_map/pallas_call | solution.py:532
  8.7 5.2 %all-to-all-start = ((f32[32,8,128]{2,1,0:T(8,128)}), f32[32,8,128]{2,1,0:T(8,128)S(1)}, u32[]{:S(2)}, u32[]{:S(2)}) async-start(f32[32,8,128]{2,1,0:T(8,128)} %get-tuple-element.48), calls=%async_computation | async-start | bytes 262144 | tf_op jit(solution)/shard_map/all_to_all | solution.py:559
  13.9 2.7 %collective-permute-start.3 = (f32[10,8,128]{2,1,0:T(8,128)S(1)}, f32[10,8,128]{2,1,0:T(8,128)S(1)}, u32[]{:S(2)}, u32[]{:S(2)}) collective-permute-start(f32[10,8,128]{2,1,0:T(8,128)S(1)} %get-tuple-element.80), channel_id=1, source_target_pairs={{0,3},{1,2},{2,1},{3,0},{4,7},{5,6},{6,5},{7,4},{8,11},{9,10},{10,... | collective-permute-start | bytes 122888 | tf_op jit(solution)/shard_map/ppermute | solution.py:554
  16.7 0.6 %collective-permute-start.2 = (f32[10,8,128]{2,1,0:T(8,128)S(1)}, f32[10,8,128]{2,1,0:T(8,128)S(1)}, u32[]{:S(2)}, u32[]{:S(2)}) collective-permute-start(f32[10,8,128]{2,1,0:T(8,128)S(1)} %get-tuple-element.81), channel_id=1, source_target_pairs={{0,1},{1,0},{2,3},{3,2},{4,5},{5,4},{6,7},{7,6},{8,9},{9,8},{10,11... | collective-permute-start | bytes 122888 | tf_op jit(solution)/shard_map/ppermute | solution.py:549
  17.2 0.3 collective-permute-start.4
  17.5 2.5 %collective-permute-start.5 = (f32[7,8,128]{2,1,0:T(8,128)S(1)}, f32[7,8,128]{2,1,0:T(8,128)S(1)}, u32[]{:S(2)}, u32[]{:S(2)}) collective-permute-start(f32[7,8,128]{2,1,0:T(8,128)S(1)} %get-tuple-element.52), channel_id=1, source_target_pairs={{0,28},{4,8},{8,4},{12,16},{16,12},{20,24},{24,20},{28,0},{1,29},{... | collective-permute-start | bytes 86024 | tf_op jit(solution)/shard_map/ppermute | solution.py:554
  20.0 0.0 collective-permute-start.6
  20.0 0.0 collective-permute-done.3
  20.0 0.8 %collective-permute-done.2 = f32[10,8,128]{2,1,0:T(8,128)S(1)} collective-permute-done((f32[10,8,128]{2,1,0:T(8,128)S(1)}, f32[10,8,128]{2,1,0:T(8,128)S(1)}, u32[]{:S(2)}, u32[]{:S(2)}) %collective-permute-start.2) | collective-permute-done | bytes 40992 | tf_op jit(solution)/shard_map/ppermute | solution.py:549
  20.8 0.1 collective-permute-done.4.refs_3_
  20.9 1.6 %shard_map.79.refs_2_ = f32[128,128]{1,0:T(8,128)S(1)} custom-call(s32[3,8,128]{2,1,0:T(8,128)S(1)} %broadcast_in_dim.2.mark_ref.refs_0_, f32[3,8,128]{2,1,0:T(8,128)S(1)} %get-tuple-element.49.refs_0_, f32[3,8,128]{2,1,0:T(8,128)S(1)} %slice.16.refs_1_, f32[3,8,128]{2,1,0:T(8,128)S(1)} %slice.17.refs_2_, f32[3,8,128]{2,1,0:T(8,128)S(1)} %collective-permute-done.4.refs_3_), custom_call_target="tpu_custom_call" | custom-call | flops 536870912 | bytes 1048576 | tf_op jit(solution)/shard_map/pallas_call | solution.py:532
  22.6 0.0 collective-permute-done.5.refs_5_
  22.6 0.0 collective-permute-done.6.refs_6_
  22.6 0.0 all-to-all-done.refs_1_.sums_ref
  22.6 2.1 %shard_map.80 = (f32[15,8,128]{2,1,0:T(8,128)S(1)}, f32[15,8,128]{2,1,0:T(8,128)S(1)}, f32[9,8,128]{2,1,0:T(8,128)S(1)}, f32[9,8,128]{2,1,0:T(8,128)S(1)}, f32[2...) custom-call(s32[3,8,128]{2,1,0:T(8,128)S(1)} %broadcast_in_dim.2.mar, ...), custom_call_target="tpu_custom_call" | custom-call | flops 2147483648 | bytes 1048576 | tf_op jit(solution)/shard_map/pallas_call | solution.py:532
  24.7 4.7 %all-to-all-start.1 = ((f32[32,1,128]{2,1,0:T(1,128)}), f32[32,1,128]{2,1,0:T(1,128)S(1)}, u32[]{:S(2)}, u32[]{:S(2)}) async-start(f32[32,1,128]{2,1,0:T(1,128)} %get-tuple-element.56), calls=%async_computation.1 | async-start | bytes 32768 | tf_op jit(solution)/shard_map/all_to_all | solution.py:559
  29.5 0.3 collective-permute-start.10
  29.8 2.6 %collective-permute-start.7 = (f32[3,8,128]{2,1,0:T(8,128)S(1)}, f32[3,8,128]{2,1,0:T(8,128)S(1)}, u32[]{:S(2)}, u32[]{:S(2)}) collective-permute-start(f32[3,8,128]{2,1,0:T(8,128)S(1)} %get-tuple-element.57), channel_id=1, source_target_pairs={{0,3},{1,2},{2,1},{3,0},{4,7},{5,6},{6,5},{7,4},{8,11},{9,10},{10,... | collective-permute-start | bytes 36872 | tf_op jit(solution)/shard_map/ppermute | solution.py:554
  32.4 0.6 %collective-permute-start.8 = (f32[3,8,128]{2,1,0:T(8,128)S(1)}, f32[3,8,128]{2,1,0:T(8,128)S(1)}, u32[]{:S(2)}, u32[]{:S(2)}) collective-permute-start(f32[3,8,128]{2,1,0:T(8,128)S(1)} %get-tuple-element.58), channel_id=1, source_target_pairs={{0,1},{1,0},{2,3},{3,2},{4,5},{5,4},{6,7},{7,6},{8,9},{9,8},{10,11... | collective-permute-start | bytes 36872 | tf_op jit(solution)/shard_map/ppermute | solution.py:549
  32.9 2.7 %collective-permute-start.9 = (f32[3,8,128]{2,1,0:T(8,128)S(1)}, f32[3,8,128]{2,1,0:T(8,128)S(1)}, u32[]{:S(2)}, u32[]{:S(2)}) collective-permute-start(f32[3,8,128]{2,1,0:T(8,128)S(1)} %get-tuple-element.59), channel_id=1, source_target_pairs={{0,28},{4,8},{8,4},{12,16},{16,12},{20,24},{24,20},{28,0},{1,29},{... | collective-permute-start | bytes 36872 | tf_op jit(solution)/shard_map/ppermute | solution.py:554
  35.7 0.2 shard_map.81.refs_3_
  35.9 0.0 collective-permute-done.10.refs_7_
  35.9 0.0 collective-permute-done.7.refs_4_
  35.9 0.1 collective-permute-done.8.refs_5_
  36.0 1.8 %collective-permute-done.9.refs_6_ = f32[3,8,128]{2,1,0:T(8,128)S(1)} collective-permute-done((f32[3,8,128]{2,1,0:T(8,128)S(1)}, f32[3,8,128]{2,1,0:T(8,128)S(1)}, u32[]{:S(2)}, u32[]{:S(2)}) %collective-permute-start.9) | collective-permute-done | bytes 12320 | tf_op jit(solution)/shard_map/ppermute | solution.py:554
  37.9 0.0 all-to-all-done.1.refs_1_
  37.9 2.3 %shard_map.82 = (f32[15,8,128]{2,1,0:T(8,128)S(1)}, f32[15,8,128]{2,1,0:T(8,128)S(1)}, f32[9,8,128]{2,1,0:T(8,128)S(1)}, f32[9,8,128]{2,1,0:T(8,128)S(1)}, f32[2...) custom-call(s32[3,8,128]{2,1,0:T(8,128)S(1)} %broadcast_in_dim.2.mar, ...), custom_call_target="tpu_custom_call" | custom-call | flops 2147483648 | bytes 1048576 | tf_op jit(solution)/shard_map/pallas_call | solution.py:532
  40.2 4.0 %all-to-all-start.2 = ((f32[32,1,128]{2,1,0:T(1,128)}), f32[32,1,128]{2,1,0:T(1,128)S(1)}, u32[]{:S(2)}, u32[]{:S(2)}) async-start(f32[32,1,128]{2,1,0:T(1,128)} %get-tuple-element.69), calls=%async_computation.2 | async-start | bytes 32768 | tf_op jit(solution)/shard_map/all_to_all | solution.py:559
  44.2 2.7 %collective-permute-start.11 = (f32[3,8,128]{2,1,0:T(8,128)S(1)}, f32[3,8,128]{2,1,0:T(8,128)S(1)}, u32[]{:S(2)}, u32[]{:S(2)}) collective-permute-start(f32[3,8,128]{2,1,0:T(8,128)S(1)} %get-tuple-element.70), channel_id=1, source_target_pairs={{0,3},{1,0},{2,1},{3,2},{4,7},{5,4},{6,5},{7,6},{8,11},{9,8},{10,9... | collective-permute-start | bytes 36872 | tf_op jit(solution)/shard_map/ppermute | solution.py:545
  46.9 2.8 %collective-permute-start.12 = (f32[3,8,128]{2,1,0:T(8,128)S(1)}, f32[3,8,128]{2,1,0:T(8,128)S(1)}, u32[]{:S(2)}, u32[]{:S(2)}) collective-permute-start(f32[3,8,128]{2,1,0:T(8,128)S(1)} %get-tuple-element.71), channel_id=1, source_target_pairs={{0,28},{4,0},{8,4},{12,8},{16,12},{20,16},{24,20},{28,24},{1,29},{... | collective-permute-start | bytes 36872 | tf_op jit(solution)/shard_map/ppermute | solution.py:545
  49.7 0.0 collective-permute-done.11.refs_4_
  49.7 1.4 %collective-permute-done.12.refs_5_ = f32[3,8,128]{2,1,0:T(8,128)S(1)} collective-permute-done((f32[3,8,128]{2,1,0:T(8,128)S(1)}, f32[3,8,128]{2,1,0:T(8,128)S(1)}, u32[]{:S(2)}, u32[]{:S(2)}) %collective-permute-start.12) | collective-permute-done | bytes 12320 | tf_op jit(solution)/shard_map/ppermute | solution.py:545
  51.1 0.1 all-to-all-done.2.refs_1_
  51.3 1.3 %shard_map.83 = (f32[9,8,128]{2,1,0:T(8,128)}, f32[9,8,128]{2,1,0:T(8,128)}) custom-call(s32[3,8,128]{2,1,0:T(8,128)S(1)} %broadcast_in_dim.2.mark_ref.refs_0_, f32[32,1,128]{2,1,0:T(1,128)S(1)} %all-to-all-done.2.refs_1_, f32[128,128]{1,0:T(8,128)S(1)} %shard_map.79.refs_2_, bf16[512,128]{1,0:T(8,128)(2,1)S(1)} %shard_map.81.refs_3_, ...), custom_call_target="tpu_custom_call" | custom-call | flops 1073741824 | bytes 1048576 | tf_op jit(solution)/shard_map/pallas_call | solution.py:532
  (5 shorter events, 0.0 us)
Async XLA Ops:
  0.6 6.5 %copy-start = (f32[1,1,3,8,3,128]{5,3,4,2,1,0:T(8,128)S(1)}, f32[1,1,3,8,3,128]{5,3,4,2,1,0:T(8,128)}, u32[]{:S(2)}) copy-start(f32[1,1,3,8,3,128]{5,3,4,2,1,0:T(8,128)} %param.6) | copy-start | bytes 110596
  0.6 6.4 %collective-permute-start = (f32[9,8,128]{2,1,0:T(8,128)}, f32[9,8,128]{2,1,0:T(8,128)S(1)}, u32[]{:S(2)}, u32[]{:S(2)}) collective-permute-start(f32[9,8,128]{2,1,0:T(8,128)} %bitcast.16), channel_id=1, source_target_pairs={{0,4},{4,8},{8,12},{12,16},{16,20},{20,24},{24,28},{28,0},{1,5},{5... | collective-permute-start | bytes 110600 | tf_op jit(solution)/shard_map/ppermute | solution.py:545
  1.1 5.9 %collective-permute-start.1 = (f32[9,8,128]{2,1,0:T(8,128)}, f32[9,8,128]{2,1,0:T(8,128)S(1)}, u32[]{:S(2)}, u32[]{:S(2)}) collective-permute-start(f32[9,8,128]{2,1,0:T(8,128)} %bitcast.17), channel_id=1, source_target_pairs={{0,1},{1,2},{2,3},{3,0},{4,5},{5,6},{6,7},{7,4},{8,9},{9,10},{10,1... | collective-permute-start | bytes 110600 | tf_op jit(solution)/shard_map/ppermute | solution.py:545
  8.7 13.9 %all-to-all-start = ((f32[32,8,128]{2,1,0:T(8,128)}), f32[32,8,128]{2,1,0:T(8,128)S(1)}, u32[]{:S(2)}, u32[]{:S(2)}) async-start(f32[32,8,128]{2,1,0:T(8,128)} %get-tuple-element.48), calls=%async_computation | async-start | bytes 262144 | tf_op jit(solution)/shard_map/all_to_all | solution.py:559
  13.9 6.1 %collective-permute-start.3 = (f32[10,8,128]{2,1,0:T(8,128)S(1)}, f32[10,8,128]{2,1,0:T(8,128)S(1)}, u32[]{:S(2)}, u32[]{:S(2)}) collective-permute-start(f32[10,8,128]{2,1,0:T(8,128)S(1)} %get-tuple-element.80), channel_id=1, source_target_pairs={{0,3},{1,2},{2,1},{3,0},{4,7},{5,6},{6,5},{7,4},{8,11},{9,10},{10,... | collective-permute-start | bytes 122888 | tf_op jit(solution)/shard_map/ppermute | solution.py:554
  16.7 4.1 %collective-permute-start.2 = (f32[10,8,128]{2,1,0:T(8,128)S(1)}, f32[10,8,128]{2,1,0:T(8,128)S(1)}, u32[]{:S(2)}, u32[]{:S(2)}) collective-permute-start(f32[10,8,128]{2,1,0:T(8,128)S(1)} %get-tuple-element.81), channel_id=1, source_target_pairs={{0,1},{1,0},{2,3},{3,2},{4,5},{5,4},{6,7},{7,6},{8,9},{9,8},{10,11... | collective-permute-start | bytes 122888 | tf_op jit(solution)/shard_map/ppermute | solution.py:549
  17.2 3.7 %collective-permute-start.4 = (f32[3,8,128]{2,1,0:T(8,128)S(1)}, f32[3,8,128]{2,1,0:T(8,128)S(1)}, u32[]{:S(2)}, u32[]{:S(2)}) collective-permute-start(f32[3,8,128]{2,1,0:T(8,128)S(1)} %get-tuple-element.49.refs_0_), channel_id=1, source_target_pairs={{0,2},{1,3},{2,0},{3,1},{4,6},{5,7},{6,4},{7,5},{8,10},{9,11},{10,... | collective-permute-start | bytes 36872 | tf_op jit(solution)/shard_map/ppermute | solution.py:549
  17.5 5.1 %collective-permute-start.5 = (f32[7,8,128]{2,1,0:T(8,128)S(1)}, f32[7,8,128]{2,1,0:T(8,128)S(1)}, u32[]{:S(2)}, u32[]{:S(2)}) collective-permute-start(f32[7,8,128]{2,1,0:T(8,128)S(1)} %get-tuple-element.52), channel_id=1, source_target_pairs={{0,28},{4,8},{8,4},{12,16},{16,12},{20,24},{24,20},{28,0},{1,29},{... | collective-permute-start | bytes 86024 | tf_op jit(solution)/shard_map/ppermute | solution.py:554
  20.0 2.6 %collective-permute-start.6 = (f32[7,8,128]{2,1,0:T(8,128)S(1)}, f32[7,8,128]{2,1,0:T(8,128)S(1)}, u32[]{:S(2)}, u32[]{:S(2)}) collective-permute-start(f32[7,8,128]{2,1,0:T(8,128)S(1)} %get-tuple-element.53), channel_id=1, source_target_pairs={{0,4},{4,0},{8,12},{12,8},{16,20},{20,16},{24,28},{28,24},{1,5},{5... | collective-permute-start | bytes 86024 | tf_op jit(solution)/shard_map/ppermute | solution.py:549
  24.7 13.1 %all-to-all-start.1 = ((f32[32,1,128]{2,1,0:T(1,128)}), f32[32,1,128]{2,1,0:T(1,128)S(1)}, u32[]{:S(2)}, u32[]{:S(2)}) async-start(f32[32,1,128]{2,1,0:T(1,128)} %get-tuple-element.56), calls=%async_computation.1 | async-start | bytes 32768 | tf_op jit(solution)/shard_map/all_to_all | solution.py:559
  29.5 6.4 %collective-permute-start.10 = (f32[3,8,128]{2,1,0:T(8,128)S(1)}, f32[3,8,128]{2,1,0:T(8,128)S(1)}, u32[]{:S(2)}, u32[]{:S(2)}) collective-permute-start(f32[3,8,128]{2,1,0:T(8,128)S(1)} %get-tuple-element.60), channel_id=1, source_target_pairs={{0,4},{4,0},{8,12},{12,8},{16,20},{20,16},{24,28},{28,24},{1,5},{5... | collective-permute-start | bytes 36872 | tf_op jit(solution)/shard_map/ppermute | solution.py:549
  29.8 6.1 %collective-permute-start.7 = (f32[3,8,128]{2,1,0:T(8,128)S(1)}, f32[3,8,128]{2,1,0:T(8,128)S(1)}, u32[]{:S(2)}, u32[]{:S(2)}) collective-permute-start(f32[3,8,128]{2,1,0:T(8,128)S(1)} %get-tuple-element.57), channel_id=1, source_target_pairs={{0,3},{1,2},{2,1},{3,0},{4,7},{5,6},{6,5},{7,4},{8,11},{9,10},{10,... | collective-permute-start | bytes 36872 | tf_op jit(solution)/shard_map/ppermute | solution.py:554
  32.4 3.7 %collective-permute-start.8 = (f32[3,8,128]{2,1,0:T(8,128)S(1)}, f32[3,8,128]{2,1,0:T(8,128)S(1)}, u32[]{:S(2)}, u32[]{:S(2)}) collective-permute-start(f32[3,8,128]{2,1,0:T(8,128)S(1)} %get-tuple-element.58), channel_id=1, source_target_pairs={{0,1},{1,0},{2,3},{3,2},{4,5},{5,4},{6,7},{7,6},{8,9},{9,8},{10,11... | collective-permute-start | bytes 36872 | tf_op jit(solution)/shard_map/ppermute | solution.py:549
  32.9 4.9 %collective-permute-start.9 = (f32[3,8,128]{2,1,0:T(8,128)S(1)}, f32[3,8,128]{2,1,0:T(8,128)S(1)}, u32[]{:S(2)}, u32[]{:S(2)}) collective-permute-start(f32[3,8,128]{2,1,0:T(8,128)S(1)} %get-tuple-element.59), channel_id=1, source_target_pairs={{0,28},{4,8},{8,4},{12,16},{16,12},{20,24},{24,20},{28,0},{1,29},{... | collective-permute-start | bytes 36872 | tf_op jit(solution)/shard_map/ppermute | solution.py:554
  40.2 11.1 %all-to-all-start.2 = ((f32[32,1,128]{2,1,0:T(1,128)}), f32[32,1,128]{2,1,0:T(1,128)S(1)}, u32[]{:S(2)}, u32[]{:S(2)}) async-start(f32[32,1,128]{2,1,0:T(1,128)} %get-tuple-element.69), calls=%async_computation.2 | async-start | bytes 32768 | tf_op jit(solution)/shard_map/all_to_all | solution.py:559
  44.2 5.6 %collective-permute-start.11 = (f32[3,8,128]{2,1,0:T(8,128)S(1)}, f32[3,8,128]{2,1,0:T(8,128)S(1)}, u32[]{:S(2)}, u32[]{:S(2)}) collective-permute-start(f32[3,8,128]{2,1,0:T(8,128)S(1)} %get-tuple-element.70), channel_id=1, source_target_pairs={{0,3},{1,0},{2,1},{3,2},{4,7},{5,4},{6,5},{7,6},{8,11},{9,8},{10,9... | collective-permute-start | bytes 36872 | tf_op jit(solution)/shard_map/ppermute | solution.py:545
  46.9 4.2 %collective-permute-start.12 = (f32[3,8,128]{2,1,0:T(8,128)S(1)}, f32[3,8,128]{2,1,0:T(8,128)S(1)}, u32[]{:S(2)}, u32[]{:S(2)}) collective-permute-start(f32[3,8,128]{2,1,0:T(8,128)S(1)} %get-tuple-element.71), channel_id=1, source_target_pairs={{0,28},{4,0},{8,4},{12,8},{16,12},{20,16},{24,20},{28,24},{1,29},{... | collective-permute-start | bytes 36872 | tf_op jit(solution)/shard_map/ppermute | solution.py:545

commit v7 on v6

--- a/solution.py
+++ b/solution.py
@@ -139,8 +139,32 @@
     return high, low
 
 
+def invert_own_block(rows_ref, place):
+    count = rows_ref.shape[0]
+    tall = count * 8
+    rows = jnp.concatenate([rows_ref[at] for at in range(count)], axis=0)
+    lane = lax.broadcasted_iota(jnp.int32, (tall, LANES), 1)
+    sub = lax.broadcasted_iota(jnp.int32, (tall, LANES), 0)
+    start = jnp.broadcast_to(place, (tall, LANES)) * tall
+    block = jnp.take_along_axis(
+        rows, jnp.minimum(start + lane, LANES - 1), axis=1, mode="promise_in_bounds"
+    )
+    diagonal = jnp.take_along_axis(block, sub, axis=1, mode="promise_in_bounds")
+    solved = jnp.where(lane == sub, 1.0 / diagonal, 0.0)
+    block = block / diagonal
+    for q in range(tall - 1):
+        solved = jnp.where(sub > q, solved - block[:, q : q + 1] * solved[q : q + 1, :], solved)
+    inside = (lane >= start) & (lane < start + tall)
+    moved = jnp.take_along_axis(
+        solved, jnp.where(inside, lane - start, 0), axis=1, mode="promise_in_bounds"
+    )
+    rows = jnp.where(inside, moved, rows)
+    for at in range(count):
+        rows_ref[at] = rows[at * 8 : (at + 1) * 8, :]
+
+
 def prepare_kernel(
-    nz, order_hbm, response_hbm, factor_hbm, corners_hbm, matrix_hbm,
+    nz, riding, order_hbm, response_hbm, factor_hbm, corners_hbm, matrix_hbm, mark_ref,
     order_ref, slots_ref, vertex_ref, ids_ref, matrix_ref, place_ref, faces_ref, rows_ref,
     response_ref, factor_ref, corners_ref, done,
 ):
@@ -159,6 +183,8 @@
     rows_ref[...] = jnp.zeros_like(rows_ref)
     for at in range(rows_ref.shape[0]):
         rows_ref[at, :, 0 : factor_ref.shape[1]] = factor_ref[at * 8 : (at + 1) * 8, :]
+    if riding:
+        invert_own_block(rows_ref, mark_ref[PLACE, 0:1, :])
     response = response_ref[...].astype(F32)
     lane = lane_iota()
     lane_square = lax.broadcasted_iota(jnp.int32, (LANES, LANES), 1)
@@ -224,23 +250,8 @@
     square[4 * tall * 8 :, :] = jnp.zeros((size - 4 * tall * 8, LANES), F32)
     square[...] = jnp.where(row < count, square[...], jnp.where(row == column, 1.0, 0.0))
     factor = square[...]
-    least = 16
-    lane = lax.broadcasted_iota(jnp.int32, (least, LANES), 1)
-    sub = lax.broadcasted_iota(jnp.int32, (least, LANES), 0)
-    corner = lax.bitwise_and(lane, LANES - least)
-    tile = jnp.zeros((least, LANES), F32)
-    for at in range(0, size, least):
-        tile = jnp.where(corner == at, factor[at : at + least, :], tile)
-    diagonal = jnp.take_along_axis(tile, corner + sub, axis=1, mode="promise_in_bounds")
-    solved = jnp.where(lane - corner == sub, 1.0 / diagonal, 0.0)
-    tile = tile / diagonal
-    for q in range(least - 1):
-        wide = jnp.take_along_axis(tile, corner + q, axis=1, mode="promise_in_bounds")
-        solved = jnp.where(sub > q, solved - wide * solved[q : q + 1, :], solved)
-    inverse = jnp.concatenate(
-        [jnp.where(corner == at, solved, 0.0) for at in range(0, size, least)], axis=0
-    )
-    width = least
+    width = count // 4
+    inverse = jnp.where(row // width == column // width, factor, 0.0)
     while width < count:
         lower = [slice(at, min(at + width, -(-count // 8) * 8)) for at in range(width, count, 2 * width)]
         below = jnp.where(
@@ -359,6 +370,12 @@
             out[2 * nz] = numbers
 
 
+def start_order(first, last):
+    if last:
+        return (0, 1)
+    return (3, 2, 1, 0) if first else (1, 3, 0, 2)
+
+
 def step_kernel(first, last, nz, ncoarse, *refs):
     refs = list(refs)
 
@@ -371,7 +388,8 @@
     packed = sums_ref.shape[1] == 1
     if packed:
         (spread_ref,) = take(1)
-    received = take(2 if last else 4)[::-1]
+    order = start_order(first, last)
+    received = [got for _, got in sorted(zip(order, take(len(order))), key=lambda pair: pair[0])]
     faces_ref, response_faces_ref, residual_ref = take(3)
     if first:
         (ids_ref,) = take(1)
@@ -626,11 +644,11 @@
     kept = jax.ShapeDtypeStruct((kept, WIDE, WIDE), matrices.dtype)
     slots = -(-nz * CORNERS // 16) * 16
     order, slots, vertex, ids, matrices, unorder, response_faces, rows = call(
-        functools.partial(prepare_kernel, nz),
+        functools.partial(prepare_kernel, nz, riding),
         [like(order), jax.ShapeDtypeStruct((slots, local_size), jnp.bfloat16),
          jax.ShapeDtypeStruct((slots, blocks * LANES), jnp.bfloat16),
          jax.ShapeDtypeStruct((8, LANES), jnp.int32), kept, like(order), tiles(tables), tiles(rows)],
-        [order, responses, part, corners.reshape(nz, 1, CORNERS), matrices],
+        [order, responses, part, corners.reshape(nz, 1, CORNERS), matrices, marks],
         pltpu.HBM,
         2**30,
         [pltpu.VMEM(responses.shape, responses.dtype), pltpu.VMEM(part.shape, F32),
@@ -672,7 +690,7 @@
                 functools.partial(spread_kernel, ncoarse), [wide], [sums], pltpu.VMEM, 2**26
             )
         rows_at = list(scatter) if packed and not first else []
-        operands = [marks, sums, inverse] + rows_at + received[::-1] + [faces, response_faces] + state
+        operands = [marks, sums, inverse] + rows_at + [received[at] for at in start_order(first, last)] + [faces, response_faces] + state
         kernel = functools.partial(step_kernel, first, last, nz, ncoarse)
         if last:
             outs = [tiles(nz * 3)] * 2

time: 52.8 us -> 52.3 us (level)
  waiting for transfers between devices: 5.52 us -> 6.76 us
  starting transfers between devices: 34.8 us -> 33.6 us
  Pallas kernels: 11.4 us -> 10.8 us
    ppermute x4, waiting for transfers between devices: 1.84 us -> 3.45 us  [paired_other(): lax.ppermute(value, axis, [(i, (i + 1 if i % 2 else i - 1) % count) for i...]
    all_to_all x3, starting transfers between devices: 13.9 us -> 12.5 us  [summed(): return lax.all_to_all(sums, ('sub', 'slab'), 0, 0, tiled=True)]
    ppermute x4, starting transfers between devices: 10.6 us -> 9.55 us  [paired_other(): lax.ppermute(value, axis, [(i, (i + 1 if i % 2 else i - 1) % count) for i...]
    ppermute x5, starting transfers between devices: 1.7 us -> 2.66 us  [paired(): lax.ppermute(value, axis, [(i, i ^ mask) for i in range(lax.axis_size(axi...]
    pallas_call x7, Pallas kernels: 11.4 us -> 10.8 us  [call(): pl.pallas_call(kernel, out_shape=outs, in_specs=specs, out_specs=[vmem] *...]
  transfers between devices with their start and end apart: 16 -> 16, of which waited for: 7 -> 7; matrix products, arithmetic and copies ran while one was open for 0% -> 0% of each run, Pallas kernels for 8% -> 7%
where the time goes in v7:
time: 52.3 us; the launch traced here: 52 us
  starting transfers between devices  33.6 us (64%)
  Pallas kernels  10.8 us (21%)
  waiting for transfers between devices  6.76 us (13%)
  between operations  0.73 us (1%)
    all_to_all x3, starting transfers between devices, summed(): return lax.all_to_all(sums, ('sub', 'slab'), 0, 0, tiled=True)  12.5 us
    pallas_call x7, Pallas kernels, call(): pl.pallas_call(kernel, out_shape=outs, in_specs=specs, out_specs=[vmem] *...  10.8 us
    ppermute x4, starting transfers between devices, paired_other(): lax.ppermute(value, axis, [(i, (i + 1 if i % 2 else i - 1) % count) for i...  9.55 us
    ppermute x4, starting transfers between devices, shifted(): lax.ppermute(value, axis, [(i, (i + steps) % count) for i in range(count)])  8.89 us
    ppermute x4, waiting for transfers between devices, paired_other(): lax.ppermute(value, axis, [(i, (i + 1 if i % 2 else i - 1) % count) for i...  3.45 us
    ppermute x5, starting transfers between devices, paired(): lax.ppermute(value, axis, [(i, i ^ mask) for i in range(lax.axis_size(axi...  2.66 us
    ppermute x4, waiting for transfers between devices, shifted(): lax.ppermute(value, axis, [(i, (i + steps) % count) for i in range(count)])  2.42 us
  transfers between devices with their start and end apart: 16, of which 7 were waited for; matrix products, arithmetic and copies ran while one was open for 0% of the time, Pallas kernels for 7%

profile of v7, /device:TPU:0, one launch (start us, length us, event | category | flops | bytes accessed | tf_op | source)
XLA Modules:
  0.0 52.0 jit_solution(4689559213912364784)
XLA Ops:
  0.6 0.0 copy-start
  0.6 0.5 collective-permute-start
  1.1 2.6 %collective-permute-start.1 = (f32[9,8,128]{2,1,0:T(8,128)}, f32[9,8,128]{2,1,0:T(8,128)S(1)}, u32[]{:S(2)}, u32[]{:S(2)}) collective-permute-start(f32[9,8,128]{2,1,0:T(8,128)} %bitcast.17), channel_id=1, source_target_pairs={{0,1},{1,2},{2,3},{3,0},{4,5},{5,6},{6,7},{7,4},{8,9},{9,10},{10,1... | collective-permute-start | bytes 110600 | tf_op jit(solution)/shard_map/ppermute | solution.py:563
  3.7 0.1 pad_add_fusion
  3.8 0.1 broadcast_in_dim.2.mark_ref.refs_0_
  3.8 2.2 %shard_map.77 = (s32[3,1,768]{2,1,0:T(1,128)S(1)}, bf16[32,768]{1,0:T(8,128)(2,1)S(1)}, bf16[32,128]{1,0:T(8,128)(2,1)S(1)}, s32[8,128]{1,0:T(8,128)S(1)}, bf16[...) custom-call(s32[3,1,768]{2,1,0:T(1,128)} %bitcast.21, ...), custom_call_target="tpu_custom_call" | custom-call | flops 1073741824 | bytes 1048576 | tf_op jit(solution)/shard_map/pallas_call | solution.py:550
  6.0 1.0 %collective-permute-done.back_x_ref = f32[9,8,128]{2,1,0:T(8,128)S(1)} collective-permute-done((f32[9,8,128]{2,1,0:T(8,128)}, f32[9,8,128]{2,1,0:T(8,128)S(1)}, u32[]{:S(2)}, u32[]{:S(2)}) %collective-permute-start) | collective-permute-done | bytes 36896 | tf_op jit(solution)/shard_map/ppermute | solution.py:563
  7.0 0.0 collective-permute-done.1.back_y_ref
  7.0 0.0 copy-done
  7.0 1.6 %shard_map.78 = (f32[15,8,128]{2,1,0:T(8,128)S(1)}, f32[18,8,128]{2,1,0:T(8,128)S(1)}, f32[32,8,128]{2,1,0:T(8,128)}, f32[7,8,128]{2,1,0:T(8,128)S(1)}, f32[7,8,...) custom-call(s32[3,8,128]{2,1,0:T(8,128)S(1)} %broadcast_in_dim.2.mark_ref.refs_0_, ...), custom_call_target="tpu_custom_call" | custom-call | flops 1073741824 | bytes 1048576 | tf_op jit(solution)/shard_map/pallas_call | solution.py:550
  8.7 5.2 %all-to-all-start = ((f32[32,8,128]{2,1,0:T(8,128)}), f32[32,8,128]{2,1,0:T(8,128)S(1)}, u32[]{:S(2)}, u32[]{:S(2)}) async-start(f32[32,8,128]{2,1,0:T(8,128)} %get-tuple-element.48), calls=%async_computation | async-start | bytes 262144 | tf_op jit(solution)/shard_map/all_to_all | solution.py:577
  13.9 2.7 %collective-permute-start.3 = (f32[10,8,128]{2,1,0:T(8,128)S(1)}, f32[10,8,128]{2,1,0:T(8,128)S(1)}, u32[]{:S(2)}, u32[]{:S(2)}) collective-permute-start(f32[10,8,128]{2,1,0:T(8,128)S(1)} %get-tuple-element.80), channel_id=1, source_target_pairs={{0,3},{1,2},{2,1},{3,0},{4,7},{5,6},{6,5},{7,4},{8,11},{9,10},{10,... | collective-permute-start | bytes 122888 | tf_op jit(solution)/shard_map/ppermute | solution.py:572
  16.6 0.6 %collective-permute-start.2 = (f32[10,8,128]{2,1,0:T(8,128)S(1)}, f32[10,8,128]{2,1,0:T(8,128)S(1)}, u32[]{:S(2)}, u32[]{:S(2)}) collective-permute-start(f32[10,8,128]{2,1,0:T(8,128)S(1)} %get-tuple-element.81), channel_id=1, source_target_pairs={{0,1},{1,0},{2,3},{3,2},{4,5},{5,4},{6,7},{7,6},{8,9},{9,8},{10,11... | collective-permute-start | bytes 122888 | tf_op jit(solution)/shard_map/ppermute | solution.py:567
  17.2 0.3 collective-permute-start.4
  17.4 2.5 %collective-permute-start.5 = (f32[7,8,128]{2,1,0:T(8,128)S(1)}, f32[7,8,128]{2,1,0:T(8,128)S(1)}, u32[]{:S(2)}, u32[]{:S(2)}) collective-permute-start(f32[7,8,128]{2,1,0:T(8,128)S(1)} %get-tuple-element.52), channel_id=1, source_target_pairs={{0,28},{4,8},{8,4},{12,16},{16,12},{20,24},{24,20},{28,0},{1,29},{... | collective-permute-start | bytes 86024 | tf_op jit(solution)/shard_map/ppermute | solution.py:572
  19.9 0.0 collective-permute-start.6
  19.9 0.0 collective-permute-done.3
  20.0 0.8 %collective-permute-done.2 = f32[10,8,128]{2,1,0:T(8,128)S(1)} collective-permute-done((f32[10,8,128]{2,1,0:T(8,128)S(1)}, f32[10,8,128]{2,1,0:T(8,128)S(1)}, u32[]{:S(2)}, u32[]{:S(2)}) %collective-permute-start.2) | collective-permute-done | bytes 40992 | tf_op jit(solution)/shard_map/ppermute | solution.py:567
  20.7 0.1 collective-permute-done.4.refs_3_
  20.8 1.1 %shard_map.79.refs_2_ = f32[128,128]{1,0:T(8,128)S(1)} custom-call(s32[3,8,128]{2,1,0:T(8,128)S(1)} %broadcast_in_dim.2.mark_ref.refs_0_, f32[3,8,128]{2,1,0:T(8,128)S(1)} %get-tuple-element.49.refs_0_, f32[3,8,128]{2,1,0:T(8,128)S(1)} %slice.16.refs_1_, f32[3,8,128]{2,1,0:T(8,128)S(1)} %slice.17.refs_2_, f32[3,8,128]{2,1,0:T(8,128)S(1)} %collective-permute-done.4.refs_3_), custom_call_target="tpu_custom_call" | custom-call | flops 536870912 | bytes 1048576 | tf_op jit(solution)/shard_map/pallas_call | solution.py:550
  21.9 0.6 %collective-permute-done.5.refs_5_ = f32[7,8,128]{2,1,0:T(8,128)S(1)} collective-permute-done((f32[7,8,128]{2,1,0:T(8,128)S(1)}, f32[7,8,128]{2,1,0:T(8,128)S(1)}, u32[]{:S(2)}, u32[]{:S(2)}) %collective-permute-start.5) | collective-permute-done | bytes 28704 | tf_op jit(solution)/shard_map/ppermute | solution.py:572
  22.5 0.0 collective-permute-done.6.refs_6_
  22.5 0.0 all-to-all-done.refs_1_.sums_ref
  22.5 2.1 %shard_map.80 = (f32[15,8,128]{2,1,0:T(8,128)S(1)}, f32[15,8,128]{2,1,0:T(8,128)S(1)}, f32[9,8,128]{2,1,0:T(8,128)S(1)}, f32[9,8,128]{2,1,0:T(8,128)S(1)}, f32[2...) custom-call(s32[3,8,128]{2,1,0:T(8,128)S(1)} %broadcast_in_dim.2.mar, ...), custom_call_target="tpu_custom_call" | custom-call | flops 2147483648 | bytes 1048576 | tf_op jit(solution)/shard_map/pallas_call | solution.py:550
  24.6 4.7 %all-to-all-start.1 = ((f32[32,1,128]{2,1,0:T(1,128)}), f32[32,1,128]{2,1,0:T(1,128)S(1)}, u32[]{:S(2)}, u32[]{:S(2)}) async-start(f32[32,1,128]{2,1,0:T(1,128)} %get-tuple-element.56), calls=%async_computation.1 | async-start | bytes 32768 | tf_op jit(solution)/shard_map/all_to_all | solution.py:577
  29.4 1.8 %collective-permute-start.10 = (f32[3,8,128]{2,1,0:T(8,128)S(1)}, f32[3,8,128]{2,1,0:T(8,128)S(1)}, u32[]{:S(2)}, u32[]{:S(2)}) collective-permute-start(f32[3,8,128]{2,1,0:T(8,128)S(1)} %get-tuple-element.60), channel_id=1, source_target_pairs={{0,1},{1,0},{2,3},{3,2},{4,5},{5,4},{6,7},{7,6},{8,9},{9,8},{10,11... | collective-permute-start | bytes 36872 | tf_op jit(solution)/shard_map/ppermute | solution.py:567
  31.2 2.8 %collective-permute-start.7 = (f32[3,8,128]{2,1,0:T(8,128)S(1)}, f32[3,8,128]{2,1,0:T(8,128)S(1)}, u32[]{:S(2)}, u32[]{:S(2)}) collective-permute-start(f32[3,8,128]{2,1,0:T(8,128)S(1)} %get-tuple-element.57), channel_id=1, source_target_pairs={{0,28},{4,8},{8,4},{12,16},{16,12},{20,24},{24,20},{28,0},{1,29},{... | collective-permute-start | bytes 36872 | tf_op jit(solution)/shard_map/ppermute | solution.py:572
  34.0 1.5 %collective-permute-start.8 = (f32[3,8,128]{2,1,0:T(8,128)S(1)}, f32[3,8,128]{2,1,0:T(8,128)S(1)}, u32[]{:S(2)}, u32[]{:S(2)}) collective-permute-start(f32[3,8,128]{2,1,0:T(8,128)S(1)} %get-tuple-element.58), channel_id=1, source_target_pairs={{0,3},{1,2},{2,1},{3,0},{4,7},{5,6},{6,5},{7,4},{8,11},{9,10},{10,... | collective-permute-start | bytes 36872 | tf_op jit(solution)/shard_map/ppermute | solution.py:572
  35.5 0.0 collective-permute-start.9
  35.5 0.2 shard_map.81.refs_3_
  35.7 0.0 collective-permute-done.10.refs_7_
  35.8 0.4 collective-permute-done.7.refs_4_
  36.2 2.4 %collective-permute-done.8.refs_5_ = f32[3,8,128]{2,1,0:T(8,128)S(1)} collective-permute-done((f32[3,8,128]{2,1,0:T(8,128)S(1)}, f32[3,8,128]{2,1,0:T(8,128)S(1)}, u32[]{:S(2)}, u32[]{:S(2)}) %collective-permute-start.8) | collective-permute-done | bytes 12320 | tf_op jit(solution)/shard_map/ppermute | solution.py:572
  38.6 0.0 collective-permute-done.9.refs_6_
  38.6 0.0 all-to-all-done.1.refs_1_
  38.6 2.3 %shard_map.82 = (f32[15,8,128]{2,1,0:T(8,128)S(1)}, f32[15,8,128]{2,1,0:T(8,128)S(1)}, f32[9,8,128]{2,1,0:T(8,128)S(1)}, f32[9,8,128]{2,1,0:T(8,128)S(1)}, f32[2...) custom-call(s32[3,8,128]{2,1,0:T(8,128)S(1)} %broadcast_in_dim.2.mar, ...), custom_call_target="tpu_custom_call" | custom-call | flops 2147483648 | bytes 1048576 | tf_op jit(solution)/shard_map/pallas_call | solution.py:550
  40.9 2.5 %all-to-all-start.2 = ((f32[32,1,128]{2,1,0:T(1,128)}), f32[32,1,128]{2,1,0:T(1,128)S(1)}, u32[]{:S(2)}, u32[]{:S(2)}) async-start(f32[32,1,128]{2,1,0:T(1,128)} %get-tuple-element.69), calls=%async_computation.2 | async-start | bytes 32768 | tf_op jit(solution)/shard_map/all_to_all | solution.py:577
  43.5 3.4 %collective-permute-start.11 = (f32[3,8,128]{2,1,0:T(8,128)S(1)}, f32[3,8,128]{2,1,0:T(8,128)S(1)}, u32[]{:S(2)}, u32[]{:S(2)}) collective-permute-start(f32[3,8,128]{2,1,0:T(8,128)S(1)} %get-tuple-element.70), channel_id=1, source_target_pairs={{0,28},{4,0},{8,4},{12,8},{16,12},{20,16},{24,20},{28,24},{1,29},{... | collective-permute-start | bytes 36872 | tf_op jit(solution)/shard_map/ppermute | solution.py:563
  46.9 2.4 %collective-permute-start.12 = (f32[3,8,128]{2,1,0:T(8,128)S(1)}, f32[3,8,128]{2,1,0:T(8,128)S(1)}, u32[]{:S(2)}, u32[]{:S(2)}) collective-permute-start(f32[3,8,128]{2,1,0:T(8,128)S(1)} %get-tuple-element.71), channel_id=1, source_target_pairs={{0,3},{1,0},{2,1},{3,2},{4,7},{5,4},{6,5},{7,6},{8,11},{9,8},{10,9... | collective-permute-start | bytes 36872 | tf_op jit(solution)/shard_map/ppermute | solution.py:563
  49.3 0.0 collective-permute-done.11.refs_4_
  49.3 1.4 %collective-permute-done.12.refs_5_ = f32[3,8,128]{2,1,0:T(8,128)S(1)} collective-permute-done((f32[3,8,128]{2,1,0:T(8,128)S(1)}, f32[3,8,128]{2,1,0:T(8,128)S(1)}, u32[]{:S(2)}, u32[]{:S(2)}) %collective-permute-start.12) | collective-permute-done | bytes 12320 | tf_op jit(solution)/shard_map/ppermute | solution.py:563
  50.7 0.0 all-to-all-done.2.refs_1_
  50.7 1.3 %shard_map.83 = (f32[9,8,128]{2,1,0:T(8,128)}, f32[9,8,128]{2,1,0:T(8,128)}) custom-call(s32[3,8,128]{2,1,0:T(8,128)S(1)} %broadcast_in_dim.2.mark_ref.refs_0_, f32[32,1,128]{2,1,0:T(1,128)S(1)} %all-to-all-done.2.refs_1_, f32[128,128]{1,0:T(8,128)S(1)} %shard_map.79.refs_2_, bf16[512,128]{1,0:T(8,128)(2,1)S(1)} %shard_map.81.refs_3_, ...), custom_call_target="tpu_custom_call" | custom-call | flops 1073741824 | bytes 1048576 | tf_op jit(solution)/shard_map/pallas_call | solution.py:550
  (5 shorter events, 0.0 us)
Async XLA Ops:
  0.6 6.4 %copy-start = (f32[1,1,3,8,3,128]{5,3,4,2,1,0:T(8,128)S(1)}, f32[1,1,3,8,3,128]{5,3,4,2,1,0:T(8,128)}, u32[]{:S(2)}) copy-start(f32[1,1,3,8,3,128]{5,3,4,2,1,0:T(8,128)} %param.6) | copy-start | bytes 110596
  0.6 6.4 %collective-permute-start = (f32[9,8,128]{2,1,0:T(8,128)}, f32[9,8,128]{2,1,0:T(8,128)S(1)}, u32[]{:S(2)}, u32[]{:S(2)}) collective-permute-start(f32[9,8,128]{2,1,0:T(8,128)} %bitcast.16), channel_id=1, source_target_pairs={{0,4},{4,8},{8,12},{12,16},{16,20},{20,24},{24,28},{28,0},{1,5},{5... | collective-permute-start | bytes 110600 | tf_op jit(solution)/shard_map/ppermute | solution.py:563
  1.1 5.9 %collective-permute-start.1 = (f32[9,8,128]{2,1,0:T(8,128)}, f32[9,8,128]{2,1,0:T(8,128)S(1)}, u32[]{:S(2)}, u32[]{:S(2)}) collective-permute-start(f32[9,8,128]{2,1,0:T(8,128)} %bitcast.17), channel_id=1, source_target_pairs={{0,1},{1,2},{2,3},{3,0},{4,5},{5,6},{6,7},{7,4},{8,9},{9,10},{10,1... | collective-permute-start | bytes 110600 | tf_op jit(solution)/shard_map/ppermute | solution.py:563
  8.7 13.9 %all-to-all-start = ((f32[32,8,128]{2,1,0:T(8,128)}), f32[32,8,128]{2,1,0:T(8,128)S(1)}, u32[]{:S(2)}, u32[]{:S(2)}) async-start(f32[32,8,128]{2,1,0:T(8,128)} %get-tuple-element.48), calls=%async_computation | async-start | bytes 262144 | tf_op jit(solution)/shard_map/all_to_all | solution.py:577
  13.9 6.1 %collective-permute-start.3 = (f32[10,8,128]{2,1,0:T(8,128)S(1)}, f32[10,8,128]{2,1,0:T(8,128)S(1)}, u32[]{:S(2)}, u32[]{:S(2)}) collective-permute-start(f32[10,8,128]{2,1,0:T(8,128)S(1)} %get-tuple-element.80), channel_id=1, source_target_pairs={{0,3},{1,2},{2,1},{3,0},{4,7},{5,6},{6,5},{7,4},{8,11},{9,10},{10,... | collective-permute-start | bytes 122888 | tf_op jit(solution)/shard_map/ppermute | solution.py:572
  16.6 4.1 %collective-permute-start.2 = (f32[10,8,128]{2,1,0:T(8,128)S(1)}, f32[10,8,128]{2,1,0:T(8,128)S(1)}, u32[]{:S(2)}, u32[]{:S(2)}) collective-permute-start(f32[10,8,128]{2,1,0:T(8,128)S(1)} %get-tuple-element.81), channel_id=1, source_target_pairs={{0,1},{1,0},{2,3},{3,2},{4,5},{5,4},{6,7},{7,6},{8,9},{9,8},{10,11... | collective-permute-start | bytes 122888 | tf_op jit(solution)/shard_map/ppermute | solution.py:567
  17.2 3.7 %collective-permute-start.4 = (f32[3,8,128]{2,1,0:T(8,128)S(1)}, f32[3,8,128]{2,1,0:T(8,128)S(1)}, u32[]{:S(2)}, u32[]{:S(2)}) collective-permute-start(f32[3,8,128]{2,1,0:T(8,128)S(1)} %get-tuple-element.49.refs_0_), channel_id=1, source_target_pairs={{0,2},{1,3},{2,0},{3,1},{4,6},{5,7},{6,4},{7,5},{8,10},{9,11},{10,... | collective-permute-start | bytes 36872 | tf_op jit(solution)/shard_map/ppermute | solution.py:567
  17.4 5.1 %collective-permute-start.5 = (f32[7,8,128]{2,1,0:T(8,128)S(1)}, f32[7,8,128]{2,1,0:T(8,128)S(1)}, u32[]{:S(2)}, u32[]{:S(2)}) collective-permute-start(f32[7,8,128]{2,1,0:T(8,128)S(1)} %get-tuple-element.52), channel_id=1, source_target_pairs={{0,28},{4,8},{8,4},{12,16},{16,12},{20,24},{24,20},{28,0},{1,29},{... | collective-permute-start | bytes 86024 | tf_op jit(solution)/shard_map/ppermute | solution.py:572
  19.9 2.6 %collective-permute-start.6 = (f32[7,8,128]{2,1,0:T(8,128)S(1)}, f32[7,8,128]{2,1,0:T(8,128)S(1)}, u32[]{:S(2)}, u32[]{:S(2)}) collective-permute-start(f32[7,8,128]{2,1,0:T(8,128)S(1)} %get-tuple-element.53), channel_id=1, source_target_pairs={{0,4},{4,0},{8,12},{12,8},{16,20},{20,16},{24,28},{28,24},{1,5},{5... | collective-permute-start | bytes 86024 | tf_op jit(solution)/shard_map/ppermute | solution.py:567
  24.6 14.0 %all-to-all-start.1 = ((f32[32,1,128]{2,1,0:T(1,128)}), f32[32,1,128]{2,1,0:T(1,128)S(1)}, u32[]{:S(2)}, u32[]{:S(2)}) async-start(f32[32,1,128]{2,1,0:T(1,128)} %get-tuple-element.56), calls=%async_computation.1 | async-start | bytes 32768 | tf_op jit(solution)/shard_map/all_to_all | solution.py:577
  29.4 6.4 %collective-permute-start.10 = (f32[3,8,128]{2,1,0:T(8,128)S(1)}, f32[3,8,128]{2,1,0:T(8,128)S(1)}, u32[]{:S(2)}, u32[]{:S(2)}) collective-permute-start(f32[3,8,128]{2,1,0:T(8,128)S(1)} %get-tuple-element.60), channel_id=1, source_target_pairs={{0,1},{1,0},{2,3},{3,2},{4,5},{5,4},{6,7},{7,6},{8,9},{9,8},{10,11... | collective-permute-start | bytes 36872 | tf_op jit(solution)/shard_map/ppermute | solution.py:567
  31.2 5.0 %collective-permute-start.7 = (f32[3,8,128]{2,1,0:T(8,128)S(1)}, f32[3,8,128]{2,1,0:T(8,128)S(1)}, u32[]{:S(2)}, u32[]{:S(2)}) collective-permute-start(f32[3,8,128]{2,1,0:T(8,128)S(1)} %get-tuple-element.57), channel_id=1, source_target_pairs={{0,28},{4,8},{8,4},{12,16},{16,12},{20,24},{24,20},{28,0},{1,29},{... | collective-permute-start | bytes 36872 | tf_op jit(solution)/shard_map/ppermute | solution.py:572
  34.0 4.6 %collective-permute-start.8 = (f32[3,8,128]{2,1,0:T(8,128)S(1)}, f32[3,8,128]{2,1,0:T(8,128)S(1)}, u32[]{:S(2)}, u32[]{:S(2)}) collective-permute-start(f32[3,8,128]{2,1,0:T(8,128)S(1)} %get-tuple-element.58), channel_id=1, source_target_pairs={{0,3},{1,2},{2,1},{3,0},{4,7},{5,6},{6,5},{7,4},{8,11},{9,10},{10,... | collective-permute-start | bytes 36872 | tf_op jit(solution)/shard_map/ppermute | solution.py:572
  35.5 3.1 %collective-permute-start.9 = (f32[3,8,128]{2,1,0:T(8,128)S(1)}, f32[3,8,128]{2,1,0:T(8,128)S(1)}, u32[]{:S(2)}, u32[]{:S(2)}) collective-permute-start(f32[3,8,128]{2,1,0:T(8,128)S(1)} %get-tuple-element.59), channel_id=1, source_target_pairs={{0,4},{4,0},{8,12},{12,8},{16,20},{20,16},{24,28},{28,24},{1,5},{5... | collective-permute-start | bytes 36872 | tf_op jit(solution)/shard_map/ppermute | solution.py:567
  40.9 9.8 %all-to-all-start.2 = ((f32[32,1,128]{2,1,0:T(1,128)}), f32[32,1,128]{2,1,0:T(1,128)S(1)}, u32[]{:S(2)}, u32[]{:S(2)}) async-start(f32[32,1,128]{2,1,0:T(1,128)} %get-tuple-element.69), calls=%async_computation.2 | async-start | bytes 32768 | tf_op jit(solution)/shard_map/all_to_all | solution.py:577
  43.5 5.8 %collective-permute-start.11 = (f32[3,8,128]{2,1,0:T(8,128)S(1)}, f32[3,8,128]{2,1,0:T(8,128)S(1)}, u32[]{:S(2)}, u32[]{:S(2)}) collective-permute-start(f32[3,8,128]{2,1,0:T(8,128)S(1)} %get-tuple-element.70), channel_id=1, source_target_pairs={{0,28},{4,0},{8,4},{12,8},{16,12},{20,16},{24,20},{28,24},{1,29},{... | collective-permute-start | bytes 36872 | tf_op jit(solution)/shard_map/ppermute | solution.py:563
  46.9 3.8 %collective-permute-start.12 = (f32[3,8,128]{2,1,0:T(8,128)S(1)}, f32[3,8,128]{2,1,0:T(8,128)S(1)}, u32[]{:S(2)}, u32[]{:S(2)}) collective-permute-start(f32[3,8,128]{2,1,0:T(8,128)S(1)} %get-tuple-element.71), channel_id=1, source_target_pairs={{0,3},{1,0},{2,1},{3,2},{4,7},{5,4},{6,5},{7,6},{8,11},{9,8},{10,9... | collective-permute-start | bytes 36872 | tf_op jit(solution)/shard_map/ppermute | solution.py:563

commit v8 on v7

--- a/solution.py
+++ b/solution.py
@@ -373,10 +373,27 @@
 def start_order(first, last):
     if last:
         return (0, 1)
-    return (3, 2, 1, 0) if first else (1, 3, 0, 2)
-
-
-def step_kernel(first, last, nz, ncoarse, *refs):
+    return (3, 2, 1, 0) if first else (3, 1, 0, 2)
+
+
+def lift(tile, response, picked, slot, wide):
+    for corner in range(CORNERS):
+        at = slot * CORNERS + corner
+        if at not in wide:
+            wide[at] = jnp.broadcast_to(picked[:, at : at + 1], (8, LANES))
+        tile = tile + wide[at] * response[corner : corner + 1, :]
+    return tile
+
+
+def corner_values(coarse, ids):
+    return pick_lanes(coarse, lax.shift_right_logical(ids, 7), lax.bitwise_and(ids, LANES - 1))
+
+
+def near_sides(last):
+    return (AHEAD_X, AHEAD_Y) if last else range(4)
+
+
+def sums_kernel(first, last, nz, ncoarse, *refs):
     refs = list(refs)
 
     def take(count):
@@ -384,60 +401,18 @@
         del refs[:count]
         return taken
 
-    mark_ref, sums_ref, inverse_ref = take(3)
+    sums_ref, inverse_ref = take(2)
     packed = sums_ref.shape[1] == 1
     if packed:
         (spread_ref,) = take(1)
-    order = start_order(first, last)
-    received = [got for _, got in sorted(zip(order, take(len(order))), key=lambda pair: pair[0])]
-    faces_ref, response_faces_ref, residual_ref = take(3)
-    if first:
-        (ids_ref,) = take(1)
-    else:
-        ids_ref, near_ref, image_ref, direction_ref, multipliers_ref, scalars_ref = take(6)
+    faces_ref, response_faces_ref, residual_ref, ids_ref = take(4)
+    if not first:
+        near_ref, scalars_ref = take(2)
+    if not first and not last:
+        direction_ref, multipliers_ref = take(2)
+    out_scalars, out_lifted, out_rest = take(3)
     if not last:
-        order_ref, matrix_ref, slots_ref, vertex_ref, place_ref = take(5)
-        (out_residual, out_image, out_direction, out_multipliers, out_scalars, out_faces, out_sums) = take(7)
-        sends = take(len(refs) - (2 if first else 0))
-        if first:
-            out_ids, out_near = take(2)
-    else:
-        out_multipliers, out_residual = take(2)
-
-    even_x, even_y = mark_ref[PARITY] == 0, mark_ref[PARITY + 1] == 0
-    lane = lane_iota()
-
-    def ahead_and_back(at):
-        if last:
-            return {AHEAD_X: received[0][at], AHEAD_Y: received[1][at]}
-        x_first, x_second, y_first, y_second = [ref[at] for ref in received]
-        return {
-            AHEAD_X: jnp.where(even_x, x_first, x_second),
-            BACK_X: jnp.where(even_x, x_second, x_first),
-            AHEAD_Y: jnp.where(even_y, y_first, y_second),
-            BACK_Y: jnp.where(even_y, y_second, y_first),
-        }
-
-    near_faces, near_responses = {}, {}
-    for z in range(nz):
-        for side, tile in ahead_and_back(z).items():
-            near_faces[side, z] = tile
-    if first:
-        ids = ids_ref[...]
-        for side, tile in ahead_and_back(2 * nz).items():
-            shift = nz * CORNERS * (side + 1)
-            moved = pltpu.roll(tile, shift, axis=1).astype(jnp.int32)
-            ids = jnp.where((lane >= shift) & (lane < shift + nz * CORNERS), moved, ids)
-        out_ids[...] = ids
-        for z in range(nz):
-            for side, tile in ahead_and_back(nz + z).items():
-                near_responses[side, z] = tile
-                out_near[side * nz + z] = tile
-    else:
-        ids = ids_ref[...]
-        for z in range(nz):
-            for side in (AHEAD_X, AHEAD_Y) if last else range(4):
-                near_responses[side, z] = near_ref[side * nz + z]
+        out_direction, out_multipliers = take(2)
 
     blocks = inverse_ref.shape[0] // LANES
     if packed:
@@ -457,69 +432,127 @@
 
     def number(at):
         block, place = divmod(ncoarse + at, LANES)
-        return sums[block][:, place : place + 1]
-
-    norm, cross, energy = number(0), number(1), energy + number(2)
+        return jnp.broadcast_to(sums[block][:, place : place + 1], (8, LANES))
+
+    norm, cross, energy = number(0), number(1), jnp.broadcast_to(energy, (8, LANES)) + number(2)
     if first:
-        curvature = energy
+        ratio, curvature = jnp.zeros_like(norm), energy
     else:
-        last_norm, last_curvature = scalars_ref[0][:, 0:1], scalars_ref[1][:, 0:1]
-        ratio = norm / last_norm
-        curvature = energy + 2.0 * ratio * cross + ratio * ratio * last_curvature
+        ratio = norm / scalars_ref[2]
+        curvature = energy + 2.0 * ratio * cross + ratio * ratio * scalars_ref[3]
     step = norm / curvature
-
-    picked = pick_lanes(coarse, lax.shift_right_logical(ids, 7), lax.bitwise_and(ids, LANES - 1))
-
-    wide = {}
-
-    def lifted(tile, response, slot):
-        for corner in range(CORNERS):
-            at = slot * CORNERS + corner
-            if at not in wide:
-                wide[at] = jnp.broadcast_to(picked[:, at : at + 1], (8, LANES))
-            tile = tile + wide[at] * response[corner : corner + 1, :]
-        return tile
+    for at, value in enumerate((step, ratio, norm, curvature)):
+        out_scalars[at] = value
+
+    picked, wide = corner_values(coarse, ids_ref[...]), {}
+    for z in range(nz):
+        for side in range(SIDES):
+            at = z * SIDES + side
+            out_lifted[at] = lift(faces_ref[at], response_faces_ref[at], picked, z, wide)
+    if first:
+        for block, tile in enumerate(coarse):
+            out_rest[block] = tile
+    else:
+        none = jnp.zeros((8, LANES), F32)
+        for side in near_sides(last):
+            for z in range(nz):
+                at = side * nz + z
+                out_rest[at] = lift(none, near_ref[at], picked, nz * (side + 1) + z, wide)
+    if last:
+        return
+    for at in range(nz * 3):
+        direction = residual_ref[at] if first else residual_ref[at] + ratio * direction_ref[at]
+        out_multipliers[at] = step * direction if first else multipliers_ref[at] + step * direction
+        out_direction[at] = direction
+
+
+def faces_kernel(first, last, nz, ncoarse, *refs):
+    refs = list(refs)
+
+    def take(count):
+        taken = refs[:count]
+        del refs[:count]
+        return taken
+
+    mark_ref, scalars_ref, lifted_ref, rest_ref = take(4)
+    order = start_order(first, last)
+    received = [got for _, got in sorted(zip(order, take(len(order))), key=lambda pair: pair[0])]
+    (residual_ref,) = take(1)
+    if first:
+        (ids_ref,) = take(1)
+    else:
+        (image_ref,) = take(1)
+    if not last:
+        order_ref, matrix_ref, slots_ref, vertex_ref, place_ref = take(5)
+        out_residual, out_image, out_faces, out_sums = take(4)
+        sends = take(len(refs) - (2 if first else 0))
+        if first:
+            out_ids, out_near = take(2)
+    else:
+        direction_ref, multipliers_ref, out_residual, out_multipliers = take(4)
+
+    even_x, even_y = mark_ref[PARITY] == 0, mark_ref[PARITY + 1] == 0
+    lane = lane_iota()
+
+    def ahead_and_back(at):
+        if last:
+            return {AHEAD_X: received[0][at], AHEAD_Y: received[1][at]}
+        x_first, x_second, y_first, y_second = [ref[at] for ref in received]
+        return {
+            AHEAD_X: jnp.where(even_x, x_first, x_second),
+            BACK_X: jnp.where(even_x, x_second, x_first),
+            AHEAD_Y: jnp.where(even_y, y_first, y_second),
+            BACK_Y: jnp.where(even_y, y_second, y_first),
+        }
+
+    near = {}
+    for z in range(nz):
+        for side, tile in ahead_and_back(z).items():
+            near[side, z] = tile
+    if first:
+        ids = ids_ref[...]
+        for side, tile in ahead_and_back(2 * nz).items():
+            shift = nz * CORNERS * (side + 1)
+            moved = pltpu.roll(tile, shift, axis=1).astype(jnp.int32)
+            ids = jnp.where((lane >= shift) & (lane < shift + nz * CORNERS), moved, ids)
+        out_ids[...] = ids
+        picked = corner_values([rest_ref[block] for block in range(rest_ref.shape[0])], ids)
+        wide = {}
+        for z in range(nz):
+            for side, tile in ahead_and_back(nz + z).items():
+                near[side, z] = lift(near[side, z], tile, picked, nz * (side + 1) + z, wide)
+                out_near[side * nz + z] = tile
+    else:
+        for z in range(nz):
+            for side in near_sides(last):
+                near[side, z] = near[side, z] + rest_ref[side * nz + z]
 
     def own_side(z, side):
-        at = z * SIDES + side
-        return lifted(faces_ref[at], response_faces_ref[at], z)
-
-    def near_side(side, z):
-        return lifted(near_faces[side, z], near_responses[side, z], nz * (side + 1) + z)
+        return lifted_ref[z * SIDES + side]
 
     fresh = [None] * (nz * 5)
-    third_down = [own_side(z, 2) for z in range(nz)]
-    for z in range(nz):
-        fresh[z * 3] = own_side(z, 3) - near_side(AHEAD_X, z)
-        fresh[z * 3 + 1] = own_side(z, 4) - near_side(AHEAD_Y, z)
-        fresh[z * 3 + 2] = own_side(z, 5) - third_down[(z + 1) % nz]
+    for z in range(nz):
+        fresh[z * 3] = own_side(z, 3) - near[AHEAD_X, z]
+        fresh[z * 3 + 1] = own_side(z, 4) - near[AHEAD_Y, z]
+        fresh[z * 3 + 2] = own_side(z, 5) - own_side((z + 1) % nz, 2)
         if not last:
-            fresh[nz * 3 + z] = near_side(BACK_X, z) - own_side(z, 0)
-            fresh[nz * 4 + z] = near_side(BACK_Y, z) - own_side(z, 1)
-
+            fresh[nz * 3 + z] = near[BACK_X, z] - own_side(z, 0)
+            fresh[nz * 4 + z] = near[BACK_Y, z] - own_side(z, 1)
+
+    step, ratio = scalars_ref[0], scalars_ref[1]
     count = nz * 3 if last else nz * 5
     residual, image = [], []
     for at in range(count):
-        new_image = fresh[at] if first else fresh[at] + ratio * image_ref[at]
-        old_residual = residual_ref[at]
-        residual.append(old_residual - step * new_image)
-        image.append(new_image)
-        if at < nz * 3:
-            direction = old_residual if first else old_residual + ratio * direction_ref[at]
-            multipliers = step * direction if first else multipliers_ref[at] + step * direction
-            if last:
-                out_multipliers[at] = multipliers
-                out_residual[at] = residual[at]
-            else:
-                out_direction[at] = direction
-                out_multipliers[at] = multipliers
+        image.append(fresh[at] if first else fresh[at] + ratio * image_ref[at])
+        residual.append(residual_ref[at] - step * image[at])
+        out_residual[at] = residual[at]
+        if not last:
+            out_image[at] = image[at]
     if last:
+        for at in range(nz * 3):
+            direction = residual_ref[at] + ratio * direction_ref[at]
+            out_multipliers[at] = multipliers_ref[at] + step * direction
         return
-    for at in range(count):
-        out_residual[at] = residual[at]
-        out_image[at] = image[at]
-    out_scalars[0] = jnp.broadcast_to(norm, (8, LANES))
-    out_scalars[1] = jnp.broadcast_to(curvature, (8, LANES))
     refs = (order_ref, matrix_ref, slots_ref, vertex_ref, place_ref, out_faces, out_sums)
     faces = local_part(nz, ncoarse, (residual[: nz * 3], residual[nz * 3 :]), image, refs)
     if len(sends) == 2:
@@ -664,7 +697,6 @@
         pltpu.VMEM,
         2**30,
     )
-    state = [residual, ids]
 
     def invert(factor):
         if not riding:
@@ -690,24 +722,35 @@
                 functools.partial(spread_kernel, ncoarse), [wide], [sums], pltpu.VMEM, 2**26
             )
         rows_at = list(scatter) if packed and not first else []
-        operands = [marks, sums, inverse] + rows_at + [received[at] for at in start_order(first, last)] + [faces, response_faces] + state
-        kernel = functools.partial(step_kernel, first, last, nz, ncoarse)
+        kept = [ids] if first else [ids, near, step]
+        if not first and not last:
+            kept += [direction, multipliers]
+        rest = inverse.shape[1] // LANES if first else nz * 4
+        outs = [tiles(4), tiles(tables), tiles(rest)] + [tiles(nz * 3)] * (0 if last else 2)
+        step, lifted, rest, *moved = call(
+            functools.partial(sums_kernel, first, last, nz, ncoarse), outs,
+            [sums, inverse] + rows_at + [faces, response_faces, residual] + kept, pltpu.VMEM, 2**29,
+        )
+        operands = [marks, step, lifted, rest]
+        operands += [received[at] for at in start_order(first, last)]
+        operands += [residual, ids if first else image]
+        kernel = functools.partial(faces_kernel, first, last, nz, ncoarse)
         if last:
-            outs = [tiles(nz * 3)] * 2
-            multipliers, residual = call(kernel, outs, operands, pltpu.VMEM, 2**30)
+            operands += [direction, multipliers]
+            residual, multipliers = call(kernel, [tiles(nz * 3)] * 2, operands, pltpu.VMEM, 2**28)
             break
-        outs = [tiles(nz * 5), tiles(nz * 5), tiles(nz * 3), tiles(nz * 3), tiles(2)]
+        direction, multipliers = moved
         sides = 2 if iteration == ITERS - 2 else 4
-        outs += [tiles(tables), jax.ShapeDtypeStruct((copies, 1, LANES), F32) if packed else tiles(blocks * copies)]
+        outs = [tiles(nz * 5), tiles(nz * 5), tiles(tables)]
+        outs += [jax.ShapeDtypeStruct((copies, 1, LANES), F32) if packed else tiles(blocks * copies)]
         outs += [tiles(nz)] * sides
         if first:
             outs += [jax.ShapeDtypeStruct((8, LANES), jnp.int32), tiles(nz * 4)]
         results = call(kernel, outs, operands + own, pltpu.VMEM, 2**31)
-        residual, image, direction, multipliers, step, faces, sums = results[:7]
-        sends = results[7 : 7 + sides]
+        residual, image, faces, sums = results[:4]
+        sends = results[4 : 4 + sides]
         if first:
-            ids, near = results[7 + sides :]
-        state = [residual, ids, near, image, direction, multipliers, step]
+            ids, near = results[4 + sides :]
 
     def placed(value):
         value = value.reshape(interface_rhs.shape[:3] + (dirs, samples, face))

time: 52.3 us -> 51.2 us (0.979)
  starting transfers between devices: 33.6 us -> 31.3 us
  waiting for transfers between devices: 6.76 us -> 7.65 us
    ppermute x4, waiting for transfers between devices: 3.45 us -> 0.01 us  [paired_other(): lax.ppermute(value, axis, [(i, (i + 1 if i % 2 else i - 1) % count) for i...]
    all_to_all x3, waiting for transfers between devices: 0.01 us -> 2.32 us  [summed(): return lax.all_to_all(sums, ('sub', 'slab'), 0, 0, tiled=True)]
    all_to_all x3, starting transfers between devices: 12.5 us -> 10.3 us  [summed(): return lax.all_to_all(sums, ('sub', 'slab'), 0, 0, tiled=True)]
    ppermute x5, waiting for transfers between devices: 0.88 us -> 2.26 us  [paired(): lax.ppermute(value, axis, [(i, i ^ mask) for i in range(lax.axis_size(axi...]
    ppermute x4, starting transfers between devices: 9.55 us -> 10.8 us  [paired_other(): lax.ppermute(value, axis, [(i, (i + 1 if i % 2 else i - 1) % count) for i...]
    ppermute x5, starting transfers between devices: 2.66 us -> 1.37 us  [paired(): lax.ppermute(value, axis, [(i, i ^ mask) for i in range(lax.axis_size(axi...]
    ppermute x4, waiting for transfers between devices: 2.42 us -> 3.05 us  [shifted(): lax.ppermute(value, axis, [(i, (i + steps) % count) for i in range(count)])]
    pallas_call x7 -> x10, Pallas kernels: 10.8 us -> 11 us  [call(): pl.pallas_call(kernel, out_shape=outs, in_specs=specs, out_specs=[vmem] *...]
  transfers between devices with their start and end apart: 16 -> 16, of which waited for: 7 -> 8; matrix products, arithmetic and copies ran while one was open for 0% -> 0% of each run, Pallas kernels for 7% -> 10%
where the time goes in v8:
time: 51.2 us; the launch traced here: 51 us
  starting transfers between devices  31.3 us (61%)
  Pallas kernels  11 us (21%)
  waiting for transfers between devices  7.65 us (15%)
  between operations  0.78 us (2%)
    pallas_call x10, Pallas kernels, call(): pl.pallas_call(kernel, out_shape=outs, in_specs=specs, out_specs=[vmem] *...  11 us
    ppermute x4, starting transfers between devices, paired_other(): lax.ppermute(value, axis, [(i, (i + 1 if i % 2 else i - 1) % count) for i...  10.8 us
    all_to_all x3, starting transfers between devices, summed(): return lax.all_to_all(sums, ('sub', 'slab'), 0, 0, tiled=True)  10.3 us
    ppermute x4, starting transfers between devices, shifted(): lax.ppermute(value, axis, [(i, (i + steps) % count) for i in range(count)])  8.83 us
    ppermute x4, waiting for transfers between devices, shifted(): lax.ppermute(value, axis, [(i, (i + steps) % count) for i in range(count)])  3.05 us
    all_to_all x3, waiting for transfers between devices, summed(): return lax.all_to_all(sums, ('sub', 'slab'), 0, 0, tiled=True)  2.32 us
    ppermute x5, waiting for transfers between devices, paired(): lax.ppermute(value, axis, [(i, i ^ mask) for i in range(lax.axis_size(axi...  2.26 us
    ppermute x5, starting transfers between devices, paired(): lax.ppermute(value, axis, [(i, i ^ mask) for i in range(lax.axis_size(axi...  1.37 us
  transfers between devices with their start and end apart: 16, of which 8 were waited for; matrix products, arithmetic and copies ran while one was open for 0% of the time, Pallas kernels for 10%

profile of v8, /device:TPU:0, one launch (start us, length us, event | category | flops | bytes accessed | tf_op | source)
XLA Modules:
  0.0 51.0 jit_solution(662316067957519563)
XLA Ops:
  0.6 0.0 copy-start
  0.6 3.0 %collective-permute-start.1 = (f32[9,8,128]{2,1,0:T(8,128)}, f32[9,8,128]{2,1,0:T(8,128)S(1)}, u32[]{:S(2)}, u32[]{:S(2)}) collective-permute-start(f32[9,8,128]{2,1,0:T(8,128)} %bitcast.16), channel_id=1, source_target_pairs={{0,1},{1,2},{2,3},{3,0},{4,5},{5,6},{6,7},{7,4},{8,9},{9,10},{10,1... | collective-permute-start | bytes 110600 | tf_op jit(solution)/shard_map/ppermute | solution.py:596
  3.6 0.0 collective-permute-start
  3.6 0.1 pad_add_fusion
  3.7 0.1 broadcast_in_dim.2.mark_ref.refs_0_
  3.8 2.2 %shard_map.77 = (s32[3,1,768]{2,1,0:T(1,128)S(1)}, bf16[32,768]{1,0:T(8,128)(2,1)S(1)}, bf16[32,128]{1,0:T(8,128)(2,1)S(1)}, s32[8,128]{1,0:T(8,128)S(1)}, bf16[...) custom-call(s32[3,1,768]{2,1,0:T(1,128)} %bitcast.21, ...), custom_call_target="tpu_custom_call" | custom-call | flops 1073741824 | bytes 1048576 | tf_op jit(solution)/shard_map/pallas_call | solution.py:583
  6.0 0.8 %collective-permute-done.1.back_y_ref = f32[9,8,128]{2,1,0:T(8,128)S(1)} collective-permute-done((f32[9,8,128]{2,1,0:T(8,128)}, f32[9,8,128]{2,1,0:T(8,128)S(1)}, u32[]{:S(2)}, u32[]{:S(2)}) %collective-permute-start.1) | collective-permute-done | bytes 36896 | tf_op jit(solution)/shard_map/ppermute | solution.py:596
  6.7 2.3 %collective-permute-done.back_x_ref = f32[9,8,128]{2,1,0:T(8,128)S(1)} collective-permute-done((f32[9,8,128]{2,1,0:T(8,128)}, f32[9,8,128]{2,1,0:T(8,128)S(1)}, u32[]{:S(2)}, u32[]{:S(2)}) %collective-permute-start) | collective-permute-done | bytes 36896 | tf_op jit(solution)/shard_map/ppermute | solution.py:596
  9.0 0.0 copy-done
  9.0 1.6 %shard_map.78 = (f32[15,8,128]{2,1,0:T(8,128)S(1)}, f32[18,8,128]{2,1,0:T(8,128)S(1)}, f32[32,8,128]{2,1,0:T(8,128)}, f32[7,8,128]{2,1,0:T(8,128)S(1)}, f32[7,8,...) custom-call(s32[3,8,128]{2,1,0:T(8,128)S(1)} %broadcast_in_dim.2.mark_ref.refs_0_, ...), custom_call_target="tpu_custom_call" | custom-call | flops 1073741824 | bytes 1048576 | tf_op jit(solution)/shard_map/pallas_call | solution.py:583
  10.7 3.1 %all-to-all-start = ((f32[32,8,128]{2,1,0:T(8,128)}), f32[32,8,128]{2,1,0:T(8,128)S(1)}, u32[]{:S(2)}, u32[]{:S(2)}) async-start(f32[32,8,128]{2,1,0:T(8,128)} %get-tuple-element.55), calls=%async_computation | async-start | bytes 262144 | tf_op jit(solution)/shard_map/all_to_all | solution.py:610
  13.8 2.7 %collective-permute-start.3 = (f32[10,8,128]{2,1,0:T(8,128)S(1)}, f32[10,8,128]{2,1,0:T(8,128)S(1)}, u32[]{:S(2)}, u32[]{:S(2)}) collective-permute-start(f32[10,8,128]{2,1,0:T(8,128)S(1)} %get-tuple-element.94), channel_id=1, source_target_pairs={{0,3},{1,2},{2,1},{3,0},{4,7},{5,6},{6,5},{7,4},{8,11},{9,10},{10,... | collective-permute-start | bytes 122888 | tf_op jit(solution)/shard_map/ppermute | solution.py:605
  16.6 0.6 %collective-permute-start.2 = (f32[10,8,128]{2,1,0:T(8,128)S(1)}, f32[10,8,128]{2,1,0:T(8,128)S(1)}, u32[]{:S(2)}, u32[]{:S(2)}) collective-permute-start(f32[10,8,128]{2,1,0:T(8,128)S(1)} %get-tuple-element.95), channel_id=1, source_target_pairs={{0,1},{1,0},{2,3},{3,2},{4,5},{5,4},{6,7},{7,6},{8,9},{9,8},{10,11... | collective-permute-start | bytes 122888 | tf_op jit(solution)/shard_map/ppermute | solution.py:600
  17.1 0.3 collective-permute-start.4
  17.4 2.5 %collective-permute-start.5 = (f32[7,8,128]{2,1,0:T(8,128)S(1)}, f32[7,8,128]{2,1,0:T(8,128)S(1)}, u32[]{:S(2)}, u32[]{:S(2)}) collective-permute-start(f32[7,8,128]{2,1,0:T(8,128)S(1)} %get-tuple-element.64), channel_id=1, source_target_pairs={{0,28},{4,8},{8,4},{12,16},{16,12},{20,24},{24,20},{28,0},{1,29},{... | collective-permute-start | bytes 86024 | tf_op jit(solution)/shard_map/ppermute | solution.py:605
  19.9 0.0 collective-permute-start.6
  19.9 0.0 collective-permute-done.3
  19.9 0.8 %collective-permute-done.2 = f32[10,8,128]{2,1,0:T(8,128)S(1)} collective-permute-done((f32[10,8,128]{2,1,0:T(8,128)S(1)}, f32[10,8,128]{2,1,0:T(8,128)S(1)}, u32[]{:S(2)}, u32[]{:S(2)}) %collective-permute-start.2) | collective-permute-done | bytes 40992 | tf_op jit(solution)/shard_map/ppermute | solution.py:600
  20.7 0.1 collective-permute-done.4.refs_3_
  20.8 1.1 %shard_map.79.refs_1_ = f32[128,128]{1,0:T(8,128)S(1)} custom-call(s32[3,8,128]{2,1,0:T(8,128)S(1)} %broadcast_in_dim.2.mark_ref.refs_0_, f32[3,8,128]{2,1,0:T(8,128)S(1)} %get-tuple-element.56.refs_0_, f32[3,8,128]{2,1,0:T(8,128)S(1)} %slice.16.refs_1_, f32[3,8,128]{2,1,0:T(8,128)S(1)} %slice.17.refs_2_, f32[3,8,128]{2,1,0:T(8,128)S(1)} %collective-permute-done.4.refs_3_), custom_call_target="tpu_custom_call" | custom-call | flops 536870912 | bytes 1048576 | tf_op jit(solution)/shard_map/pallas_call | solution.py:583
  21.9 0.3 all-to-all-done.refs_0_.sums_ref
  22.2 0.4 shard_map.80
  22.6 0.0 collective-permute-done.5.refs_6_
  22.6 0.0 collective-permute-done.6.refs_7_
  22.6 1.9 %shard_map.81 = (f32[15,8,128]{2,1,0:T(8,128)S(1)}, f32[15,8,128]{2,1,0:T(8,128)S(1)}, f32[18,8,128]{2,1,0:T(8,128)S(1)}, f32[32,1,128]{2,1,0:T(1,128)}, f32[3,8...) custom-call(s32[3,8,128]{2,1,0:T(8,128)S(1)} %broadcast_in_dim.2.mar, ...), custom_call_target="tpu_custom_call" | custom-call | flops 2147483648 | bytes 1048576 | tf_op jit(solution)/shard_map/pallas_call | solution.py:583
  24.5 4.6 %all-to-all-start.1 = ((f32[32,1,128]{2,1,0:T(1,128)}), f32[32,1,128]{2,1,0:T(1,128)S(1)}, u32[]{:S(2)}, u32[]{:S(2)}) async-start(f32[32,1,128]{2,1,0:T(1,128)} %get-tuple-element.66), calls=%async_computation.1 | async-start | bytes 32768 | tf_op jit(solution)/shard_map/all_to_all | solution.py:610
  29.1 2.7 %collective-permute-start.7 = (f32[3,8,128]{2,1,0:T(8,128)S(1)}, f32[3,8,128]{2,1,0:T(8,128)S(1)}, u32[]{:S(2)}, u32[]{:S(2)}) collective-permute-start(f32[3,8,128]{2,1,0:T(8,128)S(1)} %get-tuple-element.76), channel_id=1, source_target_pairs={{0,3},{1,2},{2,1},{3,0},{4,7},{5,6},{6,5},{7,4},{8,11},{9,10},{10,... | collective-permute-start | bytes 36872 | tf_op jit(solution)/shard_map/ppermute | solution.py:605
  31.8 2.8 %collective-permute-start.8 = (f32[3,8,128]{2,1,0:T(8,128)S(1)}, f32[3,8,128]{2,1,0:T(8,128)S(1)}, u32[]{:S(2)}, u32[]{:S(2)}) collective-permute-start(f32[3,8,128]{2,1,0:T(8,128)S(1)} %get-tuple-element.77), channel_id=1, source_target_pairs={{0,28},{4,8},{8,4},{12,16},{16,12},{20,24},{24,20},{28,0},{1,29},{... | collective-permute-start | bytes 36872 | tf_op jit(solution)/shard_map/ppermute | solution.py:605
  34.7 0.0 collective-permute-start.9
  34.7 0.5 %collective-permute-start.10 = (f32[3,8,128]{2,1,0:T(8,128)S(1)}, f32[3,8,128]{2,1,0:T(8,128)S(1)}, u32[]{:S(2)}, u32[]{:S(2)}) collective-permute-start(f32[3,8,128]{2,1,0:T(8,128)S(1)} %get-tuple-element.79), channel_id=1, source_target_pairs={{0,1},{1,0},{2,3},{3,2},{4,5},{5,4},{6,7},{7,6},{8,9},{9,8},{10,11... | collective-permute-start | bytes 36872 | tf_op jit(solution)/shard_map/ppermute | solution.py:600
  35.2 0.2 shard_map.82.refs_2_
  35.5 0.7 %all-to-all-done.1.refs_0_ = f32[32,1,128]{2,1,0:T(1,128)S(1)} async-done(((f32[32,1,128]{2,1,0:T(1,128)}), f32[32,1,128]{2,1,0:T(1,128)S(1)}, u32[]{:S(2)}, u32[]{:S(2)}) %all-to-all-start.1) | async-done | bytes 16416 | tf_op jit(solution)/shard_map/all_to_all | solution.py:610
  36.2 0.8 %shard_map.83 = (f32[4,8,128]{2,1,0:T(8,128)S(1)}, f32[18,8,128]{2,1,0:T(8,128)S(1)}, f32[12,8,128]{2,1,0:T(8,128)S(1)}, f32[9,8,128]{2,1,0:T(8,128)S(1)}, f32[9,8,128]{2,1,0:T(8,128)S(1)}) custom-call(f32[32,1,128]{2,1,0:T(1,128)S(1)} %all-to-all-done.1.refs_0_, f32[128,128]{1,0:T(8,128)S(1)} %shard_map.79.refs_1_, bf16[512,128]{1,0:T(8,128)(2,1)S(1)} %shard_map.82.refs_2_, ...), custom_call_target="tpu_custom_call" | custom-call | flops 536870912 | bytes 1048576 | tf_op jit(solution)/shard_map/pallas_call | solution.py:583
  37.0 0.0 collective-permute-done.7.refs_4_
  37.0 0.0 collective-permute-done.8.refs_5_
  37.0 0.0 collective-permute-done.9.refs_6_
  37.0 1.4 %collective-permute-done.10.refs_7_ = f32[3,8,128]{2,1,0:T(8,128)S(1)} collective-permute-done((f32[3,8,128]{2,1,0:T(8,128)S(1)}, f32[3,8,128]{2,1,0:T(8,128)S(1)}, u32[]{:S(2)}, u32[]{:S(2)}) %collective-permute-start.10) | collective-permute-done | bytes 12320 | tf_op jit(solution)/shard_map/ppermute | solution.py:600
  38.4 1.6 %shard_map.84 = (f32[15,8,128]{2,1,0:T(8,128)S(1)}, f32[15,8,128]{2,1,0:T(8,128)S(1)}, f32[18,8,128]{2,1,0:T(8,128)S(1)}, f32[32,1,128]{2,1,0:T(1,128)}, f32[3,8...) custom-call(s32[3,8,128]{2,1,0:T(8,128)S(1)} %broadcast_in_dim.2.mark_ref.refs_0_, ...), custom_call_target="tpu_custom_call" | custom-call | flops 2147483648 | bytes 1048576 | tf_op jit(solution)/shard_map/pallas_call | solution.py:583
  40.0 2.5 %all-to-all-start.2 = ((f32[32,1,128]{2,1,0:T(1,128)}), f32[32,1,128]{2,1,0:T(1,128)S(1)}, u32[]{:S(2)}, u32[]{:S(2)}) async-start(f32[32,1,128]{2,1,0:T(1,128)} %get-tuple-element.81), calls=%async_computation.2 | async-start | bytes 32768 | tf_op jit(solution)/shard_map/all_to_all | solution.py:610
  42.5 3.4 %collective-permute-start.11 = (f32[3,8,128]{2,1,0:T(8,128)S(1)}, f32[3,8,128]{2,1,0:T(8,128)S(1)}, u32[]{:S(2)}, u32[]{:S(2)}) collective-permute-start(f32[3,8,128]{2,1,0:T(8,128)S(1)} %get-tuple-element.87), channel_id=1, source_target_pairs={{0,28},{4,0},{8,4},{12,8},{16,12},{20,16},{24,20},{28,24},{1,29},{... | collective-permute-start | bytes 36872 | tf_op jit(solution)/shard_map/ppermute | solution.py:596
  45.9 2.4 %collective-permute-start.12 = (f32[3,8,128]{2,1,0:T(8,128)S(1)}, f32[3,8,128]{2,1,0:T(8,128)S(1)}, u32[]{:S(2)}, u32[]{:S(2)}) collective-permute-start(f32[3,8,128]{2,1,0:T(8,128)S(1)} %get-tuple-element.88), channel_id=1, source_target_pairs={{0,3},{1,0},{2,1},{3,2},{4,7},{5,4},{6,5},{7,6},{8,11},{9,8},{10,9... | collective-permute-start | bytes 36872 | tf_op jit(solution)/shard_map/ppermute | solution.py:596
  48.3 1.3 %all-to-all-done.2.refs_0_ = f32[32,1,128]{2,1,0:T(1,128)S(1)} async-done(((f32[32,1,128]{2,1,0:T(1,128)}), f32[32,1,128]{2,1,0:T(1,128)S(1)}, u32[]{:S(2)}, u32[]{:S(2)}) %all-to-all-start.2) | async-done | bytes 16416 | tf_op jit(solution)/shard_map/all_to_all | solution.py:610
  49.6 0.7 %shard_map.85 = (f32[4,8,128]{2,1,0:T(8,128)S(1)}, f32[18,8,128]{2,1,0:T(8,128)S(1)}, f32[12,8,128]{2,1,0:T(8,128)S(1)}) custom-call(f32[32,1,128]{2,1,0:T(1,128)S(1)} %all-to-all-done.2.refs_0_, f32[128,128]{1,0:T(8,128)S(1)} %shard_map.79.refs_1_, bf16[512,128]{1,0:T(8,128)(2,1)S(1)} %shard_map.82.refs_2_, f32[18,8,128]{2,1,0:T(8,128)S(1)} %get-tuple-element.82.refs_3_, ...), custom_call_target="tpu_custom_call" | custom-call | flops 536870912 | bytes 1048576 | tf_op jit(solution)/shard_map/pallas_call | solution.py:583
  50.3 0.0 collective-permute-done.11.refs_4_
  50.3 0.0 collective-permute-done.12.refs_5_
  50.3 0.7 %shard_map.86 = (f32[9,8,128]{2,1,0:T(8,128)}, f32[9,8,128]{2,1,0:T(8,128)}) custom-call(s32[3,8,128]{2,1,0:T(8,128)S(1)} %broadcast_in_dim.2.mark_ref.refs_0_, f32[4,8,128]{2,1,0:T(8,128)S(1)} %get-tuple-element.84.refs_1_, f32[18,8,128]{2,1,0:T(8,128)S(1)} %get-tuple-element.85.refs_2_, f32[12,8,128]{2,1,0:T(8,128)S(1)} %get-tuple-element.86.refs_3_, ...), custom_call_target="tpu_custom_call" | custom-call | flops 268435456 | bytes 1048576 | tf_op jit(solution)/shard_map/pallas_call | solution.py:583
  (5 shorter events, 0.0 us)
Async XLA Ops:
  0.6 8.4 %copy-start = (f32[1,1,3,8,3,128]{5,3,4,2,1,0:T(8,128)S(1)}, f32[1,1,3,8,3,128]{5,3,4,2,1,0:T(8,128)}, u32[]{:S(2)}) copy-start(f32[1,1,3,8,3,128]{5,3,4,2,1,0:T(8,128)} %param.6) | copy-start | bytes 110596
  0.6 6.1 %collective-permute-start.1 = (f32[9,8,128]{2,1,0:T(8,128)}, f32[9,8,128]{2,1,0:T(8,128)S(1)}, u32[]{:S(2)}, u32[]{:S(2)}) collective-permute-start(f32[9,8,128]{2,1,0:T(8,128)} %bitcast.16), channel_id=1, source_target_pairs={{0,1},{1,2},{2,3},{3,0},{4,5},{5,6},{6,7},{7,4},{8,9},{9,10},{10,1... | collective-permute-start | bytes 110600 | tf_op jit(solution)/shard_map/ppermute | solution.py:596
  3.6 5.4 %collective-permute-start = (f32[9,8,128]{2,1,0:T(8,128)}, f32[9,8,128]{2,1,0:T(8,128)S(1)}, u32[]{:S(2)}, u32[]{:S(2)}) collective-permute-start(f32[9,8,128]{2,1,0:T(8,128)} %bitcast.17), channel_id=1, source_target_pairs={{0,4},{4,8},{8,12},{12,16},{16,20},{20,24},{24,28},{28,0},{1,5},{5... | collective-permute-start | bytes 110600 | tf_op jit(solution)/shard_map/ppermute | solution.py:596
  10.7 11.6 %all-to-all-start = ((f32[32,8,128]{2,1,0:T(8,128)}), f32[32,8,128]{2,1,0:T(8,128)S(1)}, u32[]{:S(2)}, u32[]{:S(2)}) async-start(f32[32,8,128]{2,1,0:T(8,128)} %get-tuple-element.55), calls=%async_computation | async-start | bytes 262144 | tf_op jit(solution)/shard_map/all_to_all | solution.py:610
  13.8 6.1 %collective-permute-start.3 = (f32[10,8,128]{2,1,0:T(8,128)S(1)}, f32[10,8,128]{2,1,0:T(8,128)S(1)}, u32[]{:S(2)}, u32[]{:S(2)}) collective-permute-start(f32[10,8,128]{2,1,0:T(8,128)S(1)} %get-tuple-element.94), channel_id=1, source_target_pairs={{0,3},{1,2},{2,1},{3,0},{4,7},{5,6},{6,5},{7,4},{8,11},{9,10},{10,... | collective-permute-start | bytes 122888 | tf_op jit(solution)/shard_map/ppermute | solution.py:605
  16.6 4.1 %collective-permute-start.2 = (f32[10,8,128]{2,1,0:T(8,128)S(1)}, f32[10,8,128]{2,1,0:T(8,128)S(1)}, u32[]{:S(2)}, u32[]{:S(2)}) collective-permute-start(f32[10,8,128]{2,1,0:T(8,128)S(1)} %get-tuple-element.95), channel_id=1, source_target_pairs={{0,1},{1,0},{2,3},{3,2},{4,5},{5,4},{6,7},{7,6},{8,9},{9,8},{10,11... | collective-permute-start | bytes 122888 | tf_op jit(solution)/shard_map/ppermute | solution.py:600
  17.1 3.7 %collective-permute-start.4 = (f32[3,8,128]{2,1,0:T(8,128)S(1)}, f32[3,8,128]{2,1,0:T(8,128)S(1)}, u32[]{:S(2)}, u32[]{:S(2)}) collective-permute-start(f32[3,8,128]{2,1,0:T(8,128)S(1)} %get-tuple-element.56.refs_0_), channel_id=1, source_target_pairs={{0,2},{1,3},{2,0},{3,1},{4,6},{5,7},{6,4},{7,5},{8,10},{9,11},{10,... | collective-permute-start | bytes 36872 | tf_op jit(solution)/shard_map/ppermute | solution.py:600
  17.4 5.2 %collective-permute-start.5 = (f32[7,8,128]{2,1,0:T(8,128)S(1)}, f32[7,8,128]{2,1,0:T(8,128)S(1)}, u32[]{:S(2)}, u32[]{:S(2)}) collective-permute-start(f32[7,8,128]{2,1,0:T(8,128)S(1)} %get-tuple-element.64), channel_id=1, source_target_pairs={{0,28},{4,8},{8,4},{12,16},{16,12},{20,24},{24,20},{28,0},{1,29},{... | collective-permute-start | bytes 86024 | tf_op jit(solution)/shard_map/ppermute | solution.py:605
  19.9 2.7 %collective-permute-start.6 = (f32[7,8,128]{2,1,0:T(8,128)S(1)}, f32[7,8,128]{2,1,0:T(8,128)S(1)}, u32[]{:S(2)}, u32[]{:S(2)}) collective-permute-start(f32[7,8,128]{2,1,0:T(8,128)S(1)} %get-tuple-element.65), channel_id=1, source_target_pairs={{0,4},{4,0},{8,12},{12,8},{16,20},{20,16},{24,28},{28,24},{1,5},{5... | collective-permute-start | bytes 86024 | tf_op jit(solution)/shard_map/ppermute | solution.py:600
  24.5 11.7 %all-to-all-start.1 = ((f32[32,1,128]{2,1,0:T(1,128)}), f32[32,1,128]{2,1,0:T(1,128)S(1)}, u32[]{:S(2)}, u32[]{:S(2)}) async-start(f32[32,1,128]{2,1,0:T(1,128)} %get-tuple-element.66), calls=%async_computation.1 | async-start | bytes 32768 | tf_op jit(solution)/shard_map/all_to_all | solution.py:610
  29.1 7.9 %collective-permute-start.7 = (f32[3,8,128]{2,1,0:T(8,128)S(1)}, f32[3,8,128]{2,1,0:T(8,128)S(1)}, u32[]{:S(2)}, u32[]{:S(2)}) collective-permute-start(f32[3,8,128]{2,1,0:T(8,128)S(1)} %get-tuple-element.76), channel_id=1, source_target_pairs={{0,3},{1,2},{2,1},{3,0},{4,7},{5,6},{6,5},{7,4},{8,11},{9,10},{10,... | collective-permute-start | bytes 36872 | tf_op jit(solution)/shard_map/ppermute | solution.py:605
  31.8 5.1 %collective-permute-start.8 = (f32[3,8,128]{2,1,0:T(8,128)S(1)}, f32[3,8,128]{2,1,0:T(8,128)S(1)}, u32[]{:S(2)}, u32[]{:S(2)}) collective-permute-start(f32[3,8,128]{2,1,0:T(8,128)S(1)} %get-tuple-element.77), channel_id=1, source_target_pairs={{0,28},{4,8},{8,4},{12,16},{16,12},{20,24},{24,20},{28,0},{1,29},{... | collective-permute-start | bytes 36872 | tf_op jit(solution)/shard_map/ppermute | solution.py:605
  34.7 2.3 %collective-permute-start.9 = (f32[3,8,128]{2,1,0:T(8,128)S(1)}, f32[3,8,128]{2,1,0:T(8,128)S(1)}, u32[]{:S(2)}, u32[]{:S(2)}) collective-permute-start(f32[3,8,128]{2,1,0:T(8,128)S(1)} %get-tuple-element.78), channel_id=1, source_target_pairs={{0,4},{4,0},{8,12},{12,8},{16,20},{20,16},{24,28},{28,24},{1,5},{5... | collective-permute-start | bytes 36872 | tf_op jit(solution)/shard_map/ppermute | solution.py:600
  34.7 3.7 %collective-permute-start.10 = (f32[3,8,128]{2,1,0:T(8,128)S(1)}, f32[3,8,128]{2,1,0:T(8,128)S(1)}, u32[]{:S(2)}, u32[]{:S(2)}) collective-permute-start(f32[3,8,128]{2,1,0:T(8,128)S(1)} %get-tuple-element.79), channel_id=1, source_target_pairs={{0,1},{1,0},{2,3},{3,2},{4,5},{5,4},{6,7},{7,6},{8,9},{9,8},{10,11... | collective-permute-start | bytes 36872 | tf_op jit(solution)/shard_map/ppermute | solution.py:600
  40.0 9.6 %all-to-all-start.2 = ((f32[32,1,128]{2,1,0:T(1,128)}), f32[32,1,128]{2,1,0:T(1,128)S(1)}, u32[]{:S(2)}, u32[]{:S(2)}) async-start(f32[32,1,128]{2,1,0:T(1,128)} %get-tuple-element.81), calls=%async_computation.2 | async-start | bytes 32768 | tf_op jit(solution)/shard_map/all_to_all | solution.py:610
  42.5 7.8 %collective-permute-start.11 = (f32[3,8,128]{2,1,0:T(8,128)S(1)}, f32[3,8,128]{2,1,0:T(8,128)S(1)}, u32[]{:S(2)}, u32[]{:S(2)}) collective-permute-start(f32[3,8,128]{2,1,0:T(8,128)S(1)} %get-tuple-element.87), channel_id=1, source_target_pairs={{0,28},{4,0},{8,4},{12,8},{16,12},{20,16},{24,20},{28,24},{1,29},{... | collective-permute-start | bytes 36872 | tf_op jit(solution)/shard_map/ppermute | solution.py:596
  45.9 4.4 %collective-permute-start.12 = (f32[3,8,128]{2,1,0:T(8,128)S(1)}, f32[3,8,128]{2,1,0:T(8,128)S(1)}, u32[]{:S(2)}, u32[]{:S(2)}) collective-permute-start(f32[3,8,128]{2,1,0:T(8,128)S(1)} %get-tuple-element.88), channel_id=1, source_target_pairs={{0,3},{1,0},{2,1},{3,2},{4,7},{5,4},{6,5},{7,6},{8,11},{9,8},{10,9... | collective-permute-start | bytes 36872 | tf_op jit(solution)/shard_map/ppermute | solution.py:596
